TPU v7x, 32 devices: a whole 2x2x4 slice. The times are simulated.
32 devices in a mesh: wide: 8 (over y, x, core), narrow: 4 (over z).
Axes of the slice: x: 2, y: 2, z: 4, core: 2. Of those that a mesh axis runs over, the one named last changes fastest.
Arguments:
- video_clips: bfloat16 [32, 1569, 768], P(('wide', 'narrow')), may hold values from -6 to 6
- time_gain: bfloat16 [768], replicated, may hold values from 0.5 to 1.5
- time_shift: bfloat16 [768], replicated, may hold values from -1 to 1
- time_qkv: bfloat16 [768, 2304], replicated, may hold values from -0.21875 to 0.21875
- time_bias: bfloat16 [2, 768], replicated, may hold values from -1 to 1
- time_proj: bfloat16 [768, 768], replicated, may hold values from -0.4375 to 0.4375
- time_offset: bfloat16 [768], replicated, may hold values from -1 to 1
- space_gain: bfloat16 [768], replicated, may hold values from 0.5 to 1.5
- space_shift: bfloat16 [768], replicated, may hold values from -1 to 1
- space_qkv: bfloat16 [768, 2304], replicated, may hold values from -0.21875 to 0.21875
- space_bias: bfloat16 [2, 768], replicated, may hold values from -1 to 1
- space_proj: bfloat16 [768, 768], replicated, may hold values from -1.75 to 1.75
- space_offset: bfloat16 [768], replicated, may hold values from -1 to 1
- mlp_gain: bfloat16 [768], replicated, may hold values from 0.5 to 1.5
- mlp_shift: bfloat16 [768], replicated, may hold values from -1 to 1
- fc_in: bfloat16 [768, 3072], P(None, 'narrow'), may hold values from -0.21875 to 0.21875
- in_bias: bfloat16 [3072], P('narrow'), may hold values from -1 to 1
- fc_out: bfloat16 [3072, 768], P('narrow'), may hold values from -0.109375 to 0.109375
- out_bias: bfloat16 [768], replicated, may hold values from -1 to 1
- cotangent: bfloat16 [32, 1569, 768], P(('wide', 'narrow')), may hold values from -6 to 6
Outputs:
- layer_out: bfloat16 [32, 1569, 768], P(('wide', 'narrow'))
- grad_clips: float32 [32, 1569, 768], P(('wide', 'narrow'))
- grad_time_gain: float32 [768], P('narrow')
- grad_time_shift: float32 [768], P('narrow')
- grad_time_qkv: float32 [768, 2304], P('narrow', 'wide')
- grad_time_bias: float32 [2, 768], P(None, 'narrow')
- grad_time_proj: float32 [768, 768], P('narrow', 'wide')
- grad_time_offset: float32 [768], P('narrow')
- grad_space_gain: float32 [768], P('narrow')
- grad_space_shift: float32 [768], P('narrow')
- grad_space_qkv: float32 [768, 2304], P('narrow', 'wide')
- grad_space_bias: float32 [2, 768], P(None, 'narrow')
- grad_space_proj: float32 [768, 768], P('narrow', 'wide')
- grad_space_offset: float32 [768], P('narrow')
- grad_mlp_gain: float32 [768], P('narrow')
- grad_mlp_shift: float32 [768], P('narrow')
- grad_fc_in: float32 [768, 3072], P('wide', 'narrow')
- grad_in_bias: float32 [3072], P('narrow')
- grad_fc_out: float32 [3072, 768], P('narrow', 'wide')
- grad_out_bias: float32 [768], P('narrow')
All inputs are finite; a program needn't handle non-finite values.
Results may differ from a plain program's by a relative error of at most 0.02.
Values may be sent and summed in bfloat16 or wider, within the bound.
A program may use at most 384 MiB of HBM per device.

v0:
```python
from functools import partial

import jax
import jax.numpy as jnp
from jax import lax
from jax.sharding import PartitionSpec as P

HEADS = 12
HEAD_DIM = 64
FRAMES = 8
PATCHES = 196


EPSILON = 1e-06


def layer_norm(values, gain_vec, shift_vec):
    center = values - jnp.mean(values, axis=-1, keepdims=True)
    spread = jnp.mean(center * center, axis=-1, keepdims=True)
    return center * lax.rsqrt(spread + EPSILON) * gain_vec + shift_vec


def matmul(left_op, right_op):
    return jnp.dot(left_op, right_op, preferred_element_type=jnp.float32)


def matmul_tn(left_op, right_op):
    return lax.dot_general(
        left_op, right_op, (((0,), (0,)), ((), ())), preferred_element_type=jnp.float32
    )


def matmul_nt(left_op, right_op):
    return lax.dot_general(
        left_op, right_op, (((1,), (1,)), ((), ())), preferred_element_type=jnp.float32
    )


def qkv_bias(bias_pair, model_width):
    return jnp.concatenate([bias_pair[0], jnp.zeros((model_width,), jnp.float32), bias_pair[1]])


def bias_grads(grad_packed, model_width):
    column_sums = jnp.sum(grad_packed.astype(jnp.float32), axis=0)
    return jnp.stack([column_sums[:model_width], column_sums[2 * model_width :]])


def time_split(packed):
    model_width = packed.shape[1] // 3
    shape_four = (FRAMES, PATCHES, HEADS, HEAD_DIM)
    return tuple(
        (
            packed[:, which_part * model_width : (which_part + 1) * model_width].reshape(shape_four)
            for which_part in range(3)
        )
    )


def frame_view(row_block):
    model_width = row_block.shape[1]
    head_rows = jnp.broadcast_to(row_block[0:1][None], (FRAMES, 1, model_width))
    rest_rows = row_block[1:].reshape(FRAMES, PATCHES, model_width)
    return jnp.concatenate([head_rows, rest_rows], axis=1).reshape(
        FRAMES, PATCHES + 1, HEADS, HEAD_DIM
    )


def space_split(packed):
    model_width = packed.shape[1] // 3
    return tuple(
        (
            frame_view(packed[:, which_part * model_width : (which_part + 1) * model_width])
            for which_part in range(3)
        )
    )


def frame_fold(grad_parts):
    flat_rows = grad_parts.reshape(FRAMES, PATCHES + 1, -1)
    first_row = jnp.sum(flat_rows[:, 0], axis=0)[None]
    return jnp.concatenate([first_row, flat_rows[:, 1:].reshape(FRAMES * PATCHES, -1)], axis=0)


def time_scores(t_query, t_key, score_scale):
    return (
        jnp.einsum("fphd,gphd->phfg", t_query, t_key, preferred_element_type=jnp.float32)
        * score_scale
    )


def space_scores(s_query, s_key, score_scale):
    return (
        jnp.einsum("fihd,fjhd->fhij", s_query, s_key, preferred_element_type=jnp.float32)
        * score_scale
    )


def local(
    video_clips,
    time_gain,
    time_shift,
    time_qkv,
    time_bias,
    time_proj,
    time_offset,
    space_gain,
    space_shift,
    space_qkv,
    space_bias,
    space_proj,
    space_offset,
    mlp_gain,
    mlp_shift,
    fc_in,
    in_bias,
    fc_out,
    out_bias,
    cotangent,
):
    clip_count, tokens, model_width = video_clips.shape
    score_scale = HEAD_DIM ** (-0.5)
    t_gain = time_gain.astype(jnp.float32)
    t_shift = time_shift.astype(jnp.float32)
    t_pair = time_bias.astype(jnp.float32)
    t_offset = time_offset.astype(jnp.float32)
    s_gain = space_gain.astype(jnp.float32)
    s_shift = space_shift.astype(jnp.float32)
    s_pair = space_bias.astype(jnp.float32)
    s_offset = space_offset.astype(jnp.float32)
    m_gain = mlp_gain.astype(jnp.float32)
    m_shift = mlp_shift.astype(jnp.float32)
    clip_index = 0
    clip_rows = video_clips[clip_index].astype(jnp.float32)
    patches = clip_rows[1:]
    t_normed = layer_norm(patches, t_gain, t_shift).astype(jnp.bfloat16)
    t_packed = (matmul(t_normed, time_qkv) + qkv_bias(t_pair, model_width)).astype(jnp.bfloat16)
    t_query, t_key, t_value = time_split(t_packed)
    t_raw = time_scores(t_query, t_key, score_scale)
    t_logsum = jax.nn.logsumexp(t_raw, axis=-1, keepdims=True)
    t_probs = jnp.exp(t_raw - t_logsum).astype(jnp.bfloat16)
    t_attn = jnp.einsum("phfg,gphd->fphd", t_probs, t_value, preferred_element_type=jnp.float32)
    t_attn = t_attn.reshape(FRAMES * PATCHES, model_width).astype(jnp.bfloat16)
    mixed_t = patches + matmul(t_attn, time_proj) + t_offset
    full_rows = jnp.concatenate([clip_rows[0:1], mixed_t], axis=0)
    s_normed = layer_norm(full_rows, s_gain, s_shift).astype(jnp.bfloat16)
    s_packed = (matmul(s_normed, space_qkv) + qkv_bias(s_pair, model_width)).astype(jnp.bfloat16)
    s_query, s_key, s_value = space_split(s_packed)
    s_raw = space_scores(s_query, s_key, score_scale)
    s_logsum = jax.nn.logsumexp(s_raw, axis=-1, keepdims=True)
    s_probs = jnp.exp(s_raw - s_logsum).astype(jnp.bfloat16)
    s_attn = jnp.einsum("fhij,fjhd->fihd", s_probs, s_value, preferred_element_type=jnp.float32)
    s_attn = s_attn.reshape(FRAMES * (PATCHES + 1), model_width).astype(jnp.bfloat16)
    s_out = (matmul(s_attn, space_proj) + s_offset).reshape(FRAMES, PATCHES + 1, model_width)
    mixed_s = jnp.concatenate(
        [
            full_rows[0:1] + jnp.mean(s_out[:, 0], axis=0)[None],
            mixed_t + s_out[:, 1:].reshape(FRAMES * PATCHES, model_width),
        ],
        axis=0,
    )
    stored = [
        (
            patches,
            t_normed,
            t_packed,
            t_logsum,
            t_attn,
            full_rows,
            s_normed,
            s_packed,
            s_logsum,
            s_attn,
            mixed_s,
        )
    ]
    residual = jnp.concatenate([stored_item[10] for stored_item in stored], axis=0)
    own_rows = residual.shape[0]
    m_normed = layer_norm(residual, m_gain, m_shift).astype(jnp.bfloat16)
    mlp_input = lax.all_gather(m_normed, "narrow", axis=0, tiled=True)
    pre_act = matmul(mlp_input, fc_in) + in_bias.astype(jnp.float32)
    activation = jax.nn.gelu(pre_act, approximate=False).astype(jnp.bfloat16)
    branch = lax.psum_scatter(
        matmul(activation, fc_out).astype(jnp.bfloat16), "narrow", scatter_dimension=0, tiled=True
    ).astype(jnp.float32)
    result = residual + branch + out_bias.astype(jnp.float32)
    layer_out = result.reshape(clip_count, tokens, model_width).astype(jnp.bfloat16)
    grad_low = cotangent.reshape(own_rows, model_width)
    grad_res = grad_low.astype(jnp.float32)
    acc_out_bias = jnp.sum(grad_res, axis=0)
    grad_all = lax.all_gather(grad_low, "narrow", axis=0, tiled=True)
    grad_act = matmul_nt(grad_all, fc_out)
    grad_fc_out = matmul_tn(activation, grad_all)
    gelu_exact = partial(jax.nn.gelu, approximate=False)
    grad_pre = jax.vjp(gelu_exact, pre_act)[1](grad_act)[0].astype(jnp.bfloat16)
    grad_in_bias = jnp.sum(grad_pre.astype(jnp.float32), axis=0)
    grad_fc_in = matmul_tn(mlp_input, grad_pre)
    grad_normed = lax.psum_scatter(
        matmul_nt(grad_pre, fc_in).astype(jnp.bfloat16), "narrow", scatter_dimension=0, tiled=True
    ).astype(jnp.float32)
    _, pull_back = jax.vjp(layer_norm, residual, m_gain, m_shift)
    grad_mixed, acc_m_gain, acc_m_shift = pull_back(grad_normed)
    grad_mixed = grad_mixed + grad_res
    clip_index = 0
    (
        patches,
        t_normed,
        t_packed,
        t_logsum,
        t_attn,
        full_rows,
        s_normed,
        s_packed,
        s_logsum,
        s_attn,
        mixed_s,
    ) = stored[clip_index]
    head_grad = jnp.broadcast_to((grad_mixed[0:1] / FRAMES)[None], (FRAMES, 1, model_width))
    grad_frames = jnp.concatenate(
        [head_grad, grad_mixed[1:].reshape(FRAMES, PATCHES, model_width)], axis=1
    )
    grad_frames = grad_frames.reshape(FRAMES * (PATCHES + 1), model_width).astype(jnp.bfloat16)
    acc_s_offset = jnp.sum(grad_frames.astype(jnp.float32), axis=0)
    acc_s_proj = matmul_tn(s_attn, grad_frames)
    grad_attn = matmul_nt(grad_frames, space_proj).astype(jnp.bfloat16)
    grad_attn = grad_attn.reshape(FRAMES, PATCHES + 1, HEADS, HEAD_DIM)
    s_query, s_key, s_value = space_split(s_packed)
    s_weights = jnp.exp(space_scores(s_query, s_key, score_scale) - s_logsum)
    grad_weights = jnp.einsum(
        "fihd,fjhd->fhij", grad_attn, s_value, preferred_element_type=jnp.float32
    )
    inner_sum = jnp.sum(s_weights * grad_weights, axis=-1, keepdims=True)
    grad_scores = (s_weights * (grad_weights - inner_sum)).astype(jnp.bfloat16)
    grad_query = (
        jnp.einsum("fhij,fjhd->fihd", grad_scores, s_key, preferred_element_type=jnp.float32)
        * score_scale
    )
    grad_key = (
        jnp.einsum("fhij,fihd->fjhd", grad_scores, s_query, preferred_element_type=jnp.float32)
        * score_scale
    )
    grad_value = jnp.einsum(
        "fhij,fihd->fjhd",
        s_weights.astype(jnp.bfloat16),
        grad_attn,
        preferred_element_type=jnp.float32,
    )
    grad_packed = jnp.concatenate(
        [frame_fold(grad_query), frame_fold(grad_key), frame_fold(grad_value)], axis=1
    ).astype(jnp.bfloat16)
    acc_s_qkv = matmul_tn(s_normed, grad_packed)
    acc_s_bias = bias_grads(grad_packed, model_width)
    _, pull_back = jax.vjp(layer_norm, full_rows, s_gain, s_shift)
    grad_full, grad_gain, grad_shift = pull_back(matmul_nt(grad_packed, space_qkv))
    acc_s_gain = grad_gain
    acc_s_shift = grad_shift
    grad_full = grad_full + grad_mixed
    grad_t = grad_full[1:]
    grad_t_low = grad_t.astype(jnp.bfloat16)
    acc_t_offset = jnp.sum(grad_t_low.astype(jnp.float32), axis=0)
    acc_t_proj = matmul_tn(t_attn, grad_t_low)
    grad_attn_t = matmul_nt(grad_t_low, time_proj).astype(jnp.bfloat16)
    grad_attn_t = grad_attn_t.reshape(FRAMES, PATCHES, HEADS, HEAD_DIM)
    t_query, t_key, t_value = time_split(t_packed)
    t_weights = jnp.exp(time_scores(t_query, t_key, score_scale) - t_logsum)
    grad_weights_t = jnp.einsum(
        "fphd,gphd->phfg", grad_attn_t, t_value, preferred_element_type=jnp.float32
    )
    inner_sum_t = jnp.sum(t_weights * grad_weights_t, axis=-1, keepdims=True)
    grad_scores_t = (t_weights * (grad_weights_t - inner_sum_t)).astype(jnp.bfloat16)
    grad_query_t = (
        jnp.einsum("phfg,gphd->fphd", grad_scores_t, t_key, preferred_element_type=jnp.float32)
        * score_scale
    )
    grad_key_t = (
        jnp.einsum("phfg,fphd->gphd", grad_scores_t, t_query, preferred_element_type=jnp.float32)
        * score_scale
    )
    grad_value_t = jnp.einsum(
        "phfg,fphd->gphd",
        t_weights.astype(jnp.bfloat16),
        grad_attn_t,
        preferred_element_type=jnp.float32,
    )
    grad_packed_t = jnp.concatenate(
        [
            grad_query_t.reshape(FRAMES * PATCHES, model_width),
            grad_key_t.reshape(FRAMES * PATCHES, model_width),
            grad_value_t.reshape(FRAMES * PATCHES, model_width),
        ],
        axis=1,
    ).astype(jnp.bfloat16)
    acc_t_qkv = matmul_tn(t_normed, grad_packed_t)
    acc_t_bias = bias_grads(grad_packed_t, model_width)
    _, pull_back = jax.vjp(layer_norm, patches, t_gain, t_shift)
    grad_patch, grad_gain, grad_shift = pull_back(matmul_nt(grad_packed_t, time_qkv))
    grad_list = [jnp.concatenate([grad_full[0:1], grad_t + grad_patch], axis=0)]
    grad_clips = jnp.stack(grad_list, axis=0)
    shard_list = (
        lax.psum_scatter(
            grad_gain.astype(jnp.bfloat16), "narrow", scatter_dimension=0, tiled=True
        ).astype(jnp.float32),
        lax.psum_scatter(
            grad_shift.astype(jnp.bfloat16), "narrow", scatter_dimension=0, tiled=True
        ).astype(jnp.float32),
        lax.psum_scatter(
            acc_t_qkv.astype(jnp.bfloat16), "narrow", scatter_dimension=0, tiled=True
        ).astype(jnp.float32),
        lax.psum_scatter(
            acc_t_bias.astype(jnp.bfloat16), "narrow", scatter_dimension=1, tiled=True
        ).astype(jnp.float32),
        lax.psum_scatter(
            acc_t_proj.astype(jnp.bfloat16), "narrow", scatter_dimension=0, tiled=True
        ).astype(jnp.float32),
        lax.psum_scatter(
            acc_t_offset.astype(jnp.bfloat16), "narrow", scatter_dimension=0, tiled=True
        ).astype(jnp.float32),
        lax.psum_scatter(
            acc_s_gain.astype(jnp.bfloat16), "narrow", scatter_dimension=0, tiled=True
        ).astype(jnp.float32),
        lax.psum_scatter(
            acc_s_shift.astype(jnp.bfloat16), "narrow", scatter_dimension=0, tiled=True
        ).astype(jnp.float32),
        lax.psum_scatter(
            acc_s_qkv.astype(jnp.bfloat16), "narrow", scatter_dimension=0, tiled=True
        ).astype(jnp.float32),
        lax.psum_scatter(
            acc_s_bias.astype(jnp.bfloat16), "narrow", scatter_dimension=1, tiled=True
        ).astype(jnp.float32),
        lax.psum_scatter(
            acc_s_proj.astype(jnp.bfloat16), "narrow", scatter_dimension=0, tiled=True
        ).astype(jnp.float32),
        lax.psum_scatter(
            acc_s_offset.astype(jnp.bfloat16), "narrow", scatter_dimension=0, tiled=True
        ).astype(jnp.float32),
        lax.psum_scatter(
            acc_m_gain.astype(jnp.bfloat16), "narrow", scatter_dimension=0, tiled=True
        ).astype(jnp.float32),
        lax.psum_scatter(
            acc_m_shift.astype(jnp.bfloat16), "narrow", scatter_dimension=0, tiled=True
        ).astype(jnp.float32),
        lax.psum_scatter(
            acc_out_bias.astype(jnp.bfloat16), "narrow", scatter_dimension=0, tiled=True
        ).astype(jnp.float32),
    )
    shard_list = tuple(shard_list[:14]) + (grad_fc_in, grad_in_bias, grad_fc_out, shard_list[14])
    matrix_parts = (
        lax.psum_scatter(shard_list[2], "wide", scatter_dimension=1, tiled=True),
        lax.psum_scatter(shard_list[4], "wide", scatter_dimension=1, tiled=True),
        lax.psum_scatter(shard_list[8], "wide", scatter_dimension=1, tiled=True),
        lax.psum_scatter(shard_list[10], "wide", scatter_dimension=1, tiled=True),
        lax.psum_scatter(shard_list[14], "wide", scatter_dimension=0, tiled=True),
        lax.psum_scatter(shard_list[16], "wide", scatter_dimension=1, tiled=True),
    )
    vector_parts = lax.psum(
        (
            shard_list[0],
            shard_list[1],
            shard_list[3],
            shard_list[5],
            shard_list[6],
            shard_list[7],
            shard_list[9],
            shard_list[11],
            shard_list[12],
            shard_list[13],
            shard_list[15],
            shard_list[17],
        ),
        "wide",
    )
    return (
        layer_out,
        grad_clips,
        vector_parts[0],
        vector_parts[1],
        matrix_parts[0],
        vector_parts[2],
        matrix_parts[1],
        vector_parts[3],
        vector_parts[4],
        vector_parts[5],
        matrix_parts[2],
        vector_parts[6],
        matrix_parts[3],
        vector_parts[7],
        vector_parts[8],
        vector_parts[9],
        matrix_parts[4],
        vector_parts[10],
        matrix_parts[5],
        vector_parts[11],
    )


def solution(mesh):
    return jax.shard_map(
        local,
        mesh=mesh,
        in_specs=(
            P(("wide", "narrow"), None, None),
            P(),
            P(),
            P(),
            P(),
            P(),
            P(),
            P(),
            P(),
            P(),
            P(),
            P(),
            P(),
            P(),
            P(),
            P(None, "narrow"),
            P("narrow"),
            P("narrow", None),
            P(),
            P(("wide", "narrow"), None, None),
        ),
        out_specs=(
            P(("wide", "narrow"), None, None),
            P(("wide", "narrow"), None, None),
            P("narrow"),
            P("narrow"),
            P("narrow", "wide"),
            P(None, "narrow"),
            P("narrow", "wide"),
            P("narrow"),
            P("narrow"),
            P("narrow"),
            P("narrow", "wide"),
            P(None, "narrow"),
            P("narrow", "wide"),
            P("narrow"),
            P("narrow"),
            P("narrow"),
            P("wide", "narrow"),
            P("narrow"),
            P("narrow", "wide"),
            P("narrow"),
        ),
        check_vma=False,
    )
```

profile of v0, /device:TPU:0, one launch (start us, length us, event | category | flops | bytes accessed | tf_op | source)
XLA Modules:
  0.0 1920.8 jit_solution(17432855736144319317)
XLA Ops:
  13.3 6.8 add_convert_fusion.2
  23.3 8.3 reshape.355
  31.6 8.7 reshape.356
  40.4 17.1 multiply_reduce_fusion.3
  60.2 9.5 exponential_reduce_fusion.1
  73.1 8.3 reshape.354
  81.4 10.3 convert_bitcast_fusion.1
  91.7 8.4 copy.217
  100.1 6.3 convert_element_type.239
  115.9 6.9 add_convert_fusion.1
  126.9 8.3 reshape.329
  135.2 8.6 copy.221
  143.8 8.3 reshape.330
  152.1 9.0 copy.223
  163.4 16.4 multiply_reduce_fusion.1
  181.3 12.5 exponential_reduce_fusion
  195.5 8.3 reshape.328
  203.8 8.8 copy.219
  214.2 14.3 convert_bitcast_fusion.2
  240.5 6.3 convolution_add_fusion
  273.8 18.0 copy.226
  292.0 155.5 %all-gather.7.cloned.1.call-done = bf16[4,1569,768]{2,1,0:T(8,128)(2,1)} async-done(((bf16[1,1569,768]{2,1,0:T(8,128)(2,1)}), bf16[4,1569,768]{2,1,0:T(8,128)(2,1)}) %all-gather.7.cloned.1.call-update) | async-done | bytes 9639952 | tf_op jit(solution)/shard_map/all_gather | solution.py:179
  447.4 11.5 reshape.327
  458.9 51.8 %multiply_convert_fusion.1 = (bf16[6276,768]{1,0:T(8,128)(2,1)}, f32[6276,768]{1,0:T(8,128)}, f32[6276,768]{1,0:T(8,128)}) fusion(f32[768]{0:T(1024)S(1)} %convert_element_type.254, bf16[6276,768]{1,0:T(8,128)(2,1)} %reshape.327, bf16[768,768]{1,0:T(8,128)(2,1)} %param.35), kind=kOutput, calls=%fused_computation.8 | convolution fusion | flops 7721588736 | bytes 59022336 | tf_op jit(solution)/shard_map/dot_general | solution.py:24
  510.8 266.2 %all-gather.5.cloned.1.call-done = bf16[1,6276,768]{2,0,1:T(2,128)(2,1)} async-done(((bf16[1,1569,768]{2,0,1:T(2,128)(2,1)}), bf16[1,6276,768]{2,0,1:T(2,128)(2,1)}) %all-gather.5.cloned.1.call-update) | async-done | bytes 9639952 | tf_op jit(solution)/shard_map/all_gather | solution.py:190
  777.0 28.9 %convert_reduce_fusion = (f32[768]{0:T(1024)}, bf16[6276,768]{1,0:T(8,128)(2,1)}) fusion(f32[6276,768]{1,0:T(8,128)} %get-tuple-element.190, bf16[768,768]{1,0:T(8,128)(2,1)} %param.37, bf16[1,6276,768]{2,0,1:T(2,128)(2,1)} %all-gather.5.cloned.1.call-done, f32[6276,768]{1,0:T(8,128)} %get-tuple-element.210, f32[768]{0:T(1024)S(1)} %convert_element_type.254), kind=kOutput, calls=%fused_computation.6 | convolution fusion | flops 7485409280 | bytes 59025408 | tf_op jit(solution)/shard_map/dot_general | solution.py:34
  805.9 13.3 convolution_convert_fusion
  819.1 10.4 convolution_convert_fusion.1
  829.5 323.1 %fusion.73 = (bf16[1576,768]{1,0:T(8,128)(2,1)}, bf16[1576,768]{1,0:T(8,128)(2,1)}) fusion(bf16[6276,768]{1,0:T(8,128)(2,1)} %convolution_convert_fusion.1, bf16[6276,768]{1,0:T(8,128)(2,1)} %convolution_convert_fusion), kind=kCustom, calls=%all-reduce-scatter.2 | all-reduce-scatter fusion | flops 9682945 | bytes 24121856
  1163.3 13.7 concatenate.77
  1183.9 13.4 concatenate.76
  1197.3 9.1 fusion.78
  1229.2 8.3 reshape.357
  1237.5 8.6 copy.228
  1246.1 18.2 multiply_reduce_fusion
  1264.2 14.3 multiply_convert_fusion
  1278.6 6.5 broadcast_multiply_fusion.1
  1288.3 11.1 broadcast_multiply_fusion
  1305.4 13.8 fusion.49
  1364.7 7.0 fusion.74
  1371.7 12.4 fusion.72
  1407.8 8.3 reshape.358
  1416.0 12.5 convolution_convert_fusion.2
  1428.8 9.5 convert_bitcast_fusion
  1438.3 8.5 copy.248
  1446.8 6.3 reshape.323
  1453.1 15.3 multiply_reduce_fusion.2
  1468.4 11.9 multiply_convert_fusion.4
  1480.4 10.2 fusion.23
  1490.5 8.5 copy.246
  1505.3 8.4 fusion.22
  1513.6 8.4 copy.244
  1536.8 10.0 convolution_convert_fusion.3
  1567.1 44.4 %reduce-scatter.29.cloned.1.call-done = bf16[192,2304]{1,0:T(8,128)(2,1)} async-done(((bf16[768,2304]{1,0:T(8,128)(2,1)}), bf16[192,2304]{1,0:T(8,128)(2,1)}) %reduce-scatter.29.cloned.1.call-update) | async-done | bytes 884752 | tf_op jit(solution)/shard_map/reduce_scatter | solution.py:305
  1614.2 13.9 fusion.85
  1631.5 16.0 fusion.9
  1647.6 14.6 multiply_reduce_fusion.8
  1670.4 27.1 %copy.249 = f32[1,1569,768]{2,0,1:T(1,128)} copy(f32[1,1569,768]{2,1,0:T(8,128)S(1)} %maximum_bitcast_fusion) | data formatting | bytes 9639936
  1699.4 18.7 all-reduce.14
  1730.5 23.5 %all-reduce.13 = (f32[192]{0:T(256)}, f32[192]{0:T(256)}, f32[2,192]{1,0:T(2,128)}, f32[192]{0:T(256)}, f32[192]{0:T(256)}, /*index=5*/f32[192]{0:T(256)}, f32[2...) all-reduce(f32[192]{0:T(256)} %dynamic-slice_convert_fusion.8, ...), channel_id=1, replica_groups=mesh['wide'=8,'narrow'=4] {'wide'}, use_global_device_ids=true, to_apply=%region_26.0 | all-reduce | flops 3264 | bytes 24576 | tf_op jit(solution)/shard_map/psum | solution.py:354
  1757.3 17.5 reduce-scatter.47.cloned.1.call-done
  1776.7 44.2 %reduce-scatter.41.cloned.1.call-done = f32[288,192]{1,0:T(8,128)} async-done(((f32[2304,192]{1,0:T(8,128)}), f32[288,192]{1,0:T(8,128)}) %reduce-scatter.41.cloned.1.call-update) | async-done | bytes 221200
  1822.8 44.6 %reduce-scatter.37.cloned.1.call-done = f32[96,768]{1,0:T(8,128)} async-done(((f32[768,768]{1,0:T(8,128)}), f32[96,768]{1,0:T(8,128)}) %reduce-scatter.37.cloned.1.call-update) | async-done | bytes 294928 | tf_op jit(solution)/shard_map/reduce_scatter | solution.py:351
  1867.4 46.6 %reduce-scatter.39.cloned.1.call-done = f32[768,96]{0,1:T(8,128)} async-done(((f32[768,768]{0,1:T(8,128)}), f32[768,96]{0,1:T(8,128)}) %reduce-scatter.39.cloned.1.call-update) | async-done | bytes 294928 | tf_op jit(solution)/shard_map/reduce_scatter | solution.py:352
  (322 shorter events, 268.7 us)
Async XLA Ops:
  7.2 108.7 %copy-start = (bf16[768,2304]{1,0:T(8,128)(2,1)S(1)}, bf16[768,2304]{1,0:T(8,128)(2,1)}, u32[]{:S(2)}) copy-start(bf16[768,2304]{1,0:T(8,128)(2,1)} %param.29) | copy-start | bytes 10616836
  7.2 440.2 %all-gather.7.cloned.1.call-start = ((), (), s32[]{:S(2)}) async-start(), calls=%async_computation.19 | async-start | bytes 12103680 | tf_op jit(solution)/shard_map/all_gather | solution.py:179
  9.5 2.5 copy-start.4
  9.5 3.8 copy-start.60
  10.1 105.2 %copy-start.24 = (f32[1,768]{1,0:T(1,128)}, f32[1,768]{1,0:T(1,128)S(1)}, u32[]{:S(2)}) copy-start(f32[1,768]{1,0:T(1,128)S(1)} %slice_bitcast_fusion) | copy-start | bytes 9220
  113.0 2.3 copy-start.3
  163.4 16.4 copy-start.11
  228.5 12.0 copy-start.56
  267.7 3.1 copy-start.1
  273.8 18.2 copy-start.59
  273.8 503.2 %all-gather.5.cloned.1.call-start = ((), (), s32[]{:S(2)}) async-start(), calls=%async_computation.18 | async-start | bytes 24099840 | tf_op jit(solution)/shard_map/all_gather | solution.py:190
  291.9 1268.2 %reduce-scatter.31.cloned.1.call-start = ((), (), s32[]{:S(2)}) async-start(), calls=%async_computation.13 | async-start | bytes 1474560 | tf_op jit(solution)/shard_map/reduce_scatter | solution.py:311
  805.9 13.3 copy-start.61
  805.9 13.3 copy-start.62
  1152.6 24.4 %copy-start.18 = (f32[1569]{0:T(1024)S(1)}, f32[1569]{0:T(1024)}, u32[]{:S(2)}) copy-start(f32[1569]{0:T(1024)} %copy-done.17) | copy-start | bytes 18832
  1152.6 24.4 %copy-start.22 = (f32[1569]{0:T(1024)S(1)}, f32[1569]{0:T(1024)}, u32[]{:S(2)}) copy-start(f32[1569]{0:T(1024)} %copy-done.21) | copy-start | bytes 18832
  1154.1 9.3 collective-permute-start.1
  1160.6 23.3 %collective-permute-start = (bf16[21,768]{1,0:T(8,128)(2,1)}, bf16[21,768]{1,0:T(8,128)(2,1)}, u32[]{:S(2)}, u32[]{:S(2)}) collective-permute-start(bf16[21,768]{1,0:T(8,128)(2,1)} %slice.191), channel_id=1, source_target_pairs={{0,1},{1,2},{2,3},{4,5},{5,6},{6,7},{8,9},{9,10},{10,11},{12,13},{... | collective-permute-start | bytes 96776
  1177.0 6.3 copy-start.35
  1197.3 9.1 copy-start.10
  1207.1 3.0 copy-start.6
  1264.2 14.3 copy-start.12
  1278.6 6.5 copy-start.2
  1299.4 5.7 copy-start.9
  1319.2 5.7 copy-start.8
  1364.6 7.0 copy-start.20
  1364.6 7.0 copy-start.25
  1364.7 7.0 copy-start.38
  1364.7 19.5 %slice-start = ((s8[4816896]{0:T(1024)(128)(4,1)}), s8[4194304]{0:T(1024)(128)(4,1)S(1)}, s32[]{:S(2)}) async-start(s8[4816896]{0:T(1024)(128)(4,1)} %bitcast.131), calls=%async_computation.26 | async-start | bytes 8388608
  1364.7 22.7 %slice-start.4 = ((s8[4841472]{0:T(1024)(128)(4,1)}), s8[4194304]{0:T(1024)(128)(4,1)S(1)}, s32[]{:S(2)}) async-start(s8[4841472]{0:T(1024)(128)(4,1)} %bitcast.137), calls=%async_computation.30 | async-start | bytes 8388608
  1371.6 12.5 copy-start.15
  1371.7 12.5 copy-start.33
  1371.7 12.5 slice-start.1
  1371.7 12.5 copy-start.29
  1371.7 15.7 slice-start.5
  1387.4 4.4 copy-start.16
  1395.2 167.0 %reduce-scatter.35.cloned.1.call-start = ((), (), s32[]{:S(2)}) async-start(), calls=%async_computation.15 | async-start | bytes 1474560 | tf_op jit(solution)/shard_map/reduce_scatter | solution.py:329
  1401.5 162.8 %reduce-scatter.33.cloned.1.call-start = ((), (), s32[]{:S(2)}) async-start(), calls=%async_computation.14 | async-start | bytes 4423680 | tf_op jit(solution)/shard_map/reduce_scatter | solution.py:323
  1428.6 182.9 %reduce-scatter.29.cloned.1.call-start = ((), (), s32[]{:S(2)}) async-start(), calls=%async_computation.12 | async-start | bytes 4423680 | tf_op jit(solution)/shard_map/reduce_scatter | solution.py:305
  1528.4 4.9 copy-start.14
  1528.4 8.3 slice-start.2
  1530.5 6.3 slice-start.3
  1530.5 6.3 copy-start.27
  1530.5 6.3 copy-start.40
  1530.5 6.3 copy-start.42
  1530.5 6.3 copy-start.48
  1533.7 3.0 copy-start.13
  1546.8 182.0 %reduce-scatter.49.cloned.1.call-start = ((), (), s32[]{:S(2)}) async-start(), calls=%async_computation.24 | async-start | bytes 245760
  1557.1 172.5 %reduce-scatter.43.cloned.1.call-start = ((), (), s32[]{:S(2)}) async-start(), calls=%async_computation.21 | async-start | bytes 245760
  1560.0 194.1 %reduce-scatter.45.cloned.1.call-start = ((), (), s32[]{:S(2)}) async-start(), calls=%async_computation.22 | async-start | bytes 884736
  1562.1 193.6 %reduce-scatter.51.cloned.1.call-start = ((), (), s32[]{:S(2)}) async-start(), calls=%async_computation.25 | async-start | bytes 884736
  1564.2 210.6 %reduce-scatter.47.cloned.1.call-start = ((), (), s32[]{:S(2)}) async-start(), calls=%async_computation.23 | async-start | bytes 2654208
  1567.1 253.9 %reduce-scatter.41.cloned.1.call-start = ((), (), s32[]{:S(2)}) async-start(), calls=%async_computation.20 | async-start | bytes 2654208
  1614.1 253.3 %reduce-scatter.37.cloned.1.call-start = ((), (), s32[]{:S(2)}) async-start(), calls=%async_computation.16 | async-start | bytes 2654208 | tf_op jit(solution)/shard_map/reduce_scatter | solution.py:351
  1628.1 286.0 %reduce-scatter.39.cloned.1.call-start = ((), (), s32[]{:S(2)}) async-start(), calls=%async_computation.17 | async-start | bytes 2654208 | tf_op jit(solution)/shard_map/reduce_scatter | solution.py:352
  1647.6 14.6 copy-start.31
  1647.6 14.6 copy-start.43
  1666.8 3.3 slice-start.8
  1670.0 28.2 %slice-start.6 = ((s8[4841472]{0:T(1024)(128)(4,1)}), s8[647168]{0:T(1024)(128)(4,1)S(1)}, s32[]{:S(2)}) async-start(s8[4841472]{0:T(1024)(128)(4,1)} %bitcast.139), calls=%async_computation.32 | async-start | bytes 1294336
  1670.4 27.2 %copy-start.5 = (bf16[1597,768]{1,0:T(8,128)(2,1)S(1)}, bf16[1597,768]{1,0:T(8,128)(2,1)}, u32[]{:S(2)}) copy-start(bf16[1597,768]{1,0:T(8,128)(2,1)} %concatenate.77) | copy-start | bytes 7358980
  1670.4 27.9 %slice-start.7 = ((s8[4841472]{0:T(1024)(128)(4,1)}), s8[4194304]{0:T(1024)(128)(4,1)S(1)}, s32[]{:S(2)}) async-start(s8[4841472]{0:T(1024)(128)(4,1)} %bitcast.139), calls=%async_computation.33 | async-start | bytes 8388608
  1670.4 29.0 %copy-start.44 = (bf16[768]{0:T(1024)(128)(2,1)S(1)}, bf16[768]{0:T(1024)(128)(2,1)}, u32[]{:S(2)}) copy-start(bf16[768]{0:T(1024)(128)(2,1)} %get-tuple-element.183) | copy-start | bytes 4612
  1670.4 29.0 %copy-start.45 = (bf16[768]{0:T(1024)(128)(2,1)S(1)}, bf16[768]{0:T(1024)(128)(2,1)}, u32[]{:S(2)}) copy-start(bf16[768]{0:T(1024)(128)(2,1)} %get-tuple-element.140) | copy-start | bytes 4612
  1670.4 29.0 %copy-start.46 = (bf16[768]{0:T(1024)(128)(2,1)S(1)}, bf16[768]{0:T(1024)(128)(2,1)}, u32[]{:S(2)}) copy-start(bf16[768]{0:T(1024)(128)(2,1)} %reduce_sum.403) | copy-start | bytes 4612
  (24 other events, 31.3 us)
Sparse Core Ops, SparseCore 0:
  273.9 173.4 all-gather.6
  449.6 327.3 all-gather.4
  1395.3 27.3 reduce-scatter.30
  1424.9 27.8 reduce-scatter.34
  1455.0 65.0 reduce-scatter.32
  1546.9 64.5 reduce-scatter.28
  1614.3 19.6 reduce-scatter.48
  1636.9 17.5 reduce-scatter.42
  1657.7 33.2 reduce-scatter.44
  1693.9 34.9 reduce-scatter.50
  1732.3 42.5 reduce-scatter.46
  1778.4 42.4 reduce-scatter.40
  1824.9 42.5 reduce-scatter.36
  1871.6 42.4 reduce-scatter.38
where the time goes:
time: 1940 us; the launch traced here: 1920 us
  waiting for transfers between devices  619 us (32%)
  local copies, waits for them, and re-layouts  391 us (20%)
  matrix products  382 us (20%)
  blocking collectives  365 us (19%)
  other arithmetic  141 us (7%)
    unnamed x2, blocking collectives  342 us
    all_gather x1, waiting for transfers between devices, local(): grad_all = lax.all_gather(grad_low, 'narrow', axis=0, tiled=True)  266 us
    all_gather x1, waiting for transfers between devices, local(): mlp_input = lax.all_gather(m_normed, 'narrow', axis=0, tiled=True)  155 us
    unnamed x167, local copies, waits for them, and re-layouts  139 us
    dot_general x6, matrix products, matmul(): return jnp.dot(left_op, right_op, preferred_element_type=jnp.float32)  88.2 us
    dot_general x6, matrix products, matmul_nt(): lax.dot_general(left_op, right_op, (((1,), (1,)), ((), ())), preferred_el...  80.9 us
    unnamed x22, waiting for transfers between devices  62 us
    dot_general x6, matrix products, matmul_tn(): lax.dot_general(left_op, right_op, (((0,), (0,)), ((), ())), preferred_el...  61.5 us
  transfers between devices with their start and end apart: 16, of which 7 were waited for; matrix products, arithmetic and copies ran while one was open for 20% of the time, Pallas kernels for 0%

commit v1 on v0

v1 whole, which is shorter than its diff:
```python
from functools import partial

import jax
import jax.numpy as jnp
from jax import lax
from jax.experimental import pallas as pl
from jax.experimental.pallas import tpu as pltpu
from jax.sharding import PartitionSpec as P

HEADS = 12
HEAD_DIM = 64
FRAMES = 8
PATCHES = 196
ROWS = 208
CLASS = 196
TILE = 16
WIDTH = 768
GROUP = 4
GW = GROUP * HEAD_DIM
GROUPS = HEADS // GROUP
FPS = 2
STEP = FPS * ROWS
EPSILON = 1e-06
F32 = jnp.float32
BF = jnp.bfloat16
NEG = -1e30
VMEM_LIMIT = 60 * 2**20


def dg(a, b, ca, cb):
    return lax.dot_general(a, b, (((ca,), (cb,)), ((), ())), preferred_element_type=F32)


def nn(a, b):
    return dg(a, b, 1, 0)


def nt(a, b):
    return dg(a, b, 1, 1)


def tn(a, b):
    return dg(a, b, 0, 0)


def call(kernel, name, grid, ins, outs, scratch=(), flops=0, nbytes=0):
    return pl.pallas_call(
        kernel,
        name=name,
        grid=grid,
        in_specs=[s for s in ins],
        out_specs=[s for s, _ in outs],
        out_shape=[t for _, t in outs],
        scratch_shapes=list(scratch),
        compiler_params=pltpu.CompilerParams(vmem_limit_bytes=VMEM_LIMIT),
        cost_estimate=pl.CostEstimate(flops=flops, bytes_accessed=nbytes, transcendentals=0),
    )


def whole(*shape):
    return pl.BlockSpec(shape, lambda *i: (0,) * len(shape))


def frames(width):
    return pl.BlockSpec((FPS, ROWS, width), lambda i: (i, 0, 0))


def frames_out(width, dtype):
    return frames(width), jax.ShapeDtypeStruct((FRAMES, ROWS, width), dtype)


def normed(v):
    center = v - jnp.mean(v, axis=-1, keepdims=True)
    scale = lax.rsqrt(jnp.mean(center * center, axis=-1, keepdims=True) + EPSILON)
    return center * scale, scale


def norm_back(grad, xhat, scale, gain):
    g = grad * gain
    m1 = jnp.mean(g, axis=-1, keepdims=True)
    m2 = jnp.mean(g * xhat, axis=-1, keepdims=True)
    return scale * (g - m1 - xhat * m2)


def colsum(v):
    return jnp.sum(v.astype(F32), axis=0, keepdims=True)


def head_masked(block):
    lane = lax.broadcasted_iota(jnp.int32, block.shape, 1) // HEAD_DIM
    zero = jnp.zeros_like(block)
    return jnp.concatenate([jnp.where(lane == h, block, zero) for h in range(GROUP)], axis=0)


def head_select(stacked):
    rows = stacked.shape[0] // GROUP
    lane = lax.broadcasted_iota(jnp.int32, (rows, GW), 1) // HEAD_DIM
    out = stacked[:rows]
    for h in range(1, GROUP):
        out = jnp.where(lane == h, stacked[h * rows : (h + 1) * rows], out)
    return out


def softmax(scores):
    e = jnp.exp(scores - jnp.max(scores, axis=-1, keepdims=True))
    return (e * (1.0 / jnp.sum(e, axis=-1, keepdims=True))).astype(BF)


def group_cols(g, which):
    start = which * WIDTH + g * GW
    return slice(start, start + GW)


def shifted(src_ref, frame, first_row, class_on):
    start = 1 + frame * PATCHES
    base = jnp.minimum(start // TILE * TILE, src_ref.shape[0] // TILE * TILE - ROWS - TILE)
    base = pl.multiple_of(base, TILE)
    chunk = src_ref[pl.ds(base, ROWS + TILE), :]
    row = lax.broadcasted_iota(jnp.int32, (ROWS, ROWS + TILE), 0)
    col = lax.broadcasted_iota(jnp.int32, (ROWS, ROWS + TILE), 1)
    pick = ((col == row + (start - base)) & (row < PATCHES)).astype(F32).astype(BF)
    got = nn(pick, chunk)
    last = src_ref.shape[0] - 1
    end_row = src_ref[last : last + 1, :].astype(F32)
    tail = got[ROWS - TILE :]
    trow = lax.broadcasted_iota(jnp.int32, tail.shape, 0) + (ROWS - TILE)
    tail = jnp.where((trow == PATCHES - 1) & (frame == FRAMES - 1), end_row, tail)
    tail = jnp.where((trow == CLASS) & class_on, first_row, tail)
    return jnp.concatenate([got[: ROWS - TILE], tail], axis=0)


def time_in_kernel(clip_ref, cot_ref, vec_ref, bias_ref, w_ref, p_ref, g_ref, h_ref, z_ref):
    step = pl.program_id(0)
    parts = []
    for j in range(FPS):
        frame = step * FPS + j
        p = shifted(clip_ref, frame, clip_ref[0:1, :].astype(F32), frame >= 0)
        p_ref[j] = p.astype(BF)
        xhat, _ = normed(p)
        parts.append((xhat * vec_ref[0:1] + vec_ref[1:2]).astype(BF))
        g_ref[j] = shifted(cot_ref, frame, cot_ref[0:1, :].astype(F32), frame == 0).astype(BF)
    h = jnp.concatenate(parts, axis=0)
    h_ref[...] = h.reshape(FPS, ROWS, WIDTH)
    project(h, w_ref, bias_ref, z_ref)


def project(h, w_ref, bias_ref, z_ref):
    for which in range(3):
        cols = slice(which * WIDTH, (which + 1) * WIDTH)
        z = nn(h, w_ref[:, cols])
        if which != 1:
            z = z + bias_ref[which // 2 : which // 2 + 1]
        z = z.astype(BF)
        if which == 0:
            z = z * jnp.asarray(HEAD_DIM**-0.5, BF)
        z_ref[:, :, cols] = z.reshape(FPS, ROWS, WIDTH)


def time_attention_kernel(z_ref, o_ref, a_ref):
    z = z_ref[...].reshape(FRAMES * TILE, 3 * WIDTH)
    row = lax.broadcasted_iota(jnp.int32, (GROUP * FRAMES * TILE, FRAMES * TILE), 0)
    col = lax.broadcasted_iota(jnp.int32, (GROUP * FRAMES * TILE, FRAMES * TILE), 1)
    same = (row % TILE) == (col % TILE)
    for g in range(GROUPS):
        q = head_masked(z[:, group_cols(g, 0)])
        s = jnp.where(same, nt(q, z[:, group_cols(g, 1)]), NEG)
        a = softmax(s)
        a_ref[0, g] = a
        o = head_select(nn(a, z[:, group_cols(g, 2)])).astype(BF)
        o_ref[:, :, g * GW : (g + 1) * GW] = o.reshape(FRAMES, TILE, GW)


def space_kernel(
    p_ref, ot_ref, vec_ref, bias_ref, wt_ref, w_ref, wo_ref,
    full_ref, h_ref, z_ref, a_ref, o_ref, x_ref, cls_ref,
):
    p = p_ref[...].reshape(STEP, WIDTH).astype(F32)
    mixed = p + nn(ot_ref[...].reshape(STEP, WIDTH), wt_ref[...]) + vec_ref[2:3]
    row = lax.broadcasted_iota(jnp.int32, (STEP, WIDTH), 0) % ROWS
    full = jnp.where(row == CLASS, p, mixed)
    full_ref[...] = full.reshape(FPS, ROWS, WIDTH)
    xhat, _ = normed(full)
    h = (xhat * vec_ref[3:4] + vec_ref[4:5]).astype(BF)
    h_ref[...] = h.reshape(FPS, ROWS, WIDTH)
    project(h, w_ref, bias_ref, z_ref)
    key = lax.broadcasted_iota(jnp.int32, (GROUP * ROWS, ROWS), 1)
    for j in range(FPS):
        for g in range(GROUPS):
            q = head_masked(z_ref[j, :, group_cols(g, 0)])
            s = jnp.where(key <= CLASS, nt(q, z_ref[j, :, group_cols(g, 1)]), NEG)
            a = softmax(s)
            a_ref[j, g] = a
            o = head_select(nn(a, z_ref[j, :, group_cols(g, 2)])).astype(BF)
            o_ref[j, :, g * GW : (g + 1) * GW] = o
    y = nn(o_ref[...].reshape(STEP, WIDTH), wo_ref[...]) + vec_ref[5:6]
    x_ref[...] = (full + y).reshape(FPS, ROWS, WIDTH)
    for j in range(FPS):
        at = j * ROWS + CLASS - CLASS % 8
        cls_ref[j] = y[at : at + 8]


def mlp_kernel(
    x_ref, cls_ref, p_ref, g_ref, vec_ref, b_ref, wi_ref, wo_ref,
    out_ref, h_ref, act_ref, dpre_ref, dx_ref, gv_ref, gb_ref,
):
    slices = wi_ref.shape[0]
    step = pl.program_id(0)

    @pl.when(step == 0)
    def _():
        gv_ref[...] = jnp.zeros_like(gv_ref)
        gb_ref[...] = jnp.zeros_like(gb_ref)

    mean_cls = jnp.mean(cls_ref[:, CLASS % 8, :], axis=0, keepdims=True)
    first = p_ref[0, CLASS % TILE : CLASS % TILE + 1, :].astype(F32) + mean_cls
    row = lax.broadcasted_iota(jnp.int32, (STEP, WIDTH), 0) % ROWS
    x = jnp.where(row == CLASS, first, x_ref[...].reshape(STEP, WIDTH))
    g = g_ref[...].reshape(STEP, WIDTH)
    xhat, scale = normed(x)
    h = (xhat * vec_ref[6:7] + vec_ref[7:8]).astype(BF)
    h_ref[...] = h.reshape(FPS, ROWS, WIDTH)
    out = x + vec_ref[8:9]
    dh = jnp.zeros((STEP, WIDTH), F32)
    for s in range(slices):
        cols = slice(s * WIDTH, (s + 1) * WIDTH)
        pre = nn(h, wi_ref[s]) + b_ref[:, cols]
        cdf = 0.5 + 0.5 * lax.erf(pre * (0.5**0.5))
        act = (pre * cdf).astype(BF)
        slope = cdf + pre * (jnp.exp(-0.5 * pre * pre) * 0.3989422804014327)
        act_ref[:, :, cols] = act.reshape(FPS, ROWS, WIDTH)
        dpre = (nt(g, wo_ref[s]) * slope).astype(BF)
        dpre_ref[:, :, cols] = dpre.reshape(FPS, ROWS, WIDTH)
        gb_ref[0:1, cols] += colsum(dpre)
        out = out + nn(act, wo_ref[s])
        dh = dh + nt(dpre, wi_ref[s])
    out_ref[...] = out.astype(BF).reshape(FPS, ROWS, WIDTH)
    gf = g.astype(F32)
    dx_ref[...] = (gf + norm_back(dh, xhat, scale, vec_ref[6:7])).reshape(FPS, ROWS, WIDTH)
    gv_ref[0:1] += colsum(dh * xhat)
    gv_ref[1:2] += colsum(dh)
    gv_ref[2:3] += colsum(gf)


def space_back_kernel(
    dx_ref, dcls_ref, full_ref, z_ref, a_ref, vec_ref, wo_ref, w_ref, wt_ref,
    dy_ref, dz_ref, df_ref, dyt_ref, dot_ref, gv_ref, do_ref,
):
    step = pl.program_id(0)

    @pl.when(step == 0)
    def _():
        gv_ref[...] = jnp.zeros_like(gv_ref)

    dx = dx_ref[...].reshape(STEP, WIDTH)
    row = lax.broadcasted_iota(jnp.int32, (STEP, WIDTH), 0) % ROWS
    dcls = dcls_ref[0, CLASS % 8 : CLASS % 8 + 1, :] * (1.0 / FRAMES)
    dy = jnp.where(row == CLASS, dcls, jnp.where(row < CLASS, dx, 0.0)).astype(BF)
    dy_ref[...] = dy.reshape(FPS, ROWS, WIDTH)
    gv_ref[0:1, :WIDTH] += colsum(dy)
    do_ref[...] = nt(dy, wo_ref[...]).astype(BF)
    for j in range(FPS):
        for g in range(GROUPS):
            a = a_ref[j, g]
            q = head_masked(z_ref[j, :, group_cols(g, 0)])
            k = z_ref[j, :, group_cols(g, 1)]
            do = head_masked(do_ref[j * ROWS : (j + 1) * ROWS, g * GW : (g + 1) * GW])
            da = nt(do, z_ref[j, :, group_cols(g, 2)])
            af = a.astype(F32)
            ds = (af * (da - jnp.sum(af * da, axis=-1, keepdims=True))).astype(BF)
            dz_ref[j, :, group_cols(g, 0)] = (head_select(nn(ds, k)) * HEAD_DIM**-0.5).astype(BF)
            dz_ref[j, :, group_cols(g, 1)] = tn(ds, q).astype(BF)
            dz_ref[j, :, group_cols(g, 2)] = tn(a, do).astype(BF)
    dz = dz_ref[...].reshape(STEP, 3 * WIDTH)
    gv_ref[1:2, :] += colsum(dz)
    dh = nt(dz, w_ref[...])
    xhat, scale = normed(full_ref[...].reshape(STEP, WIDTH))
    gv_ref[2:3, :WIDTH] += colsum(dh * xhat)
    gv_ref[3:4, :WIDTH] += colsum(dh)
    df = dx + norm_back(dh, xhat, scale, vec_ref[3:4])
    df_ref[...] = df.reshape(FPS, ROWS, WIDTH)
    dyt = jnp.where(row < CLASS, df, 0.0).astype(BF)
    dyt_ref[...] = dyt.reshape(FPS, ROWS, WIDTH)
    gv_ref[4:5, :WIDTH] += colsum(dyt)
    dot_ref[...] = nt(dyt, wt_ref[...]).astype(BF).reshape(FPS, ROWS, WIDTH)


def time_back_kernel(z_ref, a_ref, do_ref, dz_ref):
    z = z_ref[...].reshape(FRAMES * TILE, 3 * WIDTH)
    dot = do_ref[...].reshape(FRAMES * TILE, WIDTH)
    for g in range(GROUPS):
        a = a_ref[0, g]
        q = head_masked(z[:, group_cols(g, 0)])
        do = head_masked(dot[:, g * GW : (g + 1) * GW])
        da = nt(do, z[:, group_cols(g, 2)])
        af = a.astype(F32)
        ds = (af * (da - jnp.sum(af * da, axis=-1, keepdims=True))).astype(BF)
        dq = head_select(nn(ds, z[:, group_cols(g, 1)])) * HEAD_DIM**-0.5
        for which, v in enumerate((dq, tn(ds, q), tn(a, do))):
            dz_ref[:, :, group_cols(g, which)] = v.astype(BF).reshape(FRAMES, TILE, GW)


def time_out_kernel(dz_ref, p_ref, df_ref, vec_ref, w_ref, dp_ref, gv_ref):
    step = pl.program_id(0)

    @pl.when(step == 0)
    def _():
        gv_ref[...] = jnp.zeros_like(gv_ref)

    dz = dz_ref[...].reshape(STEP, 3 * WIDTH)
    gv_ref[0:1, :] += colsum(dz)
    dh = nt(dz, w_ref[...])
    xhat, scale = normed(p_ref[...].reshape(STEP, WIDTH).astype(F32))
    gv_ref[1:2, :WIDTH] += colsum(dh * xhat)
    gv_ref[2:3, :WIDTH] += colsum(dh)
    dp = df_ref[...].reshape(STEP, WIDTH) + norm_back(dh, xhat, scale, vec_ref[0:1])
    dp_ref[...] = dp.reshape(FPS, ROWS, WIDTH)


def weight_grad(a, b, name, tile):
    rows, width = a.shape
    out_width = b.shape[1]

    def kernel(a_ref, b_ref, o_ref):
        o_ref[...] = tn(a_ref[...], b_ref[...]).astype(BF)

    return call(
        kernel,
        name,
        (width // tile,),
        [pl.BlockSpec((rows, tile), lambda i: (0, i)), whole(rows, out_width)],
        [(pl.BlockSpec((tile, out_width), lambda i: (i, 0)), jax.ShapeDtypeStruct((width, out_width), BF))],
        flops=2 * rows * width * out_width,
        nbytes=2 * (rows * width + rows * out_width + width * out_width),
    )(a, b)[0]


def unpad(padded, first):
    body = padded[:, :PATCHES].reshape(FRAMES * PATCHES, WIDTH)
    return jnp.concatenate([first, body], axis=0)[None]


def local(
    video_clips, time_gain, time_shift, time_qkv, time_bias, time_proj, time_offset,
    space_gain, space_shift, space_qkv, space_bias, space_proj, space_offset,
    mlp_gain, mlp_shift, fc_in, in_bias, fc_out, out_bias, cotangent,
):
    slices = lax.axis_size("narrow")
    hidden = slices * WIDTH
    tokens = video_clips.shape[1]
    clip = video_clips[0]
    cot = cotangent[0]
    vec = jnp.stack(
        [time_gain, time_shift, time_offset, space_gain, space_shift, space_offset, mlp_gain, mlp_shift, out_bias]
    ).astype(F32)
    nvec = vec.shape[0]
    t_bias = time_bias.astype(F32)
    s_bias = space_bias.astype(F32)
    wi = lax.all_gather(fc_in, "narrow", axis=0)
    wo = lax.all_gather(fc_out, "narrow", axis=0)
    b_in = lax.all_gather(in_bias.astype(F32), "narrow", axis=0, tiled=True)[None]

    chunks = ROWS // TILE
    a_time = (pl.BlockSpec((1, GROUPS, GROUP * FRAMES * TILE, FRAMES * TILE), lambda i: (i, 0, 0, 0)),
              jax.ShapeDtypeStruct((chunks, GROUPS, GROUP * FRAMES * TILE, FRAMES * TILE), BF))
    a_space = (pl.BlockSpec((FPS, GROUPS, GROUP * ROWS, ROWS), lambda i: (i, 0, 0, 0)),
               jax.ShapeDtypeStruct((FRAMES, GROUPS, GROUP * ROWS, ROWS), BF))

    def chunk(width):
        return pl.BlockSpec((FRAMES, TILE, width), lambda i: (0, i, 0))

    def chunk_out(width):
        return chunk(width), jax.ShapeDtypeStruct((FRAMES, ROWS, width), BF)

    rows = FRAMES * ROWS
    steps = (FRAMES // FPS,)
    p, g, ht, zt = call(
        time_in_kernel, "time_in", steps,
        [whole(tokens, WIDTH), whole(tokens, WIDTH), whole(nvec, WIDTH), whole(2, WIDTH), whole(WIDTH, 3 * WIDTH)],
        [frames_out(WIDTH, BF), frames_out(WIDTH, BF), frames_out(WIDTH, BF), frames_out(3 * WIDTH, BF)],
        flops=6 * rows * WIDTH * WIDTH, nbytes=24 * 2**20,
    )(clip, cot, vec, t_bias, time_qkv)
    ot, at = call(
        time_attention_kernel, "time_attention", (chunks,),
        [chunk(3 * WIDTH)], [chunk_out(WIDTH), a_time],
        flops=10**10, nbytes=16 * 2**20,
    )(zt)
    full, hs, zs, a_s, o_s, xs, ycls = call(
        space_kernel, "space", steps,
        [frames(WIDTH), frames(WIDTH), whole(nvec, WIDTH), whole(2, WIDTH),
         whole(WIDTH, WIDTH), whole(WIDTH, 3 * WIDTH), whole(WIDTH, WIDTH)],
        [frames_out(WIDTH, F32), frames_out(WIDTH, BF), frames_out(3 * WIDTH, BF), a_space,
         frames_out(WIDTH, BF), frames_out(WIDTH, F32),
         (pl.BlockSpec((FPS, 8, WIDTH), lambda i: (i, 0, 0)), jax.ShapeDtypeStruct((FRAMES, 8, WIDTH), F32))],
        flops=3 * 10**10, nbytes=40 * 2**20,
    )(p, ot, vec, s_bias, time_proj, space_qkv, space_proj)
    out, hm, act, dpre, dxs, gv_m, gb_m = call(
        mlp_kernel, "mlp", steps,
        [frames(WIDTH), whole(FRAMES, 8, WIDTH),
         pl.BlockSpec((1, TILE, WIDTH), lambda i: (0, CLASS // TILE, 0)), frames(WIDTH),
         whole(nvec, WIDTH), whole(1, hidden), whole(slices, WIDTH, WIDTH), whole(slices, WIDTH, WIDTH)],
        [frames_out(WIDTH, BF), frames_out(WIDTH, BF), frames_out(hidden, BF), frames_out(hidden, BF),
         frames_out(WIDTH, F32),
         (whole(8, WIDTH), jax.ShapeDtypeStruct((8, WIDTH), F32)),
         (whole(8, hidden), jax.ShapeDtypeStruct((8, hidden), F32))],
        flops=8 * rows * WIDTH * hidden, nbytes=50 * 2**20,
    )(xs, ycls, p, g, vec, b_in, wi, wo)
    g_fc_in = weight_grad(hm.reshape(rows, WIDTH), dpre.reshape(rows, hidden), "grad_fc_in", 256)
    g_fc_out = weight_grad(g.reshape(rows, WIDTH), act.reshape(rows, hidden), "grad_fc_out", 256)
    dys, dzs, df, dyt, dot, gv_s = call(
        space_back_kernel, "space_back", steps,
        [frames(WIDTH), pl.BlockSpec((1, 8, WIDTH), lambda i: (0, CLASS // 8, 0)), frames(WIDTH),
         frames(3 * WIDTH), a_space[0], whole(nvec, WIDTH),
         whole(WIDTH, WIDTH), whole(WIDTH, 3 * WIDTH), whole(WIDTH, WIDTH)],
        [frames_out(WIDTH, BF), frames_out(3 * WIDTH, BF), frames_out(WIDTH, F32),
         frames_out(WIDTH, BF), frames_out(WIDTH, BF),
         (whole(8, 3 * WIDTH), jax.ShapeDtypeStruct((8, 3 * WIDTH), F32))],
        scratch=[pltpu.VMEM((STEP, WIDTH), BF)],
        flops=3 * 10**10, nbytes=50 * 2**20,
    )(dxs, dxs, full, zs, a_s, vec, space_proj, space_qkv, time_proj)
    g_s_proj = weight_grad(o_s.reshape(rows, WIDTH), dys.reshape(rows, WIDTH), "grad_space_proj", 384)
    g_s_qkv = weight_grad(dzs.reshape(rows, 3 * WIDTH), hs.reshape(rows, WIDTH), "grad_space_qkv", 768)
    dzt, = call(
        time_back_kernel, "time_back", (chunks,),
        [chunk(3 * WIDTH), a_time[0], chunk(WIDTH)], [chunk_out(3 * WIDTH)],
        flops=10**10, nbytes=24 * 2**20,
    )(zt, at, dot)
    g_t_proj = weight_grad(ot.reshape(rows, WIDTH), dyt.reshape(rows, WIDTH), "grad_time_proj", 384)
    g_t_qkv = weight_grad(dzt.reshape(rows, 3 * WIDTH), ht.reshape(rows, WIDTH), "grad_time_qkv", 768)
    dp, gv_t = call(
        time_out_kernel, "time_out", steps,
        [frames(3 * WIDTH), frames(WIDTH), frames(WIDTH), whole(nvec, WIDTH), whole(WIDTH, 3 * WIDTH)],
        [frames_out(WIDTH, F32), (whole(8, 3 * WIDTH), jax.ShapeDtypeStruct((8, 3 * WIDTH), F32))],
        flops=6 * rows * WIDTH * WIDTH, nbytes=28 * 2**20,
    )(dzt, p, df, vec, time_qkv)

    layer_out = unpad(out, out[0, CLASS : CLASS + 1])
    grad_clips = unpad(dp, jnp.sum(df[:, CLASS], axis=0, keepdims=True))

    def scatter(grad, swap):
        part = lax.psum_scatter(grad, "wide", scatter_dimension=0, tiled=True)
        part = lax.psum_scatter(part, "narrow", scatter_dimension=1, tiled=True)
        part = part.astype(F32)
        return part.T if swap else part

    vectors = jnp.stack(
        [gv_m[0], gv_m[1], gv_m[2],
         gv_s[0, :WIDTH], gv_s[1, :WIDTH], gv_s[1, 2 * WIDTH :], gv_s[2, :WIDTH], gv_s[3, :WIDTH], gv_s[4, :WIDTH],
         gv_t[0, :WIDTH], gv_t[0, 2 * WIDTH :], gv_t[1, :WIDTH], gv_t[2, :WIDTH]]
    )
    vectors = jnp.concatenate([vectors, gb_m[0].reshape(slices, WIDTH)], axis=0)
    vectors = lax.psum(vectors, ("wide", "narrow"))
    me = lax.axis_index("narrow")
    share = WIDTH // slices
    mine = lax.dynamic_slice(vectors, (0, me * share), (13, share))
    grad_in_bias = lax.dynamic_slice(vectors, (13 + me, 0), (1, WIDTH))[0]
    return (
        layer_out,
        grad_clips,
        mine[11],
        mine[12],
        scatter(g_t_qkv, True),
        mine[9:11],
        scatter(g_t_proj.T, True),
        mine[8],
        mine[6],
        mine[7],
        scatter(g_s_qkv, True),
        mine[4:6],
        scatter(g_s_proj.T, True),
        mine[3],
        mine[0],
        mine[1],
        scatter(g_fc_in, False),
        grad_in_bias,
        scatter(g_fc_out, True),
        mine[2],
    )


def solution(mesh):
    rows = P(("wide", "narrow"), None, None)
    return jax.shard_map(
        local,
        mesh=mesh,
        in_specs=(rows,) + (P(),) * 14 + (P(None, "narrow"), P("narrow"), P("narrow", None), P(), rows),
        out_specs=(
            rows,
            rows,
            P("narrow"),
            P("narrow"),
            P("narrow", "wide"),
            P(None, "narrow"),
            P("narrow", "wide"),
            P("narrow"),
            P("narrow"),
            P("narrow"),
            P("narrow", "wide"),
            P(None, "narrow"),
            P("narrow", "wide"),
            P("narrow"),
            P("narrow"),
            P("narrow"),
            P("wide", "narrow"),
            P("narrow"),
            P("narrow", "wide"),
            P("narrow"),
        ),
        check_vma=False,
    )
```

time: 1940 us -> 729 us (0.38)
  matrix products: 382 us -> 0 us
  local copies, waits for them, and re-layouts: 391 us -> 71.9 us
  blocking collectives: 365 us -> 55.6 us
  waiting for transfers between devices: 619 us -> 317 us
  Pallas kernels: 0 us -> 246 us
  other arithmetic: 141 us -> 15.1 us
    dot_general x30 -> x0, matrix products: 382 us -> none  [the longest x6 88.2 us: matmul(): return jnp.dot(left_op, right_op, preferred_element_type=jnp.float32)]
    unnamed x2 -> x0, blocking collectives: 342 us -> none
    all_gather x2, waiting for transfers between devices: 422 us -> 93.9 us  [the longest x1 89.4 us: local(): wo = lax.all_gather(fc_out, 'narrow', axis=0)]
    pallas_call x0 -> x13, Pallas kernels: none -> 246 us  [the longest x6 61.5 us: weight_grad(): call(kernel, name, (width // tile,), [pl.BlockSpec((rows, tile), lambda i...]
    unnamed x167 -> x16, local copies, waits for them, and re-layouts: 139 us -> 43.8 us
    reshape x15 -> x2, local copies, waits for them, and re-layouts: 96.7 us -> 7.51 us  [unpad(): body = padded[:, :PATCHES].reshape(FRAMES * PATCHES, WIDTH)]
    reduce_sum x22 -> x1, other arithmetic: 74.1 us -> 0.97 us  [local(): grad_clips = unpad(dp, jnp.sum(df[:, CLASS], axis=0, keepdims=True))]
    concatenate x7 -> x1, local copies, waits for them, and re-layouts: 51.6 us -> 0.27 us  [local(): vectors = jnp.concatenate([vectors, gb_m[0].reshape(slices, WIDTH)], axis=0)]
  transfers between devices with their start and end apart: 16 -> 14, of which waited for: 7 -> 11; matrix products, arithmetic and copies ran while one was open for 20% -> 12% of each run, Pallas kernels for 0% -> 21%
where the time goes in v1:
time: 729 us; the launch traced here: 721 us
  waiting for transfers between devices  317 us (43%)
  Pallas kernels  246 us (34%)
  local copies, waits for them, and re-layouts  71.9 us (10%)
  blocking collectives  55.6 us (8%)
  other arithmetic  15.1 us (2%)
  between operations  14.5 us (2%)
    reduce_scatter x4, waiting for transfers between devices, scatter(): part = lax.psum_scatter(grad, 'wide', scatter_dimension=0, tiled=True)  117 us
    all_gather x1, waiting for transfers between devices, local(): wo = lax.all_gather(fc_out, 'narrow', axis=0)  89.4 us
    reduce_scatter x4, waiting for transfers between devices, scatter(): part = lax.psum_scatter(part, 'narrow', scatter_dimension=1, tiled=True)  63.7 us
    pallas_call x6, Pallas kernels, weight_grad(): call(kernel, name, (width // tile,), [pl.BlockSpec((rows, tile), lambda i...  61.5 us
    pallas_call x1, Pallas kernels, local(): call(mlp_kernel, 'mlp', steps, [frames(WIDTH), whole(FRAMES, 8, WIDTH), p...  45.2 us
    unnamed x16, local copies, waits for them, and re-layouts  43.8 us
    unnamed x18, waiting for transfers between devices  43.2 us
    pallas_call x1, Pallas kernels, local(): call(space_back_kernel, 'space_back', steps, [frames(WIDTH), pl.BlockSpec...  40.4 us
  transfers between devices with their start and end apart: 14, of which 11 were waited for; matrix products, arithmetic and copies ran while one was open for 12% of the time, Pallas kernels for 21%

profile of v1, /device:TPU:0, one launch (start us, length us, event | category | flops | bytes accessed | tf_op | source)
XLA Modules:
  0.0 720.8 jit_solution(14304466302448215820)
XLA Ops:
  8.0 0.7 all-gather.8.cloned.1.call-update
  8.7 0.7 stack.30
  10.1 0.7 stack.32
  10.8 0.7 stack.33
  11.5 0.7 stack.34
  12.1 0.7 stack.35
  15.6 1.3 convert_element_type.21.bias_ref
  16.9 1.3 convert_element_type.22.bias_ref
  18.1 0.7 reshape.98
  18.8 15.5 %all-gather.2 = f32[4,1,768]{2,1,0:T(1,128)} all-gather(f32[1,1,768]{2,1,0:T(1,128)S(1)} %reshape.98), channel_id=1, replica_groups=mesh['wide'=8,'narrow'=4] {'narrow'}, dimensions={0}, use_global_device_ids=true | all-gather | bytes 15360 | tf_op jit(solution)/shard_map/all_gather | solution.py:360
  34.3 14.4 %time_in.1 = (bf16[8,208,768]{2,1,0:T(8,128)(2,1)}, bf16[8,208,768]{2,1,0:T(8,128)(2,1)}, bf16[8,208,768]{2,1,0:T(8,128)(2,1)}, bf16[8,208,2304]{2,1,0:T(8,128)(2,1)}) custom-call(bf16[1569,768]{1,0:T(8,128)(2,1)} %bitcast.68, bf16[1569,768]{1,0:T(8,128)(2,1)} %bitcast.69, f32[9,768]{1,0:T(8,128)} %convert_element_type.20.vec_ref, ...), custom_call_target="tpu_custom_call" | custom-call | flops 5888802816 | bytes 25165824 | tf_op jit(solution)/shard_map/time_in/pallas_call | solution.py:376
  48.7 19.6 %time_attention.1 = (bf16[8,208,768]{2,1,0:T(8,128)(2,1)}, bf16[13,3,512,128]{3,2,1,0:T(8,128)(2,1)}) custom-call(bf16[8,208,2304]{2,1,0:T(8,128)(2,1)} %get-tuple-element.49.z_ref), custom_call_target="tpu_custom_call" | custom-call | flops 10000000000 | bytes 16777216 | tf_op jit(solution)/shard_map/time_attention/pallas_call | solution.py:382
  68.2 29.2 %space.1 = (f32[8,208,768]{2,1,0:T(8,128)}, bf16[8,208,768]{2,1,0:T(8,128)(2,1)}, bf16[8,208,2304]{2,1,0:T(8,128)(2,1)}, bf16[8,3,832,208]{3,2,1,0:T(8,128)(2,1)...) custom-call(bf16[8,208,768]{2,1,0:T(8,128)(2,1)} %get-tuple-element.48.p_ref, ...), custom_call_target="tpu_custom_call" | custom-call | flops 30000001024 | bytes 41943040 | tf_op jit(solution)/shard_map/space/pallas_call | solution.py:387
  97.5 4.4 all-gather.6.cloned.1.call-done
  101.9 89.4 %all-gather.8.cloned.1.call-done = bf16[3072,768]{1,0:T(8,128)(2,1)} async-done(((bf16[768,768]{1,0:T(8,128)(2,1)}), bf16[3072,768]{1,0:T(8,128)(2,1)}) %all-gather.8.cloned.1.call-update) | async-done | bytes 4718608 | tf_op jit(solution)/shard_map/all_gather | solution.py:359
  191.3 45.2 %mlp.1 = (bf16[8,208,768]{2,1,0:T(8,128)(2,1)}, bf16[8,208,768]{2,1,0:T(8,128)(2,1)}, bf16[8,208,3072]{2,1,0:T(8,128)(2,1)}, bf16[8,208,3072]{2,1,0:T(8,128)(2,1...) custom-call(f32[8,208,768]{2,1,0:T(8,128)} %get-tuple-element.51.x_ref, ...), custom_call_target="tpu_custom_call" | custom-call | flops 31406948352 | bytes 52428800 | tf_op jit(solution)/shard_map/mlp/pallas_call | solution.py:396
  236.6 40.4 %space_back.1 = (bf16[8,208,768]{2,1,0:T(8,128)(2,1)}, bf16[8,208,2304]{2,1,0:T(8,128)(2,1)}, f32[8,208,768]{2,1,0:T(8,128)}, bf16[8,208,768]{2,1,0:T(8,128)(2,1...) custom-call(f32[8,208,768]{2,1,0:T(8,128)} %get-tuple-element.55.dx_ref.dcls_ref, ...), custom_call_target="tpu_custom_call" | custom-call | flops 30000001024 | bytes 52428800 | tf_op jit(solution)/shard_map/space_back/pallas_call | solution.py:409
  277.0 5.5 grad_time_proj.1
  282.5 2.4 copy.50
  284.9 5.5 grad_space_proj.1
  290.4 2.4 copy.54
  292.9 21.1 %time_back.1.dz_ref = bf16[8,208,2304]{2,1,0:T(8,128)(2,1)} custom-call(bf16[8,208,2304]{2,1,0:T(8,128)(2,1)} %get-tuple-element.49.z_ref, bf16[13,3,512,128]{3,2,1,0:T(8,128)(2,1)} %get-tuple-element.60.a_ref, bf16[8,208,768]{2,1,0:T(8,128)(2,1)} %get-tuple-element.61.do_ref), custom_call_target="tpu_custom_call" | custom-call | flops 10000000000 | bytes 25165824 | tf_op jit(solution)/shard_map/time_back/pallas_call | solution.py:422
  314.0 10.7 %grad_time_qkv.1 = bf16[2304,768]{1,0:T(8,128)(2,1)} custom-call(bf16[1664,2304]{1,0:T(8,128)(2,1)} %bitcast.72, bf16[1664,768]{1,0:T(8,128)(2,1)} %bitcast.76), custom_call_target="tpu_custom_call" | custom-call | flops 5888802816 | bytes 13762560 | tf_op jit(solution)/shard_map/grad_time_qkv/pallas_call | solution.py:326
  324.8 10.6 %grad_space_qkv.1 = bf16[2304,768]{1,0:T(8,128)(2,1)} custom-call(bf16[1664,2304]{1,0:T(8,128)(2,1)} %bitcast.73, bf16[1664,768]{1,0:T(8,128)(2,1)} %bitcast.77), custom_call_target="tpu_custom_call" | custom-call | flops 5888802816 | bytes 13762560 | tf_op jit(solution)/shard_map/grad_space_qkv/pallas_call | solution.py:326
  335.5 14.6 %grad_fc_in.1 = bf16[768,3072]{1,0:T(8,128)(2,1)} custom-call(bf16[1664,768]{1,0:T(8,128)(2,1)} %bitcast.75, bf16[1664,3072]{1,0:T(8,128)(2,1)} %bitcast.71), custom_call_target="tpu_custom_call" | custom-call | flops 7851737088 | bytes 17498112 | tf_op jit(solution)/shard_map/grad_fc_in/pallas_call | solution.py:326
  350.1 14.6 %grad_fc_out.1 = bf16[768,3072]{1,0:T(8,128)(2,1)} custom-call(bf16[1664,768]{1,0:T(8,128)(2,1)} %bitcast.74, bf16[1664,3072]{1,0:T(8,128)(2,1)} %bitcast.70), custom_call_target="tpu_custom_call" | custom-call | flops 7851737088 | bytes 17498112 | tf_op jit(solution)/shard_map/grad_fc_out/pallas_call | solution.py:326
  364.8 1.7 copy.51
  366.6 1.7 copy.55
  368.4 44.0 %reduce-scatter.21.cloned.1.call-done = bf16[288,768]{1,0:T(8,128)(2,1)} async-done(((bf16[2304,768]{1,0:T(8,128)(2,1)}), bf16[288,768]{1,0:T(8,128)(2,1)}) %reduce-scatter.21.cloned.1.call-update) | async-done | bytes 442384 | tf_op jit(solution)/shard_map/reduce_scatter | solution.py:440
  412.5 2.1 copy.48
  414.6 49.3 %reduce-scatter.25.cloned.1.call-done = bf16[288,768]{1,0:T(8,128)(2,1)} async-done(((bf16[2304,768]{1,0:T(8,128)(2,1)}), bf16[288,768]{1,0:T(8,128)(2,1)}) %reduce-scatter.25.cloned.1.call-update) | async-done | bytes 442384 | tf_op jit(solution)/shard_map/reduce_scatter | solution.py:440
  463.9 2.1 copy.52
  466.0 0.7 slice.84
  466.8 0.7 slice.85
  467.5 0.7 slice.86
  468.3 1.9 slice.80
  470.1 2.4 reshape.82
  472.5 14.4 %time_out.1 = (f32[8,208,768]{2,1,0:T(8,128)}, f32[8,2304]{1,0:T(8,128)}) custom-call(bf16[8,208,2304]{2,1,0:T(8,128)(2,1)} %time_back.1.dz_ref, bf16[8,208,768]{2,1,0:T(8,128)(2,1)} %get-tuple-element.48.p_ref, f32[8,208,768]{2,1,0:T(8,128)} %get-tuple-element.59.df_ref, f32[9,768]{1,0:T(8,128)} %convert_element_type.20.vec_ref, bf16[768,2304]{1,0:T(8,128)(2,1)} %w_ref.7), custom_call_target="tpu_custom_call" | custom-call | flops 5888802816 | bytes 29360128 | tf_op jit(solution)/shard_map/time_out/pallas_call | solution.py:429
  486.8 5.0 slice.82
  491.8 5.2 reshape.83
  497.0 1.0 slice_reduce_fusion
  497.9 23.3 %reduce-scatter.29.cloned.1.call-done = bf16[96,3072]{1,0:T(8,128)(2,1)} async-done(((bf16[768,3072]{1,0:T(8,128)(2,1)}), bf16[96,3072]{1,0:T(8,128)(2,1)}) %reduce-scatter.29.cloned.1.call-update) | async-done | bytes 589840 | tf_op jit(solution)/shard_map/reduce_scatter | solution.py:440
  521.3 2.7 maximum_bitcast_fusion
  524.0 26.9 %copy.45 = f32[1,1569,768]{2,0,1:T(1,128)} copy(f32[1,1569,768]{2,1,0:T(8,128)S(1)} %maximum_bitcast_fusion) | data formatting | bytes 9639936
  551.0 0.7 slice.89
  551.7 0.9 slice_reduce_fusion.1
  552.7 0.8 fusion.2
  553.7 40.1 %psum.7 = f32[17,768]{1,0:T(8,128)S(1)} all-reduce(f32[17,768]{1,0:T(8,128)S(1)} %concatenate.12), channel_id=1, replica_groups=mesh['wide'=8,'narrow'=4] {'wide','narrow'}, use_global_device_ids=true, to_apply=%region_1.0 | all-reduce | flops 13056 | bytes 104448 | tf_op jit(solution)/shard_map/psum | solution.py:451
  595.8 0.7 slice_bitcast_fusion
  596.5 2.0 maximum_bitcast_fusion.1
  598.5 3.1 reduce-scatter.23.cloned.1.call-done
  601.6 1.4 convert_bitcast_fusion.4
  603.1 18.9 %reduce-scatter.27.cloned.1.call-done = bf16[96,192]{0,1:T(8,128)(2,1)} async-done(((bf16[96,768]{0,1:T(8,128)(2,1)}), bf16[96,192]{0,1:T(8,128)(2,1)}) %reduce-scatter.27.cloned.1.call-update) | async-done | bytes 36880 | tf_op jit(solution)/shard_map/reduce_scatter | solution.py:441
  622.0 1.4 convert_bitcast_fusion.3
  623.5 21.0 %reduce-scatter.37.cloned.1.call-done = bf16[192,288]{1,0:T(8,128)(2,1)} async-done(((bf16[768,288]{1,0:T(8,128)(2,1)}), bf16[192,288]{1,0:T(8,128)(2,1)}) %reduce-scatter.37.cloned.1.call-update) | async-done | bytes 110608
  644.5 1.0 copy.49
  645.5 0.9 copy.46
  646.4 20.6 %reduce-scatter.41.cloned.1.call-done = bf16[192,288]{1,0:T(8,128)(2,1)} async-done(((bf16[768,288]{1,0:T(8,128)(2,1)}), bf16[192,288]{1,0:T(8,128)(2,1)}) %reduce-scatter.41.cloned.1.call-update) | async-done | bytes 110608
  667.0 1.0 copy.53
  668.0 0.9 copy.47
  668.9 20.7 %reduce-scatter.31.cloned.1.call-done = bf16[96,768]{1,0:T(8,128)(2,1)} async-done(((bf16[96,3072]{1,0:T(8,128)(2,1)}), bf16[96,768]{1,0:T(8,128)(2,1)}) %reduce-scatter.31.cloned.1.call-update) | async-done | bytes 147472 | tf_op jit(solution)/shard_map/reduce_scatter | solution.py:441
  689.6 1.6 convert_element_type.24
  691.3 20.9 %reduce-scatter.35.cloned.1.call-done = bf16[96,768]{1,0:T(8,128)(2,1)} async-done(((bf16[96,3072]{1,0:T(8,128)(2,1)}), bf16[96,768]{1,0:T(8,128)(2,1)}) %reduce-scatter.35.cloned.1.call-update) | async-done | bytes 147472 | tf_op jit(solution)/shard_map/reduce_scatter | solution.py:441
  712.1 1.6 convert_bitcast_fusion
  (49 shorter events, 7.2 us)
Async XLA Ops:
  7.2 94.7 %all-gather.6.cloned.1.call-start = ((), (), s32[]{:S(2)}) async-start(), calls=%async_computation.20 | async-start | bytes 5898240 | tf_op jit(solution)/shard_map/all_gather | solution.py:358
  7.9 183.4 %all-gather.8.cloned.1.call-start = ((), (), s32[]{:S(2)}) async-start(), calls=%async_computation.21 | async-start | bytes 5898240 | tf_op jit(solution)/shard_map/all_gather | solution.py:359
  8.7 356.1 %reduce-scatter.39.cloned.1.call-start = ((), (), s32[]{:S(2)}) async-start(), calls=%async_computation.23 | async-start | bytes 1327104
  284.9 81.7 %reduce-scatter.43.cloned.1.call-start = ((), (), s32[]{:S(2)}) async-start(), calls=%async_computation.25 | async-start | bytes 1327104
  292.9 119.6 %reduce-scatter.21.cloned.1.call-start = ((), (), s32[]{:S(2)}) async-start(), calls=%async_computation.12 | async-start | bytes 3981312 | tf_op jit(solution)/shard_map/reduce_scatter | solution.py:440
  324.7 139.2 %reduce-scatter.25.cloned.1.call-start = ((), (), s32[]{:S(2)}) async-start(), calls=%async_computation.14 | async-start | bytes 3981312 | tf_op jit(solution)/shard_map/reduce_scatter | solution.py:440
  335.4 185.8 %reduce-scatter.29.cloned.1.call-start = ((), (), s32[]{:S(2)}) async-start(), calls=%async_computation.16 | async-start | bytes 5308416 | tf_op jit(solution)/shard_map/reduce_scatter | solution.py:440
  350.0 246.4 %reduce-scatter.33.cloned.1.call-start = ((), (), s32[]{:S(2)}) async-start(), calls=%async_computation.18 | async-start | bytes 5308416 | tf_op jit(solution)/shard_map/reduce_scatter | solution.py:440
  364.7 236.9 %reduce-scatter.23.cloned.1.call-start = ((), (), s32[]{:S(2)}) async-start(), calls=%async_computation.13 | async-start | bytes 245760 | tf_op jit(solution)/shard_map/reduce_scatter | solution.py:441
  366.5 255.5 %reduce-scatter.27.cloned.1.call-start = ((), (), s32[]{:S(2)}) async-start(), calls=%async_computation.15 | async-start | bytes 245760 | tf_op jit(solution)/shard_map/reduce_scatter | solution.py:441
  368.4 276.1 %reduce-scatter.37.cloned.1.call-start = ((), (), s32[]{:S(2)}) async-start(), calls=%async_computation.22 | async-start | bytes 737280
  414.6 252.4 %reduce-scatter.41.cloned.1.call-start = ((), (), s32[]{:S(2)}) async-start(), calls=%async_computation.24 | async-start | bytes 737280
  466.0 223.7 %reduce-scatter.31.cloned.1.call-start = ((), (), s32[]{:S(2)}) async-start(), calls=%async_computation.17 | async-start | bytes 737280 | tf_op jit(solution)/shard_map/reduce_scatter | solution.py:441
  521.3 190.9 %reduce-scatter.35.cloned.1.call-start = ((), (), s32[]{:S(2)}) async-start(), calls=%async_computation.19 | async-start | bytes 737280 | tf_op jit(solution)/shard_map/reduce_scatter | solution.py:441
  524.0 27.0 %copy-start.1 = (f32[8,768]{1,0:T(8,128)S(1)}, f32[8,768]{1,0:T(8,128)}, u32[]{:S(2)}) copy-start(f32[8,768]{1,0:T(8,128)} %get-tuple-element.63) | copy-start | bytes 73732
  524.0 72.5 %copy-start = (bf16[1568,768]{1,0:T(8,128)(2,1)S(1)}, bf16[1568,768]{1,0:T(8,128)(2,1)}, u32[]{:S(2)}) copy-start(bf16[1568,768]{1,0:T(8,128)(2,1)} %reshape.82) | copy-start | bytes 7225348
Sparse Core Ops, SparseCore 0:
  9.6 92.2 all-gather.5
  103.5 87.8 all-gather.7
  285.0 35.1 reduce-scatter.38
  323.6 36.7 reduce-scatter.42
  364.3 48.0 reduce-scatter.20
  415.8 48.0 reduce-scatter.24
  467.3 53.8 reduce-scatter.28
  525.1 54.3 reduce-scatter.32
  582.3 19.3 reduce-scatter.22
  604.4 17.5 reduce-scatter.26
  624.3 20.1 reduce-scatter.36
  646.6 20.3 reduce-scatter.40
  669.3 20.3 reduce-scatter.30
  691.8 20.3 reduce-scatter.34

commit v2 on v1

--- a/solution.py
+++ b/solution.py
@@ -24,7 +24,8 @@
 F32 = jnp.float32
 BF = jnp.bfloat16
 NEG = -1e30
-VMEM_LIMIT = 60 * 2**20
+VMEM_LIMIT = 62 * 2**20
+CHUNKS = 8
 
 
 def dg(a, b, ca, cb):
@@ -43,7 +44,8 @@
     return dg(a, b, 0, 0)
 
 
-def call(kernel, name, grid, ins, outs, scratch=(), flops=0, nbytes=0):
+def call(kernel, name, grid, ins, outs, scratch=(), flops=0, nbytes=0, remote=None):
+    extra = {} if remote is None else dict(collective_id=remote, has_side_effects=True)
     return pl.pallas_call(
         kernel,
         name=name,
@@ -52,13 +54,13 @@
         out_specs=[s for s, _ in outs],
         out_shape=[t for _, t in outs],
         scratch_shapes=list(scratch),
-        compiler_params=pltpu.CompilerParams(vmem_limit_bytes=VMEM_LIMIT),
+        compiler_params=pltpu.CompilerParams(vmem_limit_bytes=VMEM_LIMIT, **extra),
         cost_estimate=pl.CostEstimate(flops=flops, bytes_accessed=nbytes, transcendentals=0),
     )
 
 
 def whole(*shape):
-    return pl.BlockSpec(shape, lambda *i: (0,) * len(shape))
+    return pl.BlockSpec(shape, lambda *i: (0,) * len(shape), pipeline_mode=pl.Buffered(1))
 
 
 def frames(width):
@@ -109,6 +111,143 @@
 def group_cols(g, which):
     start = which * WIDTH + g * GW
     return slice(start, start + GW)
+
+
+def hosted():
+    return lax.axis_size("wide") == CHUNKS
+
+
+def own_index():
+    return lax.axis_index("wide") if hosted() else jnp.int32(0)
+
+
+def peer(axis, bit):
+    return {axis: jnp.bitwise_xor(lax.axis_index(axis), bit)}
+
+
+PEERS = (("wide", 1), ("wide", 2), ("wide", 4), ("narrow", 1), ("narrow", 2), ("narrow", 3))
+
+
+def greet():
+    barrier = pltpu.get_barrier_semaphore()
+    for axis, bit in PEERS:
+        pl.semaphore_signal(barrier, inc=1, device_id=peer(axis, bit), device_id_type=pl.DeviceIdType.MESH)
+    pl.semaphore_wait(barrier, len(PEERS))
+
+
+def send(src, dst, sems, k, axis, bit):
+    return pltpu.make_async_remote_copy(
+        src_ref=src, dst_ref=dst, send_sem=sems.at[0, k], recv_sem=sems.at[1, k],
+        device_id=peer(axis, bit), device_id_type=pl.DeviceIdType.MESH,
+    )
+
+
+def start(copies):
+    for c in copies:
+        c.start()
+
+
+def wait(copies):
+    for c in copies:
+        c.wait()
+
+
+def plus(a, b):
+    return (a.astype(F32) + b.astype(F32)).astype(BF)
+
+
+class PlaneSum:
+    SEMS = 7
+
+    @staticmethod
+    def scratch(rows):
+        half = rows // 2
+        return [
+            pltpu.VMEM((4, 2, half, WIDTH), BF),
+            pltpu.VMEM((4, 2, half, WIDTH), BF),
+            pltpu.VMEM((2, 2, half, WIDTH), BF),
+            pltpu.SemaphoreType.DMA((2, PlaneSum.SEMS)),
+            pltpu.SemaphoreType.DMA,
+        ]
+
+    def __init__(self, own, oth, recv, got, near, sems, own_sem):
+        self.own, self.oth, self.recv, self.got, self.near, self.sems = own, oth, recv, got, near, sems
+        self.own_sem = own_sem
+
+    def load(self):
+        return [pltpu.make_async_copy(self.own, self.got, self.own_sem)]
+
+    def chip(self):
+        return [send(self.oth, self.recv, self.sems, 0, "wide", 1)]
+
+    def first(self):
+        got, near, sems = self.got, self.near, self.sems
+        return [
+            send(got.at[1, 0], near.at[0, 0], sems, 1, "wide", 2),
+            send(got.at[3, 0], near.at[0, 1], sems, 2, "wide", 2),
+            send(got.at[2, 1], near.at[1, 0], sems, 3, "wide", 4),
+            send(got.at[3, 1], near.at[1, 1], sems, 4, "wide", 4),
+        ]
+
+    def second(self):
+        got, recv, sems = self.got, self.recv, self.sems
+        return [
+            send(got.at[2, 0], recv.at[0, 0], sems, 5, "wide", 4),
+            send(got.at[1, 1], recv.at[0, 1], sems, 6, "wide", 2),
+        ]
+
+    def stage0(self):
+        start(self.load())
+        start(self.chip())
+
+    def stage1(self):
+        wait(self.load())
+        wait(self.chip())
+
+        @pl.loop(0, 4)
+        def _(q):
+            for h in range(2):
+                self.got[q, h] = plus(self.got[q, h], self.recv[q, h])
+
+        start(self.first())
+
+    def stage2(self):
+        wait(self.first())
+        for q, h, way, i in ((0, 0, 0, 0), (2, 0, 0, 1), (0, 1, 1, 0), (1, 1, 1, 1)):
+            self.got[q, h] = plus(self.got[q, h], self.near[way, i])
+        start(self.second())
+
+    def stage3(self):
+        wait(self.second())
+        for h in range(2):
+            self.got[0, h] = plus(self.got[0, h], self.recv[0, h])
+
+
+def halves(piece):
+    return piece.reshape(4, 2, -1, WIDTH)
+
+
+class LineSum:
+    def __init__(self, parts, recv, sems):
+        self.parts, self.recv, self.sems = parts, recv, sems
+
+    @staticmethod
+    def scratch(rows, width):
+        return [pltpu.VMEM((3, rows, width), BF), pltpu.SemaphoreType.DMA((2, 3))]
+
+    def copies(self):
+        line = lax.axis_index("narrow")
+        return [
+            send(self.parts.at[jnp.bitwise_xor(line, b)], self.recv.at[b - 1], self.sems, b - 1, "narrow", b)
+            for b in (1, 2, 3)
+        ]
+
+    def result(self):
+        wait(self.copies())
+        total = self.parts[lax.axis_index("narrow")].astype(F32)
+        for b in range(3):
+            total = total + self.recv[b].astype(F32)
+        return total
 
 
 def shifted(src_ref, frame, first_row, class_on):
@@ -199,46 +338,176 @@
         cls_ref[j] = y[at : at + 8]
 
 
-def mlp_kernel(
-    x_ref, cls_ref, p_ref, g_ref, vec_ref, b_ref, wi_ref, wo_ref,
-    out_ref, h_ref, act_ref, dpre_ref, dx_ref, gv_ref, gb_ref,
-):
-    slices = wi_ref.shape[0]
+def mlp_kernel(first_call, *refs):
+    if first_call:
+        (x_ref, cls_ref, p_ref, g_ref, vec_ref, win_ref, wout_ref, bin_ref, wa_ref, wb_ref,
+         h_ref, acc_ref, dh_ref, own_ref, oth_ref, gv_ref, gb_ref,
+         w_buf, bias_buf, h_buf, g_buf, act_buf, dpre_buf, t_buf, sem) = refs
+    else:
+        (x_ref, cls_ref, p_ref, g_ref, vec_ref, h_ref, acc_ref, dh_ref, wa_ref, wb_ref, wc_ref, wd_ref,
+         *refs) = refs
+        refs = list(refs)
+        near_refs = [refs.pop(0), refs.pop(0)] if hosted() else None
+        out_ref, dx_ref, own_ref, oth_ref, gv_ref, gb_ref = refs[:6]
+        refs = refs[6:]
+        near_out = refs.pop(0) if hosted() else None
+        w_buf, bias_buf, h_buf, g_buf, act_buf, dpre_buf, t_buf, out_buf, sem = refs[:9]
+        refs = refs[9:]
     step = pl.program_id(0)
+    me = own_index()
+    core = lax.rem(lax.axis_index("wide"), 2)
+    line = lax.axis_index("narrow")
+    swap = jnp.int32(0) if first_call else ((line == 1) | (line == 2)).astype(jnp.int32)
+    row_steps = FRAMES // FPS
+    if not first_call and hosted():
+        plane = PlaneSum(*near_refs, *refs[:5])
+        rz, zsem = refs[5:]
+
+        def line_copies():
+            return [send(plane.got.at[0, m, pl.ds(96, 96)], rz.at[m], zsem, m, "narrow", 1) for m in range(2)]
+
+        def near_total():
+            wait(line_copies())
+            for m in range(2):
+                near_out[m] = plane.got[0, m, 0:96].astype(F32) + rz[m].astype(F32)
+
+        def line_stage():
+            plane.stage3()
+            start(line_copies())
+
+        plan = {1: plane.stage1, 3: plane.stage2, 4: line_stage}
+
+        @pl.when(step == 0)
+        def _():
+            greet()
+            plane.stage0()
+
+        for k, action in plan.items():
+            pl.when(step == k)(action)
 
     @pl.when(step == 0)
     def _():
         gv_ref[...] = jnp.zeros_like(gv_ref)
         gb_ref[...] = jnp.zeros_like(gb_ref)
 
-    mean_cls = jnp.mean(cls_ref[:, CLASS % 8, :], axis=0, keepdims=True)
-    first = p_ref[0, CLASS % TILE : CLASS % TILE + 1, :].astype(F32) + mean_cls
-    row = lax.broadcasted_iota(jnp.int32, (STEP, WIDTH), 0) % ROWS
-    x = jnp.where(row == CLASS, first, x_ref[...].reshape(STEP, WIDTH))
-    g = g_ref[...].reshape(STEP, WIDTH)
-    xhat, scale = normed(x)
-    h = (xhat * vec_ref[6:7] + vec_ref[7:8]).astype(BF)
-    h_ref[...] = h.reshape(FPS, ROWS, WIDTH)
-    out = x + vec_ref[8:9]
-    dh = jnp.zeros((STEP, WIDTH), F32)
-    for s in range(slices):
-        cols = slice(s * WIDTH, (s + 1) * WIDTH)
-        pre = nn(h, wi_ref[s]) + b_ref[:, cols]
-        cdf = 0.5 + 0.5 * lax.erf(pre * (0.5**0.5))
-        act = (pre * cdf).astype(BF)
-        slope = cdf + pre * (jnp.exp(-0.5 * pre * pre) * 0.3989422804014327)
-        act_ref[:, :, cols] = act.reshape(FPS, ROWS, WIDTH)
-        dpre = (nt(g, wo_ref[s]) * slope).astype(BF)
-        dpre_ref[:, :, cols] = dpre.reshape(FPS, ROWS, WIDTH)
-        gb_ref[0:1, cols] += colsum(dpre)
-        out = out + nn(act, wo_ref[s])
-        dh = dh + nt(dpre, wi_ref[s])
-    out_ref[...] = out.astype(BF).reshape(FPS, ROWS, WIDTH)
-    gf = g.astype(F32)
-    dx_ref[...] = (gf + norm_back(dh, xhat, scale, vec_ref[6:7])).reshape(FPS, ROWS, WIDTH)
-    gv_ref[0:1] += colsum(dh * xhat)
-    gv_ref[1:2] += colsum(dh)
-    gv_ref[2:3] += colsum(gf)
+        def fetch(src, dst, k):
+            return pltpu.make_async_copy(src, dst, sem.at[k])
+
+        pairs = [(wa_ref, wb_ref)] if first_call else [(wa_ref, wb_ref), (wc_ref, wd_ref)]
+        base = 1 if first_call else 0
+        for c in range(2):
+
+            @pl.when(core == c)
+            def _():
+                todo = []
+                for i, (mine, sib) in enumerate(pairs):
+                    slot = base + i
+                    into = (mine, sib) if c == 0 else (sib, mine)
+                    for m in range(2):
+                        todo.append(fetch(into[m].at[0:WIDTH], w_buf.at[m, slot], len(todo)))
+                    todo.append(fetch(mine.at[WIDTH : WIDTH + TILE], bias_buf.at[slot], len(todo)))
+                for t in todo:
+                    t.start()
+                for t in todo:
+                    t.wait()
+
+    if first_call:
+
+        def weight(m, slot):
+            return (win_ref, wout_ref)[m][...] if slot == 0 else w_buf[m, slot]
+
+        def bias(slot):
+            return bin_ref[...] if slot == 0 else bias_buf[slot, 0:1].astype(F32)
+    else:
+
+        def weight(m, slot):
+            return w_buf[m, slot]
+
+        def bias(slot):
+            return bias_buf[slot, 0:1].astype(F32)
+
+    @pl.when(step < row_steps)
+    def _():
+        at = pl.ds(pl.multiple_of(step * STEP, STEP), STEP)
+        x = x_ref[...].reshape(STEP, WIDTH)
+        mean_cls = jnp.mean(cls_ref[:, CLASS % 8, :], axis=0, keepdims=True)
+        first = p_ref[0, CLASS % TILE : CLASS % TILE + 1, :].astype(F32) + mean_cls
+        row = lax.broadcasted_iota(jnp.int32, (STEP, WIDTH), 0) % ROWS
+        x = jnp.where(row == CLASS, first, x)
+        xhat, scale = normed(x)
+        g = g_ref[...].reshape(STEP, WIDTH)
+        if first_call:
+            h = (xhat * vec_ref[6:7] + vec_ref[7:8]).astype(BF)
+            h_ref[...] = h.reshape(FPS, ROWS, WIDTH)
+            acc = x + vec_ref[8:9]
+            dh = None
+        else:
+            h = h_ref[...].reshape(STEP, WIDTH)
+            acc = acc_ref[...].reshape(STEP, WIDTH)
+            dh = dh_ref[...].reshape(STEP, WIDTH)
+        h_buf[at, :] = h
+        g_buf[at, :] = g
+        for s in range(2):
+            cols = slice(s * WIDTH, (s + 1) * WIDTH)
+            pre = nn(h, weight(0, s)) + bias(s)
+            cdf = 0.5 + 0.5 * lax.erf(pre * (0.5**0.5))
+            act = (pre * cdf).astype(BF)
+            slope = cdf + pre * (jnp.exp(-0.5 * pre * pre) * 0.3989422804014327)
+            act_buf[at, cols] = act
+            dpre = (nt(g, weight(1, s)) * slope).astype(BF)
+            dpre_buf[at, cols] = dpre
+            gb_ref[s : s + 1, :] += colsum(dpre)
+            acc = acc + nn(act, weight(1, s))
+            back = nt(dpre, weight(0, s))
+            dh = back if dh is None else dh + back
+        if first_call:
+            acc_ref[...] = acc.reshape(FPS, ROWS, WIDTH)
+            dh_ref[...] = dh.reshape(FPS, ROWS, WIDTH)
+        else:
+            for k in range(row_steps):
+
+                @pl.when(step == k)
+                def _():
+                    if k == 0:
+                        out_buf[0:1, :] = acc[CLASS : CLASS + 1]
+                    for j in range(FPS):
+                        start = 1 + (k * FPS + j) * PATCHES
+                        out_buf[start : start + PATCHES, :] = acc[j * ROWS : j * ROWS + PATCHES]
+
+            gf = g.astype(F32)
+            dx_ref[...] = (gf + norm_back(dh, xhat, scale, vec_ref[6:7])).reshape(FPS, ROWS, WIDTH)
+            gv_ref[0:1] += colsum(dh * xhat)
+            gv_ref[1:2] += colsum(dh)
+            gv_ref[2:3] += colsum(gf)
+
+    def matrix(unit, left_ref, right_ref):
+        t_buf[...] = left_ref[...].T
+        for s in range(2):
+            got = nn(t_buf[...], right_ref[:, s * WIDTH : (s + 1) * WIDTH]).astype(BF)
+            for w in range(CHUNKS):
+                put_chunk(own_ref, oth_ref, me, w, 2 * unit + jnp.bitwise_xor(s, swap), got[w * 96 : (w + 1) * 96])
+
+    @pl.when(step == row_steps)
+    def _():
+        matrix(0, h_buf, dpre_buf)
+        if not first_call:
+            out_ref[0] = out_buf[...].astype(BF)
+
+    @pl.when(step == row_steps + 1)
+    def _():
+        matrix(1, g_buf, act_buf)
+        if not first_call and hosted():
+            near_total()
+
+
+def put_chunk(own_ref, oth_ref, me, w, unit, value):
+    rel = jnp.bitwise_xor(me, w)
+    place = rel // 2
+    for c, ref in enumerate((own_ref, oth_ref)):
+
+        @pl.when(rel % 2 == c)
+        def _():
+            ref[place, unit] = value
 
 
 def space_back_kernel(
@@ -305,6 +574,7 @@
     @pl.when(step == 0)
     def _():
         gv_ref[...] = jnp.zeros_like(gv_ref)
+        dp_ref[0, 0:1, :] = jnp.zeros((1, WIDTH), F32)
 
     dz = dz_ref[...].reshape(STEP, 3 * WIDTH)
     gv_ref[0:1, :] += colsum(dz)
@@ -312,31 +582,117 @@
     xhat, scale = normed(p_ref[...].reshape(STEP, WIDTH).astype(F32))
     gv_ref[1:2, :WIDTH] += colsum(dh * xhat)
     gv_ref[2:3, :WIDTH] += colsum(dh)
-    dp = df_ref[...].reshape(STEP, WIDTH) + norm_back(dh, xhat, scale, vec_ref[0:1])
-    dp_ref[...] = dp.reshape(FPS, ROWS, WIDTH)
-
-
-def weight_grad(a, b, name, tile):
-    rows, width = a.shape
-    out_width = b.shape[1]
-
-    def kernel(a_ref, b_ref, o_ref):
-        o_ref[...] = tn(a_ref[...], b_ref[...]).astype(BF)
-
+    df = df_ref[...].reshape(STEP, WIDTH)
+    dp = df + norm_back(dh, xhat, scale, vec_ref[0:1])
+    for j in range(FPS):
+        dp_ref[0, 0:1, :] += df[j * ROWS + CLASS : j * ROWS + CLASS + 1]
+    for k in range(FRAMES // FPS):
+
+        @pl.when(step == k)
+        def _():
+            for j in range(FPS):
+                start = 1 + (k * FPS + j) * PATCHES
+                dp_ref[0, start : start + PATCHES, :] = dp[j * ROWS : j * ROWS + PATCHES]
+
+
+def pair_grad_kernel(dz_ref, h_ref, dy_ref, o_ref, own_ref, oth_ref):
+    step = pl.program_id(0)
+    me = lax.axis_index("wide") if lax.axis_size("wide") == CHUNKS else jnp.int32(0)
+    half = CHUNKS // 2
+
+    @pl.when(step < 2)
+    def _():
+        got = tn(dz_ref[...], h_ref[...]).astype(BF)
+        for i in range(half):
+            w = step * half + i
+            put_rows(own_ref, oth_ref, me, w, 0, got[i * 288 : (i + 1) * 288])
+
+    @pl.when(step == 2)
+    def _():
+        got = tn(dy_ref[...], o_ref[...]).astype(BF)
+        for w in range(CHUNKS):
+            put_rows(own_ref, oth_ref, me, w, 288, got[w * 96 : (w + 1) * 96])
+
+
+def put_rows(own_ref, oth_ref, me, w, start, value):
+    rel = jnp.bitwise_xor(me, w)
+    place = rel // 2
+    for c, ref in enumerate((own_ref, oth_ref)):
+
+        @pl.when(rel % 2 == c)
+        def _():
+            ref[place, start : start + value.shape[0], :] = value
+
+
+PIECE = (CHUNKS // 2, 384, WIDTH)
+
+
+def pair_grad(dz, h, dy, o, name):
+    rows = FRAMES * ROWS
     return call(
-        kernel,
-        name,
-        (width // tile,),
-        [pl.BlockSpec((rows, tile), lambda i: (0, i)), whole(rows, out_width)],
-        [(pl.BlockSpec((tile, out_width), lambda i: (i, 0)), jax.ShapeDtypeStruct((width, out_width), BF))],
-        flops=2 * rows * width * out_width,
-        nbytes=2 * (rows * width + rows * out_width + width * out_width),
-    )(a, b)[0]
-
-
-def unpad(padded, first):
-    body = padded[:, :PATCHES].reshape(FRAMES * PATCHES, WIDTH)
-    return jnp.concatenate([first, body], axis=0)[None]
+        pair_grad_kernel, name, (3,),
+        [pl.BlockSpec((rows, 3 * WIDTH // 2), lambda i: (0, jnp.minimum(i, 1))),
+         whole(rows, WIDTH), whole(rows, WIDTH), whole(rows, WIDTH)],
+        [(whole(*PIECE), jax.ShapeDtypeStruct(PIECE, BF))] * 2,
+    )(dz.reshape(rows, 3 * WIDTH), h.reshape(rows, WIDTH), dy.reshape(rows, WIDTH), o.reshape(rows, WIDTH))
+
+
+def flip(value, axis, bit):
+    return lax.ppermute(value, axis, [(i, i ^ bit) for i in range(lax.axis_size(axis))])
+
+
+def hop(value, pairs):
+    return lax.ppermute(value, "narrow", pairs)
+
+
+def add(a, b):
+    return (a.astype(F32) + b.astype(F32)).astype(BF)
+
+
+def plane_sum(own, oth):
+    got = add(own, flip(oth, "wide", 1))
+    half = 192
+    rx = flip(jnp.stack([got[1, :half], got[3, :half]]), "wide", 2)
+    ry = flip(jnp.stack([got[2, half:], got[3, half:]]), "wide", 4)
+    na, ya = add(got[0, :half], rx[0]), add(got[2, :half], rx[1])
+    nb, xb = add(got[0, half:], ry[0]), add(got[1, half:], ry[1])
+    ra = flip(ya, "wide", 4)
+    rb = flip(xb, "wide", 2)
+    return jnp.concatenate([add(na, ra), add(nb, rb)])
+
+
+def unit_sum(own, oth):
+    if lax.axis_size("wide") == CHUNKS:
+        return plane_sum(own.reshape(PIECE), oth.reshape(PIECE)).reshape(2, 2, 96, WIDTH)
+    both = jnp.stack([own, oth], axis=1).reshape(CHUNKS, 4, 96, WIDTH)
+    both = both.transpose(1, 0, 2, 3).reshape(4, WIDTH, WIDTH)
+    both = lax.psum_scatter(both, "wide", scatter_dimension=1, tiled=True)
+    return both.reshape(2, 2, -1, WIDTH)
+
+
+def pair_sum(own, oth, me):
+    if lax.axis_size("wide") == CHUNKS:
+        rows = plane_sum(own, oth)
+        cut = 288
+    else:
+        both = jnp.stack([own, oth], axis=1).reshape(CHUNKS, 384, WIDTH)
+        first = both[:, :288].reshape(3 * WIDTH, WIDTH)
+        second = both[:, 288:].reshape(WIDTH, WIDTH)
+        first = lax.psum_scatter(first, "wide", scatter_dimension=0, tiled=True)
+        second = lax.psum_scatter(second, "wide", scatter_dimension=0, tiled=True)
+        rows = jnp.concatenate([first, second])
+        cut = first.shape[0]
+    parts = rows.T.reshape(lax.axis_size("narrow"), -1, rows.shape[0])
+    total = line_sum(parts, me)
+    return total[:, :cut], total[:, cut:]
+
+
+def line_sum(parts, me):
+    total = lax.dynamic_index_in_dim(parts, me, 0, False).astype(F32)
+    for bit in (1, 2, 3):
+        other = lax.dynamic_index_in_dim(parts, jnp.bitwise_xor(me, bit), 0, False)
+        total = total + flip(other, "narrow", bit).astype(F32)
+    return total
 
 
 def local(
@@ -345,7 +701,6 @@
     mlp_gain, mlp_shift, fc_in, in_bias, fc_out, out_bias, cotangent,
 ):
     slices = lax.axis_size("narrow")
-    hidden = slices * WIDTH
     tokens = video_clips.shape[1]
     clip = video_clips[0]
     cot = cotangent[0]
@@ -355,9 +710,22 @@
     nvec = vec.shape[0]
     t_bias = time_bias.astype(F32)
     s_bias = space_bias.astype(F32)
-    wi = lax.all_gather(fc_in, "narrow", axis=0)
-    wo = lax.all_gather(fc_out, "narrow", axis=0)
-    b_in = lax.all_gather(in_bias.astype(F32), "narrow", axis=0, tiled=True)[None]
+    me_n = lax.axis_index("narrow")
+    me_w = lax.axis_index("wide")
+    mine = jnp.where(me_w % 2 == 0, fc_in, fc_out)
+    bias_rows = jnp.broadcast_to(in_bias[None], (TILE, WIDTH))
+    mine = jnp.concatenate([mine, bias_rows], axis=0)
+    near = flip(mine, "narrow", 1)
+    mid1 = hop(mine, [(1, 2), (2, 1)])
+    near_s = flip(near, "wide", 1)
+    end1 = hop(mid1, [(1, 0), (2, 3)])
+    mid2 = hop(near, [(1, 2), (2, 1)])
+    end2 = hop(mid2, [(1, 0), (2, 3)])
+    inner = (me_n == 1) | (me_n == 2)
+    far1 = jnp.where(inner, mid1, end1)
+    far1_s = flip(far1, "wide", 1)
+    far2 = jnp.where(inner, mid2, end2)
+    far2_s = flip(far2, "wide", 1)
 
     chunks = ROWS // TILE
     a_time = (pl.BlockSpec((1, GROUPS, GROUP * FRAMES * TILE, FRAMES * TILE), lambda i: (i, 0, 0, 0)),
@@ -393,19 +761,47 @@
          (pl.BlockSpec((FPS, 8, WIDTH), lambda i: (i, 0, 0)), jax.ShapeDtypeStruct((FRAMES, 8, WIDTH), F32))],
         flops=3 * 10**10, nbytes=40 * 2**20,
     )(p, ot, vec, s_bias, time_proj, space_qkv, space_proj)
-    out, hm, act, dpre, dxs, gv_m, gb_m = call(
-        mlp_kernel, "mlp", steps,
-        [frames(WIDTH), whole(FRAMES, 8, WIDTH),
-         pl.BlockSpec((1, TILE, WIDTH), lambda i: (0, CLASS // TILE, 0)), frames(WIDTH),
-         whole(nvec, WIDTH), whole(1, hidden), whole(slices, WIDTH, WIDTH), whole(slices, WIDTH, WIDTH)],
-        [frames_out(WIDTH, BF), frames_out(WIDTH, BF), frames_out(hidden, BF), frames_out(hidden, BF),
-         frames_out(WIDTH, F32),
-         (whole(8, WIDTH), jax.ShapeDtypeStruct((8, WIDTH), F32)),
-         (whole(8, hidden), jax.ShapeDtypeStruct((8, hidden), F32))],
-        flops=8 * rows * WIDTH * hidden, nbytes=50 * 2**20,
-    )(xs, ycls, p, g, vec, b_in, wi, wo)
-    g_fc_in = weight_grad(hm.reshape(rows, WIDTH), dpre.reshape(rows, hidden), "grad_fc_in", 256)
-    g_fc_out = weight_grad(g.reshape(rows, WIDTH), act.reshape(rows, hidden), "grad_fc_out", 256)
+    any_ref = pl.BlockSpec(memory_space=pl.ANY)
+    last = FRAMES // FPS - 1
+    row_in = pl.BlockSpec((FPS, ROWS, WIDTH), lambda i: (jnp.minimum(i, last), 0, 0))
+
+    def row_out(dtype):
+        return row_in, jax.ShapeDtypeStruct((FRAMES, ROWS, WIDTH), dtype)
+
+    unit_shape = (CHUNKS // 2, 4, 96, WIDTH)
+    units = [(whole(*unit_shape), jax.ShapeDtypeStruct(unit_shape, BF))] * 2
+    vec_out = [(whole(8, WIDTH), jax.ShapeDtypeStruct((8, WIDTH), F32))] * 2
+    bufs = [
+        pltpu.VMEM((2, 2, WIDTH, WIDTH), BF), pltpu.VMEM((2, TILE, WIDTH), BF),
+        pltpu.VMEM((rows, WIDTH), BF), pltpu.VMEM((rows, WIDTH), BF),
+        pltpu.VMEM((rows, 2 * WIDTH), BF), pltpu.VMEM((rows, 2 * WIDTH), BF), pltpu.VMEM((WIDTH, rows), BF),
+    ]
+    hm, acc, dh, a_own, a_oth, _, gb_a = call(
+        partial(mlp_kernel, True), "mlp_near", (last + 3,),
+        [row_in, whole(FRAMES, 8, WIDTH),
+         pl.BlockSpec((1, TILE, WIDTH), lambda i: (0, CLASS // TILE, 0)), row_in,
+         whole(nvec, WIDTH), whole(WIDTH, WIDTH), whole(WIDTH, WIDTH), whole(1, WIDTH), any_ref, any_ref],
+        [row_out(BF), row_out(F32), row_out(F32)] + units + vec_out,
+        scratch=bufs + [pltpu.SemaphoreType.DMA((8,))],
+    )(xs, ycls, p, g, vec, fc_in, fc_out, in_bias.astype(F32)[None], near, near_s)
+    units_in = []
+    near_out = []
+    near_args = []
+    near_scratch = []
+    if hosted():
+        units_in = [any_ref, any_ref]
+        near_args = [halves(a_own), halves(a_oth)]
+        near_out = [(whole(2, 96, WIDTH), jax.ShapeDtypeStruct((2, 96, WIDTH), F32))]
+        near_scratch = PlaneSum.scratch(384) + [pltpu.VMEM((2, 96, WIDTH), BF), pltpu.SemaphoreType.DMA((2, 2))]
+    layer_out, dxs, b_own, b_oth, gv_m, gb_b, *near_sum = call(
+        partial(mlp_kernel, False), "mlp_far", (last + 3,),
+        [row_in, whole(FRAMES, 8, WIDTH),
+         pl.BlockSpec((1, TILE, WIDTH), lambda i: (0, CLASS // TILE, 0)), row_in,
+         whole(nvec, WIDTH), row_in, row_in, row_in, any_ref, any_ref, any_ref, any_ref] + units_in,
+        [(whole(1, tokens, WIDTH), jax.ShapeDtypeStruct((1, tokens, WIDTH), BF)), row_out(F32)] + units + vec_out + near_out,
+        scratch=bufs + [pltpu.VMEM((tokens, WIDTH), F32), pltpu.SemaphoreType.DMA((8,))] + near_scratch,
+        remote=1 if hosted() else None,
+    )(xs, ycls, p, g, vec, hm, acc, dh, far1, far1_s, far2, far2_s, *near_args)
     dys, dzs, df, dyt, dot, gv_s = call(
         space_back_kernel, "space_back", steps,
         [frames(WIDTH), pl.BlockSpec((1, 8, WIDTH), lambda i: (0, CLASS // 8, 0)), frames(WIDTH),
@@ -417,62 +813,66 @@
         scratch=[pltpu.VMEM((STEP, WIDTH), BF)],
         flops=3 * 10**10, nbytes=50 * 2**20,
     )(dxs, dxs, full, zs, a_s, vec, space_proj, space_qkv, time_proj)
-    g_s_proj = weight_grad(o_s.reshape(rows, WIDTH), dys.reshape(rows, WIDTH), "grad_space_proj", 384)
-    g_s_qkv = weight_grad(dzs.reshape(rows, 3 * WIDTH), hs.reshape(rows, WIDTH), "grad_space_qkv", 768)
+    s_own, s_oth = pair_grad(dzs, hs, dys, o_s, "grad_space")
     dzt, = call(
         time_back_kernel, "time_back", (chunks,),
         [chunk(3 * WIDTH), a_time[0], chunk(WIDTH)], [chunk_out(3 * WIDTH)],
         flops=10**10, nbytes=24 * 2**20,
     )(zt, at, dot)
-    g_t_proj = weight_grad(ot.reshape(rows, WIDTH), dyt.reshape(rows, WIDTH), "grad_time_proj", 384)
-    g_t_qkv = weight_grad(dzt.reshape(rows, 3 * WIDTH), ht.reshape(rows, WIDTH), "grad_time_qkv", 768)
-    dp, gv_t = call(
+    t_own, t_oth = pair_grad(dzt, ht, dyt, ot, "grad_time")
+    grad_clips, gv_t = call(
         time_out_kernel, "time_out", steps,
         [frames(3 * WIDTH), frames(WIDTH), frames(WIDTH), whole(nvec, WIDTH), whole(WIDTH, 3 * WIDTH)],
-        [frames_out(WIDTH, F32), (whole(8, 3 * WIDTH), jax.ShapeDtypeStruct((8, 3 * WIDTH), F32))],
+        [(whole(1, tokens, WIDTH), jax.ShapeDtypeStruct((1, tokens, WIDTH), F32)),
+         (whole(8, 3 * WIDTH), jax.ShapeDtypeStruct((8, 3 * WIDTH), F32))],
         flops=6 * rows * WIDTH * WIDTH, nbytes=28 * 2**20,
     )(dzt, p, df, vec, time_qkv)
 
-    layer_out = unpad(out, out[0, CLASS : CLASS + 1])
-    grad_clips = unpad(dp, jnp.sum(df[:, CLASS], axis=0, keepdims=True))
-
-    def scatter(grad, swap):
-        part = lax.psum_scatter(grad, "wide", scatter_dimension=0, tiled=True)
-        part = lax.psum_scatter(part, "narrow", scatter_dimension=1, tiled=True)
-        part = part.astype(F32)
-        return part.T if swap else part
+    if hosted():
+        fc = near_sum[0]
+    else:
+        near_sum = unit_sum(a_own, a_oth)
+        fc = near_sum[:, 0].astype(F32) + flip(near_sum[:, 1], "narrow", 1).astype(F32)
+    far_sum = unit_sum(b_own, b_oth)
+    fc = fc + flip(far_sum[:, 0], "narrow", 2).astype(F32) + flip(far_sum[:, 1], "narrow", 3).astype(F32)
+    s_qkv, s_proj = pair_sum(s_own, s_oth, me_n)
+    t_qkv, t_proj = pair_sum(t_own, t_oth, me_n)
 
     vectors = jnp.stack(
         [gv_m[0], gv_m[1], gv_m[2],
          gv_s[0, :WIDTH], gv_s[1, :WIDTH], gv_s[1, 2 * WIDTH :], gv_s[2, :WIDTH], gv_s[3, :WIDTH], gv_s[4, :WIDTH],
          gv_t[0, :WIDTH], gv_t[0, 2 * WIDTH :], gv_t[1, :WIDTH], gv_t[2, :WIDTH]]
     )
-    vectors = jnp.concatenate([vectors, gb_m[0].reshape(slices, WIDTH)], axis=0)
+    lower = me_n < 2
+    places = (me_n, jnp.bitwise_xor(me_n, 1), jnp.where(lower, 2, 1), jnp.where(lower, 3, 0))
+    hidden_rows = jnp.zeros((slices, WIDTH), F32)
+    for place, row in zip(places, (gb_a[0], gb_a[1], gb_b[0], gb_b[1])):
+        hidden_rows = lax.dynamic_update_slice(hidden_rows, row[None], (place, 0))
+    vectors = jnp.concatenate([vectors, hidden_rows], axis=0)
     vectors = lax.psum(vectors, ("wide", "narrow"))
-    me = lax.axis_index("narrow")
     share = WIDTH // slices
-    mine = lax.dynamic_slice(vectors, (0, me * share), (13, share))
-    grad_in_bias = lax.dynamic_slice(vectors, (13 + me, 0), (1, WIDTH))[0]
+    mine = lax.dynamic_slice(vectors, (0, me_n * share), (13, share))
+    grad_in_bias = lax.dynamic_slice(vectors, (13 + me_n, 0), (1, WIDTH))[0]
     return (
         layer_out,
         grad_clips,
         mine[11],
         mine[12],
-        scatter(g_t_qkv, True),
+        t_qkv,
         mine[9:11],
-        scatter(g_t_proj.T, True),
+        t_proj,
         mine[8],
         mine[6],
         mine[7],
-        scatter(g_s_qkv, True),
+        s_qkv,
         mine[4:6],
-        scatter(g_s_proj.T, True),
+        s_proj,
         mine[3],
         mine[0],
         mine[1],
-        scatter(g_fc_in, False),
+        fc[0],
         grad_in_bias,
-        scatter(g_fc_out, True),
+        fc[1].T,
         mine[2],
     )
 

time: 729 us -> 503 us (0.69)
  waiting for transfers between devices: 317 us -> 106 us
  local copies, waits for them, and re-layouts: 71.9 us -> 28.1 us
  starting transfers between devices: 0.57 us -> 32.8 us
  Pallas kernels: 246 us -> 269 us
  blocking collectives: 55.6 us -> 39 us
  between operations: 14.5 us -> 1.52 us
    reduce_scatter x8 -> x0, waiting for transfers between devices: 180 us -> none  [the longest x4 117 us: scatter(): part = lax.psum_scatter(grad, 'wide', scatter_dimension=0, tiled=True)]
    ppermute x0 -> x31, waiting for transfers between devices: none -> 106 us  [the longest x27 89.2 us: flip(): lax.ppermute(value, axis, [(i, i ^ bit) for i in range(lax.axis_size(axis...]
    all_gather x2 -> x0, waiting for transfers between devices: 93.9 us -> none  [the longest x1 89.4 us: local(): wo = lax.all_gather(fc_out, 'narrow', axis=0)]
    unnamed x18 -> x0, waiting for transfers between devices: 43.2 us -> none
    ppermute x0 -> x31, starting transfers between devices: none -> 32.8 us  [the longest x27 27.7 us: flip(): lax.ppermute(value, axis, [(i, i ^ bit) for i in range(lax.axis_size(axis...]
    unnamed x16 -> x50, local copies, waits for them, and re-layouts: 43.8 us -> 14.7 us
    pallas_call x7 -> x4, Pallas kernels: 107 us -> 130 us  [the longest x1 56.6 us: local(): call(partial(mlp_kernel, False), 'mlp_far', (last + 3,), [row_in, whole(F...]
    all_gather x1 -> x0, blocking collectives: 15.5 us -> none  [local(): lax.all_gather(in_bias.astype(F32), 'narrow', axis=0, tiled=True)[None]]
  transfers between devices with their start and end apart: 14 -> 31, of which waited for: 11 -> 10; matrix products, arithmetic and copies ran while one was open for 12% -> 8% of each run, Pallas kernels for 21% -> 43%
where the time goes in v2:
time: 503 us; the launch traced here: 495 us
  Pallas kernels  269 us (53%)
  waiting for transfers between devices  106 us (21%)
  blocking collectives  39 us (8%)
  starting transfers between devices  32.8 us (7%)
  local copies, waits for them, and re-layouts  28.1 us (6%)
  other arithmetic  18.6 us (4%)
    ppermute x27, waiting for transfers between devices, flip(): lax.ppermute(value, axis, [(i, i ^ bit) for i in range(lax.axis_size(axis...  89.2 us
    pallas_call x1, Pallas kernels, local(): call(partial(mlp_kernel, False), 'mlp_far', (last + 3,), [row_in, whole(F...  56.6 us
    pallas_call x1, Pallas kernels, local(): call(space_back_kernel, 'space_back', steps, [frames(WIDTH), pl.BlockSpec...  40.1 us
    pallas_call x1, Pallas kernels, local(): call(partial(mlp_kernel, True), 'mlp_near', (last + 3,), [row_in, whole(F...  40 us
    psum x1, blocking collectives, local(): vectors = lax.psum(vectors, ('wide', 'narrow'))  39 us
    pallas_call x2, Pallas kernels, pair_grad(): call(pair_grad_kernel, name, (3,), [pl.BlockSpec((rows, 3 * WIDTH // 2),...  32.9 us
    pallas_call x1, Pallas kernels, local(): call(space_kernel, 'space', steps, [frames(WIDTH), frames(WIDTH), whole(n...  29.3 us
    ppermute x27, starting transfers between devices, flip(): lax.ppermute(value, axis, [(i, i ^ bit) for i in range(lax.axis_size(axis...  27.7 us
  transfers between devices with their start and end apart: 31, of which 10 were waited for; matrix products, arithmetic and copies ran while one was open for 8% of the time, Pallas kernels for 43%

profile of v2, /device:TPU:0, one launch (start us, length us, event | category | flops | bytes accessed | tf_op | source)
XLA Modules:
  0.0 494.7 jit_solution(10816775908356058120)
XLA Ops:
  0.8 1.5 broadcast_select_fusion.2
  2.4 3.1 collective-permute-start
  5.4 0.7 collective-permute-start.2
  6.2 25.9 %collective-permute-done.refs_8_ = bf16[784,768]{1,0:T(8,128)(2,1)} collective-permute-done((bf16[784,768]{1,0:T(8,128)(2,1)S(1)}, bf16[784,768]{1,0:T(8,128)(2,1)}, u32[]{:S(2)}, u32[]{:S(2)}) %collective-permute-start) | collective-permute-done | bytes 1204256 | tf_op jit(solution)/shard_map/ppermute | solution.py:641
  32.0 1.7 collective-permute-start.5
  34.0 0.6 convert_element_type.304.vec_ref.refs_4_
  35.3 1.3 collective-permute-start.3
  36.6 14.3 %time_in.1 = (bf16[8,208,768]{2,1,0:T(8,128)(2,1)}, bf16[8,208,768]{2,1,0:T(8,128)(2,1)}, bf16[8,208,768]{2,1,0:T(8,128)(2,1)}, bf16[8,208,2304]{2,1,0:T(8,128)(2,1)}) custom-call(bf16[1569,768]{1,0:T(8,128)(2,1)} %bitcast.134, bf16[1569,768]{1,0:T(8,128)(2,1)} %bitcast.135, f32[9,768]{1,0:T(8,128)} %convert_element_type.304.vec_ref.refs_4_, ...), custom_call_target="tpu_custom_call" | custom-call | flops 5888802816 | bytes 25165824 | tf_op jit(solution)/shard_map/time_in/pallas_call | solution.py:744
  51.5 1.3 collective-permute-start.6
  52.8 19.6 %time_attention.1 = (bf16[8,208,768]{2,1,0:T(8,128)(2,1)}, bf16[13,3,512,128]{3,2,1,0:T(8,128)(2,1)}) custom-call(bf16[8,208,2304]{2,1,0:T(8,128)(2,1)} %get-tuple-element.59.z_ref), custom_call_target="tpu_custom_call" | custom-call | flops 10000000000 | bytes 16777216 | tf_op jit(solution)/shard_map/time_attention/pallas_call | solution.py:750
  72.4 1.4 broadcast_select_fusion.1.refs_8_
  74.4 16.9 %collective-permute-done.6 = bf16[784,768]{1,0:T(8,128)(2,1)} collective-permute-done((bf16[784,768]{1,0:T(8,128)(2,1)}, bf16[784,768]{1,0:T(8,128)(2,1)}, u32[]{:S(2)}, u32[]{:S(2)}) %collective-permute-start.6) | collective-permute-done | bytes 1204256 | tf_op jit(solution)/shard_map/ppermute | solution.py:645
  91.3 2.5 broadcast_select_fusion.refs_10_
  93.7 29.3 %space.1 = (f32[8,208,768]{2,1,0:T(8,128)}, bf16[8,208,768]{2,1,0:T(8,128)(2,1)}, bf16[8,208,2304]{2,1,0:T(8,128)(2,1)}, bf16[8,3,832,208]{3,2,1,0:T(8,128)(2,1)...) custom-call(bf16[8,208,768]{2,1,0:T(8,128)(2,1)} %get-tuple-element.58.p_ref.refs_2_, ...), custom_call_target="tpu_custom_call" | custom-call | flops 30000001024 | bytes 41943040 | tf_op jit(solution)/shard_map/space/pallas_call | solution.py:755
  123.6 40.0 %mlp_near.1 = (bf16[8,208,768]{2,1,0:T(8,128)(2,1)}, f32[8,208,768]{2,1,0:T(8,128)}, f32[8,208,768]{2,1,0:T(8,128)}, bf16[4,4,96,768]{3,2,1,0:T(8,128)(2,1)}, bf...) custom-call(f32[8,208,768]{2,1,0:T(8,128)} %get-tuple-element.61.refs_0_, ...), custom_call_target="tpu_custom_call" | custom-call | tf_op jit(solution)/shard_map/mlp_near/pallas_call | solution.py:779
  163.6 0.8 fusion.30
  164.6 56.6 %mlp_far.1 = (bf16[1,1569,768]{2,1,0:T(8,128)(2,1)}, f32[8,208,768]{2,1,0:T(8,128)}, bf16[4,4,96,768]{3,2,1,0:T(8,128)(2,1)}, bf16[4,4,96,768]{3,2,1,0:T(8,128)(...) custom-call(f32[8,208,768]{2,1,0:T(8,128)} %get-tuple-element.61.refs_0_, ...), custom_call_target="tpu_custom_call" | custom-call | tf_op jit(solution)/shard_map/mlp_far/pallas_call | solution.py:796
  221.3 40.1 %space_back.1 = (bf16[8,208,768]{2,1,0:T(8,128)(2,1)}, bf16[8,208,2304]{2,1,0:T(8,128)(2,1)}, f32[8,208,768]{2,1,0:T(8,128)}, bf16[8,208,768]{2,1,0:T(8,128)(2,1...) custom-call(f32[8,208,768]{2,1,0:T(8,128)} %get-tuple-element.71.dx_ref.dcls_ref, ...), custom_call_target="tpu_custom_call" | custom-call | flops 30000001024 | bytes 52428800 | tf_op jit(solution)/shard_map/space_back/pallas_call | solution.py:805
  261.4 16.5 %grad_space.1 = (bf16[4,384,768]{2,1,0:T(8,128)(2,1)}, bf16[4,384,768]{2,1,0:T(8,128)(2,1)}) custom-call(bf16[1664,2304]{1,0:T(8,128)(2,1)} %bitcast.109, bf16[1664,768]{1,0:T(8,128)(2,1)} %bitcast.112, bf16[1664,768]{1,0:T(8,128)(2,1)} %bitcast.115, bf16[1664,768]{1,0:T(8,128)(2,1)} %bitcast.113), custom_call_target="tpu_custom_call" | custom-call | tf_op jit(solution)/shard_map/grad_space/pallas_call | solution.py:632
  278.4 20.9 %time_back.1.dz_ref = bf16[8,208,2304]{2,1,0:T(8,128)(2,1)} custom-call(bf16[8,208,2304]{2,1,0:T(8,128)(2,1)} %get-tuple-element.59.z_ref, bf16[13,3,512,128]{3,2,1,0:T(8,128)(2,1)} %get-tuple-element.70.a_ref, bf16[8,208,768]{2,1,0:T(8,128)(2,1)} %get-tuple-element.75.do_ref), custom_call_target="tpu_custom_call" | custom-call | flops 10000000000 | bytes 25165824 | tf_op jit(solution)/shard_map/time_back/pallas_call | solution.py:817
  299.3 16.5 %grad_time.1 = (bf16[4,384,768]{2,1,0:T(8,128)(2,1)}, bf16[4,384,768]{2,1,0:T(8,128)(2,1)}) custom-call(bf16[1664,2304]{1,0:T(8,128)(2,1)} %bitcast.108, bf16[1664,768]{1,0:T(8,128)(2,1)} %bitcast.110, bf16[1664,768]{1,0:T(8,128)(2,1)} %bitcast.114, bf16[1664,768]{1,0:T(8,128)(2,1)} %bitcast.111), custom_call_target="tpu_custom_call" | custom-call | tf_op jit(solution)/shard_map/grad_time/pallas_call | solution.py:632
  315.8 14.9 %time_out.1 = (f32[1,1569,768]{2,1,0:T(8,128)}, f32[8,2304]{1,0:T(8,128)}) custom-call(bf16[8,208,2304]{2,1,0:T(8,128)(2,1)} %time_back.1.dz_ref, bf16[8,208,768]{2,1,0:T(8,128)(2,1)} %get-tuple-element.58.p_ref.refs_2_, f32[8,208,768]{2,1,0:T(8,128)} %get-tuple-element.76.df_ref, f32[9,768]{1,0:T(8,128)} %convert_element_type.304.vec_ref.refs_4_, ...), custom_call_target="tpu_custom_call" | custom-call | flops 5888802816 | bytes 29360128 | tf_op jit(solution)/shard_map/time_out/pallas_call | solution.py:823
  330.6 0.7 slice.202
  331.4 0.7 slice.200
  332.1 0.7 slice.201
  332.8 0.7 slice.205
  333.6 13.2 %copy.53 = f32[1,1569,768]{2,0,1:T(1,128)} copy(f32[1,1569,768]{2,1,0:T(8,128)} %get-tuple-element.117) | data formatting | bytes 9639936
  346.8 0.8 fusion.29
  347.7 0.8 fusion.28
  348.7 39.0 %psum.7 = f32[17,768]{1,0:T(8,128)S(1)} all-reduce(f32[17,768]{1,0:T(8,128)S(1)} %concatenate.17), channel_id=1, replica_groups=mesh['wide'=8,'narrow'=4] {'wide','narrow'}, use_global_device_ids=true, to_apply=%region_0.1 | all-reduce | flops 13056 | bytes 104448 | tf_op jit(solution)/shard_map/psum | solution.py:852
  388.4 0.7 fusion.26
  389.0 2.2 fusion
  391.4 2.3 collective-permute-start.25
  394.4 2.2 add_convert_fusion
  396.7 1.5 collective-permute-start.17
  398.4 2.2 add_convert_fusion.1
  400.7 2.0 collective-permute-start.9
  402.8 5.3 %collective-permute-done.25 = bf16[2,192,768]{2,1,0:T(8,128)(2,1)S(1)} collective-permute-done((bf16[2,192,768]{2,1,0:T(8,128)(2,1)S(1)}, bf16[2,192,768]{2,1,0:T(8,128)(2,1)S(1)}, u32[]{:S(2)}, u32[]{:S(2)}) %collective-permute-start.25) | collective-permute-done | bytes 589856 | tf_op jit(solution)/shard_map/ppermute | solution.py:641
  408.0 2.0 collective-permute-start.11
  410.0 0.7 fusion.27
  410.9 9.7 %collective-permute-done.17 = bf16[2,192,768]{2,1,0:T(8,128)(2,1)S(1)} collective-permute-done((bf16[2,192,768]{2,1,0:T(8,128)(2,1)S(1)}, bf16[2,192,768]{2,1,0:T(8,128)(2,1)S(1)}, u32[]{:S(2)}, u32[]{:S(2)}) %collective-permute-start.17) | collective-permute-done | bytes 589856 | tf_op jit(solution)/shard_map/ppermute | solution.py:641
  420.7 2.0 collective-permute-start.28
  422.8 0.6 collective-permute-start.18
  423.5 9.8 %collective-permute-done.9 = bf16[2,192,768]{2,1,0:T(8,128)(2,1)S(1)} collective-permute-done((bf16[2,192,768]{2,1,0:T(8,128)(2,1)S(1)}, bf16[2,192,768]{2,1,0:T(8,128)(2,1)S(1)}, u32[]{:S(2)}, u32[]{:S(2)}) %collective-permute-start.9) | collective-permute-done | bytes 589856 | tf_op jit(solution)/shard_map/ppermute | solution.py:641
  433.3 2.0 collective-permute-start.20
  435.3 1.0 fusion.8
  436.9 4.7 collective-permute-done.26
  442.0 0.9 slice_bitcast_fusion.3
  442.9 1.6 collective-permute-start.29
  444.5 3.5 collective-permute-done.18
  447.9 1.6 collective-permute-start.30
  450.1 0.8 dynamic-slice_bitcast_fusion.2
  451.4 2.3 collective-permute-start.22
  453.7 1.6 collective-permute-start.23
  455.2 1.4 fusion.6
  457.1 5.9 %collective-permute-done.21 = bf16[192,384]{1,0:T(8,128)(2,1)S(1)} collective-permute-done((bf16[192,384]{1,0:T(8,128)(2,1)}, bf16[192,384]{1,0:T(8,128)(2,1)S(1)}, u32[]{:S(2)}, u32[]{:S(2)}) %collective-permute-start.21) | collective-permute-done | bytes 147488 | tf_op jit(solution)/shard_map/ppermute | solution.py:641
  463.5 17.8 %collective-permute-done.22 = bf16[192,384]{1,0:T(8,128)(2,1)S(1)} collective-permute-done((bf16[192,384]{1,0:T(8,128)(2,1)}, bf16[192,384]{1,0:T(8,128)(2,1)S(1)}, u32[]{:S(2)}, u32[]{:S(2)}) %collective-permute-start.22) | collective-permute-done | bytes 147488 | tf_op jit(solution)/shard_map/ppermute | solution.py:641
  481.3 1.6 collective-permute-start.15
  483.0 0.8 slice.282
  483.7 6.5 %collective-permute-done.14 = bf16[192,384]{1,0:T(8,128)(2,1)S(1)} collective-permute-done((bf16[192,384]{1,0:T(8,128)(2,1)S(1)}, bf16[192,384]{1,0:T(8,128)(2,1)S(1)}, u32[]{:S(2)}, u32[]{:S(2)}) %collective-permute-start.14) | collective-permute-done | bytes 147488 | tf_op jit(solution)/shard_map/ppermute | solution.py:641
  490.3 0.8 slice.270
  491.1 1.1 convert_add_fusion.7
  492.2 0.8 slice_bitcast_fusion
  493.1 1.4 copy.61
  (127 shorter events, 8.8 us)
Async XLA Ops:
  0.7 1.6 copy-start.11
  0.7 33.1 %copy-start.15 = (bf16[768]{0:T(1024)(128)(2,1)S(1)}, bf16[768]{0:T(1024)(128)(2,1)}, u32[]{:S(2)}) copy-start(bf16[768]{0:T(1024)(128)(2,1)} %param.21) | copy-start | bytes 4612
  0.7 33.1 %copy-start.16 = (bf16[768]{0:T(1024)(128)(2,1)S(1)}, bf16[768]{0:T(1024)(128)(2,1)}, u32[]{:S(2)}) copy-start(bf16[768]{0:T(1024)(128)(2,1)} %param.22) | copy-start | bytes 4612
  0.7 33.1 %copy-start.17 = (bf16[768]{0:T(1024)(128)(2,1)S(1)}, bf16[768]{0:T(1024)(128)(2,1)}, u32[]{:S(2)}) copy-start(bf16[768]{0:T(1024)(128)(2,1)} %param.26) | copy-start | bytes 4612
  0.7 33.1 %copy-start.18 = (bf16[768]{0:T(1024)(128)(2,1)S(1)}, bf16[768]{0:T(1024)(128)(2,1)}, u32[]{:S(2)}) copy-start(bf16[768]{0:T(1024)(128)(2,1)} %param.27) | copy-start | bytes 4612
  0.7 33.1 %copy-start.19 = (bf16[768]{0:T(1024)(128)(2,1)S(1)}, bf16[768]{0:T(1024)(128)(2,1)}, u32[]{:S(2)}) copy-start(bf16[768]{0:T(1024)(128)(2,1)} %param.28) | copy-start | bytes 4612
  0.7 33.1 %copy-start.20 = (bf16[768]{0:T(1024)(128)(2,1)S(1)}, bf16[768]{0:T(1024)(128)(2,1)}, u32[]{:S(2)}) copy-start(bf16[768]{0:T(1024)(128)(2,1)} %param.32) | copy-start | bytes 4612
  0.7 33.1 %copy-start.21 = (bf16[768]{0:T(1024)(128)(2,1)S(1)}, bf16[768]{0:T(1024)(128)(2,1)}, u32[]{:S(2)}) copy-start(bf16[768]{0:T(1024)(128)(2,1)} %param.33) | copy-start | bytes 4612
  0.8 33.2 %copy-start.22 = (bf16[768]{0:T(1024)(128)(2,1)S(1)}, bf16[768]{0:T(1024)(128)(2,1)}, u32[]{:S(2)}) copy-start(bf16[768]{0:T(1024)(128)(2,1)} %param.34) | copy-start | bytes 4612
  0.8 33.2 %copy-start.23 = (bf16[768]{0:T(1024)(128)(2,1)S(1)}, bf16[768]{0:T(1024)(128)(2,1)}, u32[]{:S(2)}) copy-start(bf16[768]{0:T(1024)(128)(2,1)} %param.38) | copy-start | bytes 4612
  0.8 33.9 %copy-start.13 = (bf16[2,768]{1,0:T(2,128)(2,1)S(1)}, bf16[2,768]{1,0:T(2,128)(2,1)}, u32[]{:S(2)}) copy-start(bf16[2,768]{1,0:T(2,128)(2,1)} %param.24) | copy-start | bytes 9220
  2.4 29.7 %collective-permute-start = (bf16[784,768]{1,0:T(8,128)(2,1)S(1)}, bf16[784,768]{1,0:T(8,128)(2,1)}, u32[]{:S(2)}, u32[]{:S(2)}) collective-permute-start(bf16[784,768]{1,0:T(8,128)(2,1)S(1)} %pad_maximum_fusion), channel_id=1, source_target_pairs={{0,1},{1,0},{2,3},{3,2},{4,5},{5,4},{6,7},{7,6},{8,9},{9,8},{10,11... | collective-permute-start | bytes 3612680 | tf_op jit(solution)/shard_map/ppermute | solution.py:641
  5.4 29.8 %collective-permute-start.2 = (bf16[784,768]{1,0:T(8,128)(2,1)S(1)}, bf16[784,768]{1,0:T(8,128)(2,1)S(1)}, u32[]{:S(2)}, u32[]{:S(2)}) collective-permute-start(bf16[784,768]{1,0:T(8,128)(2,1)S(1)} %pad_maximum_fusion), channel_id=1, source_target_pairs={{1,2},{2,1},{5,6},{6,5},{9,10},{10,9},{13,14},{14,13},{17,18},{18,... | collective-permute-start | bytes 3612680 | tf_op jit(solution)/shard_map/ppermute | solution.py:645
  32.0 19.5 %collective-permute-start.5 = (bf16[784,768]{1,0:T(8,128)(2,1)}, bf16[784,768]{1,0:T(8,128)(2,1)}, u32[]{:S(2)}, u32[]{:S(2)}) collective-permute-start(bf16[784,768]{1,0:T(8,128)(2,1)} %collective-permute-done.refs_8_), channel_id=1, source_target_pairs={{1,2},{2,1},{5,6},{6,5},{9,10},{10,9},{13,14},{14,13},{17,18},{18,... | collective-permute-start | bytes 3612680 | tf_op jit(solution)/shard_map/ppermute | solution.py:645
  35.3 15.7 %copy-start.5 = (bf16[784,768]{1,0:T(8,128)(2,1)}, bf16[784,768]{1,0:T(8,128)(2,1)S(1)}, u32[]{:S(2)}) copy-start(bf16[784,768]{1,0:T(8,128)(2,1)S(1)} %collective-permute-done.2) | copy-start | bytes 3612676
  35.3 37.2 %collective-permute-start.3 = (bf16[784,768]{1,0:T(8,128)(2,1)S(1)}, bf16[784,768]{1,0:T(8,128)(2,1)}, u32[]{:S(2)}, u32[]{:S(2)}) collective-permute-start(bf16[784,768]{1,0:T(8,128)(2,1)S(1)} %collective-permute-done.2), channel_id=1, source_target_pairs={{1,0},{2,3},{5,4},{6,7},{9,8},{10,11},{13,12},{14,15},{17,16},{18,... | collective-permute-start | bytes 3612680 | tf_op jit(solution)/shard_map/ppermute | solution.py:645
  36.5 14.4 %copy-start.14 = (bf16[2,768]{1,0:T(2,128)(2,1)S(1)}, bf16[2,768]{1,0:T(2,128)(2,1)}, u32[]{:S(2)}) copy-start(bf16[2,768]{1,0:T(2,128)(2,1)} %param.30) | copy-start | bytes 9220
  51.5 39.8 %collective-permute-start.6 = (bf16[784,768]{1,0:T(8,128)(2,1)}, bf16[784,768]{1,0:T(8,128)(2,1)}, u32[]{:S(2)}, u32[]{:S(2)}) collective-permute-start(bf16[784,768]{1,0:T(8,128)(2,1)} %collective-permute-done.5), channel_id=1, source_target_pairs={{1,0},{2,3},{5,4},{6,7},{9,8},{10,11},{13,12},{14,15},{17,16},{18,... | collective-permute-start | bytes 3612680 | tf_op jit(solution)/shard_map/ppermute | solution.py:645
  72.4 51.2 %collective-permute-start.1 = (bf16[784,768]{1,0:T(8,128)(2,1)}, bf16[784,768]{1,0:T(8,128)(2,1)}, u32[]{:S(2)}, u32[]{:S(2)}) collective-permute-start(bf16[784,768]{1,0:T(8,128)(2,1)} %collective-permute-done.refs_8_), channel_id=1, source_target_pairs={{0,4},{4,0},{8,12},{12,8},{16,20},{20,16},{24,28},{28,24},{1,5},{5... | collective-permute-start | bytes 3612680 | tf_op jit(solution)/shard_map/ppermute | solution.py:641
  73.8 49.2 %copy-start = (bf16[784,768]{1,0:T(8,128)(2,1)}, bf16[784,768]{1,0:T(8,128)(2,1)S(1)}, u32[]{:S(2)}) copy-start(bf16[784,768]{1,0:T(8,128)(2,1)S(1)} %broadcast_select_fusion.1.refs_8_) | copy-start | bytes 3612676
  73.9 90.7 %collective-permute-start.4 = (bf16[784,768]{1,0:T(8,128)(2,1)S(1)}, bf16[784,768]{1,0:T(8,128)(2,1)}, u32[]{:S(2)}, u32[]{:S(2)}) collective-permute-start(bf16[784,768]{1,0:T(8,128)(2,1)S(1)} %broadcast_select_fusion.1.refs_8_), channel_id=1, source_target_pairs={{0,4},{4,0},{8,12},{12,8},{16,20},{20,16},{24,28},{28,24},{1,5},{5... | collective-permute-start | bytes 3612680 | tf_op jit(solution)/shard_map/ppermute | solution.py:641
  93.7 70.8 %collective-permute-start.7 = (bf16[784,768]{1,0:T(8,128)(2,1)}, bf16[784,768]{1,0:T(8,128)(2,1)}, u32[]{:S(2)}, u32[]{:S(2)}) collective-permute-start(bf16[784,768]{1,0:T(8,128)(2,1)} %broadcast_select_fusion.refs_10_), channel_id=1, source_target_pairs={{0,4},{4,0},{8,12},{12,8},{16,20},{20,16},{24,28},{28,24},{1,5},{5... | collective-permute-start | bytes 3612680 | tf_op jit(solution)/shard_map/ppermute | solution.py:641
  221.2 167.8 %collective-permute-start.24 = (bf16[4,384,768]{2,1,0:T(8,128)(2,1)}, bf16[4,384,768]{2,1,0:T(8,128)(2,1)}, u32[]{:S(2)}, u32[]{:S(2)}) collective-permute-start(bf16[4,384,768]{2,1,0:T(8,128)(2,1)} %bitcast.136), channel_id=1, source_target_pairs={{0,4},{4,0},{8,12},{12,8},{16,20},{20,16},{24,28},{28,24},{1,5},{5... | collective-permute-start | bytes 7077896 | tf_op jit(solution)/shard_map/ppermute | solution.py:641
  277.9 116.5 %collective-permute-start.16 = (bf16[4,384,768]{2,1,0:T(8,128)(2,1)}, bf16[4,384,768]{2,1,0:T(8,128)(2,1)}, u32[]{:S(2)}, u32[]{:S(2)}) collective-permute-start(bf16[4,384,768]{2,1,0:T(8,128)(2,1)} %get-tuple-element.92), channel_id=1, source_target_pairs={{0,4},{4,0},{8,12},{12,8},{16,20},{20,16},{24,28},{28,24},{1,5},{5... | collective-permute-start | bytes 7077896 | tf_op jit(solution)/shard_map/ppermute | solution.py:641
  315.7 82.6 %collective-permute-start.8 = (bf16[4,384,768]{2,1,0:T(8,128)(2,1)}, bf16[4,384,768]{2,1,0:T(8,128)(2,1)}, u32[]{:S(2)}, u32[]{:S(2)}) collective-permute-start(bf16[4,384,768]{2,1,0:T(8,128)(2,1)} %get-tuple-element.86), channel_id=1, source_target_pairs={{0,4},{4,0},{8,12},{12,8},{16,20},{20,16},{24,28},{28,24},{1,5},{5... | collective-permute-start | bytes 7077896 | tf_op jit(solution)/shard_map/ppermute | solution.py:641
  315.7 17.8 %copy-start.12 = (f32[8,768]{1,0:T(8,128)S(1)}, f32[8,768]{1,0:T(8,128)}, u32[]{:S(2)}) copy-start(f32[8,768]{1,0:T(8,128)} %get-tuple-element.78) | copy-start | bytes 73732
  333.6 55.5 %copy-start.2 = (bf16[4,4,96,768]{3,2,1,0:T(8,128)(2,1)S(1)}, bf16[4,4,96,768]{3,2,1,0:T(8,128)(2,1)}, u32[]{:S(2)}) copy-start(bf16[4,4,96,768]{3,2,1,0:T(8,128)(2,1)} %get-tuple-element.94) | copy-start | bytes 7077892
  391.3 3.1 copy-start.4
  391.4 16.6 %collective-permute-start.25 = (bf16[2,192,768]{2,1,0:T(8,128)(2,1)S(1)}, bf16[2,192,768]{2,1,0:T(8,128)(2,1)S(1)}, u32[]{:S(2)}, u32[]{:S(2)}) collective-permute-start(bf16[2,192,768]{2,1,0:T(8,128)(2,1)S(1)} %pad_maximum_fusion.3), channel_id=1, source_target_pairs={{0,8},{4,12},{8,0},{12,4},{16,24},{20,28},{24,16},{28,20},{1,9},{5... | collective-permute-start | bytes 1769480 | tf_op jit(solution)/shard_map/ppermute | solution.py:641
  393.8 16.9 %collective-permute-start.27 = (bf16[2,192,768]{2,1,0:T(8,128)(2,1)S(1)}, bf16[2,192,768]{2,1,0:T(8,128)(2,1)S(1)}, u32[]{:S(2)}, u32[]{:S(2)}) collective-permute-start(bf16[2,192,768]{2,1,0:T(8,128)(2,1)S(1)} %stack.66), channel_id=1, source_target_pairs={{0,16},{4,20},{8,24},{12,28},{16,0},{20,4},{24,8},{28,12},{1,17},{... | collective-permute-start | bytes 1769480 | tf_op jit(solution)/shard_map/ppermute | solution.py:641
  396.6 1.8 copy-start.3
  396.7 23.9 %collective-permute-start.17 = (bf16[2,192,768]{2,1,0:T(8,128)(2,1)S(1)}, bf16[2,192,768]{2,1,0:T(8,128)(2,1)S(1)}, u32[]{:S(2)}, u32[]{:S(2)}) collective-permute-start(bf16[2,192,768]{2,1,0:T(8,128)(2,1)S(1)} %pad_maximum_fusion.2), channel_id=1, source_target_pairs={{0,8},{4,12},{8,0},{12,4},{16,24},{20,28},{24,16},{28,20},{1,9},{5... | collective-permute-start | bytes 1769480 | tf_op jit(solution)/shard_map/ppermute | solution.py:641
  398.3 24.4 %collective-permute-start.19 = (bf16[2,192,768]{2,1,0:T(8,128)(2,1)S(1)}, bf16[2,192,768]{2,1,0:T(8,128)(2,1)S(1)}, u32[]{:S(2)}, u32[]{:S(2)}) collective-permute-start(bf16[2,192,768]{2,1,0:T(8,128)(2,1)S(1)} %stack.65), channel_id=1, source_target_pairs={{0,16},{4,20},{8,24},{12,28},{16,0},{20,4},{24,8},{28,12},{1,17},{... | collective-permute-start | bytes 1769480 | tf_op jit(solution)/shard_map/ppermute | solution.py:641
  400.7 32.6 %collective-permute-start.9 = (bf16[2,192,768]{2,1,0:T(8,128)(2,1)S(1)}, bf16[2,192,768]{2,1,0:T(8,128)(2,1)S(1)}, u32[]{:S(2)}, u32[]{:S(2)}) collective-permute-start(bf16[2,192,768]{2,1,0:T(8,128)(2,1)S(1)} %pad_maximum_fusion.1), channel_id=1, source_target_pairs={{0,8},{4,12},{8,0},{12,4},{16,24},{20,28},{24,16},{28,20},{1,9},{5... | collective-permute-start | bytes 1769480 | tf_op jit(solution)/shard_map/ppermute | solution.py:641
  408.0 27.3 %collective-permute-start.11 = (bf16[2,192,768]{2,1,0:T(8,128)(2,1)S(1)}, bf16[2,192,768]{2,1,0:T(8,128)(2,1)S(1)}, u32[]{:S(2)}, u32[]{:S(2)}) collective-permute-start(bf16[2,192,768]{2,1,0:T(8,128)(2,1)S(1)} %stack.64), channel_id=1, source_target_pairs={{0,16},{4,20},{8,24},{12,28},{16,0},{20,4},{24,8},{28,12},{1,17},{... | collective-permute-start | bytes 1769480 | tf_op jit(solution)/shard_map/ppermute | solution.py:641
  410.8 30.8 %collective-permute-start.26 = (bf16[192,768]{1,0:T(8,128)(2,1)S(1)}, bf16[192,768]{1,0:T(8,128)(2,1)S(1)}, u32[]{:S(2)}, u32[]{:S(2)}) collective-permute-start(bf16[192,768]{1,0:T(8,128)(2,1)S(1)} %get-tuple-element.138), channel_id=1, source_target_pairs={{0,16},{4,20},{8,24},{12,28},{16,0},{20,4},{24,8},{28,12},{1,17},{... | collective-permute-start | bytes 884744 | tf_op jit(solution)/shard_map/ppermute | solution.py:641
  420.7 21.1 %collective-permute-start.28 = (bf16[192,768]{1,0:T(8,128)(2,1)S(1)}, bf16[192,768]{1,0:T(8,128)(2,1)S(1)}, u32[]{:S(2)}, u32[]{:S(2)}) collective-permute-start(bf16[192,768]{1,0:T(8,128)(2,1)S(1)} %get-tuple-element.139), channel_id=1, source_target_pairs={{0,8},{4,12},{8,0},{12,4},{16,24},{20,28},{24,16},{28,20},{1,9},{5... | collective-permute-start | bytes 884744 | tf_op jit(solution)/shard_map/ppermute | solution.py:641
  422.8 25.1 %collective-permute-start.18 = (bf16[192,768]{1,0:T(8,128)(2,1)S(1)}, bf16[192,768]{1,0:T(8,128)(2,1)S(1)}, u32[]{:S(2)}, u32[]{:S(2)}) collective-permute-start(bf16[192,768]{1,0:T(8,128)(2,1)S(1)} %get-tuple-element.144), channel_id=1, source_target_pairs={{0,16},{4,20},{8,24},{12,28},{16,0},{20,4},{24,8},{28,12},{1,17},{... | collective-permute-start | bytes 884744 | tf_op jit(solution)/shard_map/ppermute | solution.py:641
  433.3 8.4 %copy-start.6 = (bf16[2,192,768]{2,1,0:T(8,128)(2,1)}, bf16[2,192,768]{2,1,0:T(8,128)(2,1)S(1)}, u32[]{:S(2)}) copy-start(bf16[2,192,768]{2,1,0:T(8,128)(2,1)S(1)} %collective-permute-done.9) | copy-start | bytes 1769476
  433.3 16.2 %collective-permute-start.20 = (bf16[192,768]{1,0:T(8,128)(2,1)S(1)}, bf16[192,768]{1,0:T(8,128)(2,1)S(1)}, u32[]{:S(2)}, u32[]{:S(2)}) collective-permute-start(bf16[192,768]{1,0:T(8,128)(2,1)S(1)} %get-tuple-element.145), channel_id=1, source_target_pairs={{0,8},{4,12},{8,0},{12,4},{16,24},{20,28},{24,16},{28,20},{1,9},{5... | collective-permute-start | bytes 884744 | tf_op jit(solution)/shard_map/ppermute | solution.py:641
  435.3 6.4 %copy-start.7 = (bf16[2,192,768]{2,1,0:T(8,128)(2,1)}, bf16[2,192,768]{2,1,0:T(8,128)(2,1)S(1)}, u32[]{:S(2)}) copy-start(bf16[2,192,768]{2,1,0:T(8,128)(2,1)S(1)} %collective-permute-done.11) | copy-start | bytes 1769476
  436.3 15.0 %collective-permute-start.10 = (bf16[192,768]{1,0:T(8,128)(2,1)}, bf16[192,768]{1,0:T(8,128)(2,1)}, u32[]{:S(2)}, u32[]{:S(2)}) collective-permute-start(bf16[192,768]{1,0:T(8,128)(2,1)} %get-tuple-element.150), channel_id=1, source_target_pairs={{0,16},{4,20},{8,24},{12,28},{16,0},{20,4},{24,8},{28,12},{1,17},{... | collective-permute-start | bytes 884744 | tf_op jit(solution)/shard_map/ppermute | solution.py:641
  441.7 12.0 %collective-permute-start.12 = (bf16[192,768]{1,0:T(8,128)(2,1)}, bf16[192,768]{1,0:T(8,128)(2,1)}, u32[]{:S(2)}, u32[]{:S(2)}) collective-permute-start(bf16[192,768]{1,0:T(8,128)(2,1)} %get-tuple-element.151), channel_id=1, source_target_pairs={{0,8},{4,12},{8,0},{12,4},{16,24},{20,28},{24,16},{28,20},{1,9},{5... | collective-permute-start | bytes 884744 | tf_op jit(solution)/shard_map/ppermute | solution.py:641
  442.9 48.2 %collective-permute-start.29 = (bf16[2,96,768]{2,1,0:T(8,128)(2,1)}, bf16[2,96,768]{2,1,0:T(8,128)(2,1)}, u32[]{:S(2)}, u32[]{:S(2)}) collective-permute-start(bf16[2,96,768]{2,1,0:T(8,128)(2,1)} %get-tuple-element.156), channel_id=1, source_target_pairs={{0,2},{1,3},{2,0},{3,1},{4,6},{5,7},{6,4},{7,5},{8,10},{9,11},{10,... | collective-permute-start | bytes 884744 | tf_op jit(solution)/shard_map/ppermute | solution.py:641
  447.9 43.1 %collective-permute-start.30 = (bf16[2,96,768]{2,1,0:T(8,128)(2,1)}, bf16[2,96,768]{2,1,0:T(8,128)(2,1)}, u32[]{:S(2)}, u32[]{:S(2)}) collective-permute-start(bf16[2,96,768]{2,1,0:T(8,128)(2,1)} %get-tuple-element.157), channel_id=1, source_target_pairs={{0,3},{1,2},{2,1},{3,0},{4,7},{5,6},{6,5},{7,4},{8,11},{9,10},{10,... | collective-permute-start | bytes 884744 | tf_op jit(solution)/shard_map/ppermute | solution.py:641
  450.8 12.2 %collective-permute-start.21 = (bf16[192,384]{1,0:T(8,128)(2,1)}, bf16[192,384]{1,0:T(8,128)(2,1)S(1)}, u32[]{:S(2)}, u32[]{:S(2)}) collective-permute-start(bf16[192,384]{1,0:T(8,128)(2,1)} %get-tuple-element.158), channel_id=1, source_target_pairs={{0,1},{1,0},{2,3},{3,2},{4,5},{5,4},{6,7},{7,6},{8,9},{9,8},{10,11... | collective-permute-start | bytes 442376 | tf_op jit(solution)/shard_map/ppermute | solution.py:641
  451.4 29.9 %collective-permute-start.22 = (bf16[192,384]{1,0:T(8,128)(2,1)}, bf16[192,384]{1,0:T(8,128)(2,1)S(1)}, u32[]{:S(2)}, u32[]{:S(2)}) collective-permute-start(bf16[192,384]{1,0:T(8,128)(2,1)} %get-tuple-element.160), channel_id=1, source_target_pairs={{0,2},{1,3},{2,0},{3,1},{4,6},{5,7},{6,4},{7,5},{8,10},{9,11},{10,... | collective-permute-start | bytes 442376 | tf_op jit(solution)/shard_map/ppermute | solution.py:641
  453.7 27.6 %collective-permute-start.23 = (bf16[192,384]{1,0:T(8,128)(2,1)S(1)}, bf16[192,384]{1,0:T(8,128)(2,1)S(1)}, u32[]{:S(2)}, u32[]{:S(2)}) collective-permute-start(bf16[192,384]{1,0:T(8,128)(2,1)S(1)} %get-tuple-element.159), channel_id=1, source_target_pairs={{0,3},{1,2},{2,1},{3,0},{4,7},{5,6},{6,5},{7,4},{8,11},{9,10},{10,... | collective-permute-start | bytes 442376 | tf_op jit(solution)/shard_map/ppermute | solution.py:641
  456.7 34.4 %copy-start.8 = (f32[2,96,768]{2,1,0:T(8,128)S(1)}, f32[2,96,768]{2,1,0:T(8,128)}, u32[]{:S(2)}) copy-start(f32[2,96,768]{2,1,0:T(8,128)} %get-tuple-element.93) | copy-start | bytes 1769476
  463.0 20.7 %collective-permute-start.13 = (bf16[192,384]{1,0:T(8,128)(2,1)S(1)}, bf16[192,384]{1,0:T(8,128)(2,1)S(1)}, u32[]{:S(2)}, u32[]{:S(2)}) collective-permute-start(bf16[192,384]{1,0:T(8,128)(2,1)S(1)} %get-tuple-element.161), channel_id=1, source_target_pairs={{0,1},{1,0},{2,3},{3,2},{4,5},{5,4},{6,7},{7,6},{8,9},{9,8},{10,11... | collective-permute-start | bytes 442376 | tf_op jit(solution)/shard_map/ppermute | solution.py:641
  481.3 9.0 %collective-permute-start.14 = (bf16[192,384]{1,0:T(8,128)(2,1)S(1)}, bf16[192,384]{1,0:T(8,128)(2,1)S(1)}, u32[]{:S(2)}, u32[]{:S(2)}) collective-permute-start(bf16[192,384]{1,0:T(8,128)(2,1)S(1)} %get-tuple-element.163), channel_id=1, source_target_pairs={{0,2},{1,3},{2,0},{3,1},{4,6},{5,7},{6,4},{7,5},{8,10},{9,11},{10,... | collective-permute-start | bytes 442376 | tf_op jit(solution)/shard_map/ppermute | solution.py:641
  481.3 11.8 %copy-start.1 = (bf16[1,1569,768]{2,1,0:T(8,128)(2,1)S(1)}, bf16[1,1569,768]{2,1,0:T(8,128)(2,1)}, u32[]{:S(2)}) copy-start(bf16[1,1569,768]{2,1,0:T(8,128)(2,1)} %get-tuple-element.201) | copy-start | bytes 7229956
  481.3 9.0 %collective-permute-start.15 = (bf16[192,384]{1,0:T(8,128)(2,1)S(1)}, bf16[192,384]{1,0:T(8,128)(2,1)S(1)}, u32[]{:S(2)}, u32[]{:S(2)}) collective-permute-start(bf16[192,384]{1,0:T(8,128)(2,1)S(1)} %get-tuple-element.162), channel_id=1, source_target_pairs={{0,3},{1,2},{2,1},{3,0},{4,7},{5,6},{6,5},{7,4},{8,11},{9,10},{10,... | collective-permute-start | bytes 442376 | tf_op jit(solution)/shard_map/ppermute | solution.py:641
  483.0 11.5 %copy-start.9 = (f32[192,384]{1,0:T(8,128)}, f32[192,384]{1,0:T(8,128)S(1)}, u32[]{:S(2)}) copy-start(f32[192,384]{1,0:T(8,128)S(1)} %fusion.20) | copy-start | bytes 884740
  490.3 4.2 copy-start.10

commit v3 on v2

--- a/solution.py
+++ b/solution.py
@@ -125,14 +125,22 @@
     return {axis: jnp.bitwise_xor(lax.axis_index(axis), bit)}
 
 
-PEERS = (("wide", 1), ("wide", 2), ("wide", 4), ("narrow", 1), ("narrow", 2), ("narrow", 3))
-
-
-def greet():
+RING = (("wide", 1), ("narrow", 1), ("narrow", 3))
+PLANE = (("wide", 1), ("wide", 2), ("wide", 4))
+LINE = (("narrow", 1), ("narrow", 2), ("narrow", 3))
+PEERS = PLANE + LINE
+
+
+def inner():
+    line = lax.axis_index("narrow")
+    return (line == 1) | (line == 2)
+
+
+def greet(peers=PEERS):
     barrier = pltpu.get_barrier_semaphore()
-    for axis, bit in PEERS:
+    for axis, bit in peers:
         pl.semaphore_signal(barrier, inc=1, device_id=peer(axis, bit), device_id_type=pl.DeviceIdType.MESH)
-    pl.semaphore_wait(barrier, len(PEERS))
+    pl.semaphore_wait(barrier, len(peers))
 
 
 def send(src, dst, sems, k, axis, bit):
@@ -153,7 +161,7 @@
 
 
 def plus(a, b):
-    return (a.astype(F32) + b.astype(F32)).astype(BF)
+    return a + b
 
 
 class PlaneSum:
@@ -268,19 +276,65 @@
     return jnp.concatenate([got[: ROWS - TILE], tail], axis=0)
 
 
-def time_in_kernel(clip_ref, cot_ref, vec_ref, bias_ref, w_ref, p_ref, g_ref, h_ref, z_ref):
+def time_kernel(
+    clip_ref, cot_ref, vec_ref, bias_ref, w_ref, mine_ref,
+    p_ref, g_ref, h_ref, z_ref, o_ref, a_ref, near_ref, mid_ref, sib_ref,
+    z_buf, sems,
+):
     step = pl.program_id(0)
-    parts = []
-    for j in range(FPS):
-        frame = step * FPS + j
-        p = shifted(clip_ref, frame, clip_ref[0:1, :].astype(F32), frame >= 0)
-        p_ref[j] = p.astype(BF)
-        xhat, _ = normed(p)
-        parts.append((xhat * vec_ref[0:1] + vec_ref[1:2]).astype(BF))
-        g_ref[j] = shifted(cot_ref, frame, cot_ref[0:1, :].astype(F32), frame == 0).astype(BF)
-    h = jnp.concatenate(parts, axis=0)
-    h_ref[...] = h.reshape(FPS, ROWS, WIDTH)
-    project(h, w_ref, bias_ref, z_ref)
+    row_steps = FRAMES // FPS
+    steps = pl.num_programs(0)
+
+    def near():
+        return send(mine_ref, near_ref, sems, 0, "narrow", 1)
+
+    def mid():
+        return send(mine_ref, mid_ref, sems, 1, "narrow", 3)
+
+    def sibling():
+        return send(near_ref, sib_ref, sems, 2, "wide", 1)
+
+    @pl.when(step == 0)
+    def _():
+        greet(RING)
+        near().start()
+
+        @pl.when(inner())
+        def _():
+            mid().start()
+
+    @pl.when(step < row_steps)
+    def _():
+        parts = []
+        for j in range(FPS):
+            frame = step * FPS + j
+            p = shifted(clip_ref, frame, clip_ref[0:1, :].astype(F32), frame >= 0)
+            p_ref[j] = p.astype(BF)
+            xhat, _ = normed(p)
+            parts.append((xhat * vec_ref[0:1] + vec_ref[1:2]).astype(BF))
+            g_ref[j] = shifted(cot_ref, frame, cot_ref[0:1, :].astype(F32), frame == 0).astype(BF)
+        h = jnp.concatenate(parts, axis=0)
+        h_ref[...] = h.reshape(FPS, ROWS, WIDTH)
+        project(h, w_ref, bias_ref, z_ref)
+        z_buf[pl.ds(step * FPS, FPS)] = z_ref[...]
+
+    @pl.when(step >= row_steps)
+    def _():
+        at = pl.multiple_of((step - row_steps) * TILE, TILE)
+        time_attention(z_buf[:, pl.ds(at, TILE), :], o_ref, a_ref)
+
+    @pl.when(step == steps - 3)
+    def _():
+        near().wait()
+        sibling().start()
+
+    @pl.when(step == steps - 1)
+    def _():
+        sibling().wait()
+
+        @pl.when(inner())
+        def _():
+            mid().wait()
 
 
 def project(h, w_ref, bias_ref, z_ref):
@@ -295,8 +349,8 @@
         z_ref[:, :, cols] = z.reshape(FPS, ROWS, WIDTH)
 
 
-def time_attention_kernel(z_ref, o_ref, a_ref):
-    z = z_ref[...].reshape(FRAMES * TILE, 3 * WIDTH)
+def time_attention(z, o_ref, a_ref):
+    z = z.reshape(FRAMES * TILE, 3 * WIDTH)
     row = lax.broadcasted_iota(jnp.int32, (GROUP * FRAMES * TILE, FRAMES * TILE), 0)
     col = lax.broadcasted_iota(jnp.int32, (GROUP * FRAMES * TILE, FRAMES * TILE), 1)
     same = (row % TILE) == (col % TILE)
@@ -310,9 +364,26 @@
 
 
 def space_kernel(
-    p_ref, ot_ref, vec_ref, bias_ref, wt_ref, w_ref, wo_ref,
-    full_ref, h_ref, z_ref, a_ref, o_ref, x_ref, cls_ref,
+    p_ref, ot_ref, vec_ref, bias_ref, wt_ref, w_ref, wo_ref, near_ref, mid_ref,
+    full_ref, h_ref, z_ref, a_ref, o_ref, x_ref, cls_ref, end_ref, mid2_ref, sems,
 ):
+    step = pl.program_id(0)
+
+    def end():
+        return send(mid_ref, end_ref, sems, 0, "narrow", 1)
+
+    def mid2():
+        return send(near_ref, mid2_ref, sems, 1, "narrow", 3)
+
+    @pl.when(step == 0)
+    def _():
+        greet(RING)
+
+        @pl.when(inner())
+        def _():
+            end().start()
+            mid2().start()
+
     p = p_ref[...].reshape(STEP, WIDTH).astype(F32)
     mixed = p + nn(ot_ref[...].reshape(STEP, WIDTH), wt_ref[...]) + vec_ref[2:3]
     row = lax.broadcasted_iota(jnp.int32, (STEP, WIDTH), 0) % ROWS
@@ -337,31 +408,85 @@
         at = j * ROWS + CLASS - CLASS % 8
         cls_ref[j] = y[at : at + 8]
 
+    @pl.when((step == pl.num_programs(0) - 1) & inner())
+    def _():
+        end().wait_send()
+        mid2().wait()
+
+    @pl.when((step == pl.num_programs(0) - 1) & jnp.logical_not(inner()))
+    def _():
+        end().wait_recv()
+
 
 def mlp_kernel(first_call, *refs):
-    if first_call:
-        (x_ref, cls_ref, p_ref, g_ref, vec_ref, win_ref, wout_ref, bin_ref, wa_ref, wb_ref,
-         h_ref, acc_ref, dh_ref, own_ref, oth_ref, gv_ref, gb_ref,
-         w_buf, bias_buf, h_buf, g_buf, act_buf, dpre_buf, t_buf, sem) = refs
-    else:
-        (x_ref, cls_ref, p_ref, g_ref, vec_ref, h_ref, acc_ref, dh_ref, wa_ref, wb_ref, wc_ref, wd_ref,
-         *refs) = refs
-        refs = list(refs)
-        near_refs = [refs.pop(0), refs.pop(0)] if hosted() else None
-        out_ref, dx_ref, own_ref, oth_ref, gv_ref, gb_ref = refs[:6]
-        refs = refs[6:]
-        near_out = refs.pop(0) if hosted() else None
-        w_buf, bias_buf, h_buf, g_buf, act_buf, dpre_buf, t_buf, out_buf, sem = refs[:9]
-        refs = refs[9:]
+    refs = list(refs)
+
+    def take(n):
+        got = refs[:n]
+        del refs[:n]
+        return got
+
     step = pl.program_id(0)
     me = own_index()
     core = lax.rem(lax.axis_index("wide"), 2)
-    line = lax.axis_index("narrow")
-    swap = jnp.int32(0) if first_call else ((line == 1) | (line == 2)).astype(jnp.int32)
     row_steps = FRAMES // FPS
-    if not first_call and hosted():
-        plane = PlaneSum(*near_refs, *refs[:5])
-        rz, zsem = refs[5:]
+    chained = not first_call and hosted()
+    x_ref, cls_ref, p_ref, g_ref, vec_ref = take(5)
+    if first_call:
+        win_ref, wout_ref, bin_ref, near_ref, near_s_ref, mid_ref, end_ref, mid2_ref = take(8)
+        h_ref, acc_ref, dh_ref, own_ref, oth_ref, gv_ref, gb_ref, end2_ref, far_s_ref, far2_s_ref = take(10)
+        swap = jnp.int32(0)
+    else:
+        h_ref, acc_ref, dh_ref, mid_ref, end_ref, far_s_ref, mid2_ref, end2_ref, far2_s_ref = take(9)
+        near_refs = take(2) if chained else None
+        out_ref, dx_ref, own_ref, oth_ref, gv_ref, gb_ref = take(6)
+        near_out = take(1)[0] if chained else None
+        swap = inner().astype(jnp.int32)
+    w_buf, bias_buf, h_buf, g_buf, act_buf, dpre_buf, t_buf, sem = take(8)
+    if first_call:
+        (rsems,) = take(1)
+
+        def end2():
+            return send(mid2_ref, end2_ref, rsems, 0, "narrow", 1)
+
+        def sibling(k, i):
+            src = ((end_ref, mid_ref), (end2_ref, mid2_ref))[k][i]
+            return send(src, (far_s_ref, far2_s_ref)[k], rsems, 1 + k, "wide", 1)
+
+        def either(k, action):
+            for i in range(2):
+
+                @pl.when(inner() == (i == 1))
+                def _():
+                    action(sibling(k, i))
+
+        @pl.when(step == 0)
+        def _():
+            greet(RING)
+
+            @pl.when(inner())
+            def _():
+                end2().start()
+
+            either(0, lambda c: c.start())
+
+        @pl.when(step == row_steps)
+        def _():
+            @pl.when(inner())
+            def _():
+                end2().wait_send()
+
+            @pl.when(jnp.logical_not(inner()))
+            def _():
+                end2().wait_recv()
+
+            either(1, lambda c: c.start())
+
+    else:
+        (out_buf,) = take(1)
+    if chained:
+        plane = PlaneSum(*near_refs, *take(5))
+        rz, zsem = take(2)
 
         def line_copies():
             return [send(plane.got.at[0, m, pl.ds(96, 96)], rz.at[m], zsem, m, "narrow", 1) for m in range(2)]
@@ -389,27 +514,29 @@
     def _():
         gv_ref[...] = jnp.zeros_like(gv_ref)
         gb_ref[...] = jnp.zeros_like(gb_ref)
-
-        def fetch(src, dst, k):
-            return pltpu.make_async_copy(src, dst, sem.at[k])
-
-        pairs = [(wa_ref, wb_ref)] if first_call else [(wa_ref, wb_ref), (wc_ref, wd_ref)]
-        base = 1 if first_call else 0
         for c in range(2):
-
-            @pl.when(core == c)
-            def _():
-                todo = []
-                for i, (mine, sib) in enumerate(pairs):
-                    slot = base + i
-                    into = (mine, sib) if c == 0 else (sib, mine)
-                    for m in range(2):
-                        todo.append(fetch(into[m].at[0:WIDTH], w_buf.at[m, slot], len(todo)))
-                    todo.append(fetch(mine.at[WIDTH : WIDTH + TILE], bias_buf.at[slot], len(todo)))
-                for t in todo:
-                    t.start()
-                for t in todo:
-                    t.wait()
+            for i in range(2):
+
+                @pl.when((core == c) & (inner() == (i == 1)))
+                def _():
+                    if first_call:
+                        slots = [(1, near_ref, near_s_ref)]
+                    else:
+                        slots = [(0, (end_ref, mid_ref)[i], far_s_ref), (1, (end2_ref, mid2_ref)[i], far2_s_ref)]
+                    todo = []
+                    for slot, mine, sib in slots:
+                        into = (mine, sib) if c == 0 else (sib, mine)
+                        todo += [
+                            pltpu.make_async_copy(into[m].at[0:WIDTH], w_buf.at[m, slot], sem.at[3 * slot + m])
+                            for m in range(2)
+                        ]
+                        todo.append(
+                            pltpu.make_async_copy(
+                                mine.at[WIDTH : WIDTH + TILE], bias_buf.at[slot], sem.at[3 * slot + 2]
+                            )
+                        )
+                    start(todo)
+                    wait(todo)
 
     if first_call:
 
@@ -496,8 +623,11 @@
     @pl.when(step == row_steps + 1)
     def _():
         matrix(1, g_buf, act_buf)
-        if not first_call and hosted():
+        if chained:
             near_total()
+        if first_call:
+            either(0, lambda c: c.wait())
+            either(1, lambda c: c.wait())
 
 
 def put_chunk(own_ref, oth_ref, me, w, unit, value):
@@ -510,11 +640,38 @@
             ref[place, unit] = value
 
 
-def space_back_kernel(
-    dx_ref, dcls_ref, full_ref, z_ref, a_ref, vec_ref, wo_ref, w_ref, wt_ref,
-    dy_ref, dz_ref, df_ref, dyt_ref, dot_ref, gv_ref, do_ref,
-):
+def space_back_kernel(*refs):
+    refs = list(refs)
+
+    def take(n):
+        got = refs[:n]
+        del refs[:n]
+        return got
+
+    dx_ref, dcls_ref, full_ref, z_ref, a_ref, vec_ref, wo_ref, w_ref, wt_ref = take(9)
+    far_refs = take(2) if hosted() else None
+    dy_ref, dz_ref, df_ref, dyt_ref, dot_ref, gv_ref = take(6)
+    far_out = take(1)[0] if hosted() else None
+    (do_ref,) = take(1)
     step = pl.program_id(0)
+    plane = PlaneSum(*far_refs, *take(5)) if hosted() else None
+
+    def begin():
+        greet(PLANE)
+        plane.stage0()
+
+    def finish():
+        plane.stage3()
+        far_out[...] = plane.got[0]
+
+    def checkpoint(j):
+        if hosted():
+            plan = {0: begin, FPS: plane.stage1, 2 * FPS + 1: plane.stage2, 4 * FPS: finish}
+            for k, action in plan.items():
+                if k % FPS == j % FPS and (j < FPS) == (k < 4 * FPS):
+                    pl.when(step == (k - j) // FPS)(action)
+
+    checkpoint(0)
 
     @pl.when(step == 0)
     def _():
@@ -528,6 +685,8 @@
     gv_ref[0:1, :WIDTH] += colsum(dy)
     do_ref[...] = nt(dy, wo_ref[...]).astype(BF)
     for j in range(FPS):
+        if j > 0:
+            checkpoint(j)
         for g in range(GROUPS):
             a = a_ref[j, g]
             q = head_masked(z_ref[j, :, group_cols(g, 0)])
@@ -551,54 +710,37 @@
     dyt_ref[...] = dyt.reshape(FPS, ROWS, WIDTH)
     gv_ref[4:5, :WIDTH] += colsum(dyt)
     dot_ref[...] = nt(dyt, wt_ref[...]).astype(BF).reshape(FPS, ROWS, WIDTH)
-
-
-def time_back_kernel(z_ref, a_ref, do_ref, dz_ref):
-    z = z_ref[...].reshape(FRAMES * TILE, 3 * WIDTH)
-    dot = do_ref[...].reshape(FRAMES * TILE, WIDTH)
-    for g in range(GROUPS):
-        a = a_ref[0, g]
-        q = head_masked(z[:, group_cols(g, 0)])
-        do = head_masked(dot[:, g * GW : (g + 1) * GW])
-        da = nt(do, z[:, group_cols(g, 2)])
-        af = a.astype(F32)
-        ds = (af * (da - jnp.sum(af * da, axis=-1, keepdims=True))).astype(BF)
-        dq = head_select(nn(ds, z[:, group_cols(g, 1)])) * HEAD_DIM**-0.5
-        for which, v in enumerate((dq, tn(ds, q), tn(a, do))):
-            dz_ref[:, :, group_cols(g, which)] = v.astype(BF).reshape(FRAMES, TILE, GW)
-
-
-def time_out_kernel(dz_ref, p_ref, df_ref, vec_ref, w_ref, dp_ref, gv_ref):
+    checkpoint(FPS)
+
+
+def space_grad_kernel(*refs):
+    refs = list(refs)
+
+    def take(n):
+        got = refs[:n]
+        del refs[:n]
+        return got
+
+    dz_ref, h_ref, dy_ref, o_ref, dyt_ref, ot_ref = take(6)
+    near_ref, far_ref = take(2) if hosted() else (None, None)
+    own_ref, oth_ref = take(2)
+    fc_ref = take(1)[0] if hosted() else None
     step = pl.program_id(0)
-
-    @pl.when(step == 0)
-    def _():
-        gv_ref[...] = jnp.zeros_like(gv_ref)
-        dp_ref[0, 0:1, :] = jnp.zeros((1, WIDTH), F32)
-
-    dz = dz_ref[...].reshape(STEP, 3 * WIDTH)
-    gv_ref[0:1, :] += colsum(dz)
-    dh = nt(dz, w_ref[...])
-    xhat, scale = normed(p_ref[...].reshape(STEP, WIDTH).astype(F32))
-    gv_ref[1:2, :WIDTH] += colsum(dh * xhat)
-    gv_ref[2:3, :WIDTH] += colsum(dh)
-    df = df_ref[...].reshape(STEP, WIDTH)
-    dp = df + norm_back(dh, xhat, scale, vec_ref[0:1])
-    for j in range(FPS):
-        dp_ref[0, 0:1, :] += df[j * ROWS + CLASS : j * ROWS + CLASS + 1]
-    for k in range(FRAMES // FPS):
-
-        @pl.when(step == k)
-        def _():
-            for j in range(FPS):
-                start = 1 + (k * FPS + j) * PATCHES
-                dp_ref[0, start : start + PATCHES, :] = dp[j * ROWS : j * ROWS + PATCHES]
-
-
-def pair_grad_kernel(dz_ref, h_ref, dy_ref, o_ref, own_ref, oth_ref):
-    step = pl.program_id(0)
-    me = lax.axis_index("wide") if lax.axis_size("wide") == CHUNKS else jnp.int32(0)
+    me = own_index()
     half = CHUNKS // 2
+    if hosted():
+        rz, zsem = take(2)
+
+        def line_copies():
+            return [
+                send(far_ref.at[m, pl.ds(96 * i, 96)], rz.at[m, i], zsem, 2 * m + i, "narrow", 2 + i)
+                for m in range(2) for i in range(2)
+            ]
+
+        @pl.when(step == 0)
+        def _():
+            greet(LINE)
+            start(line_copies())
 
     @pl.when(step < 2)
     def _():
@@ -607,11 +749,21 @@
             w = step * half + i
             put_rows(own_ref, oth_ref, me, w, 0, got[i * 288 : (i + 1) * 288])
 
-    @pl.when(step == 2)
-    def _():
-        got = tn(dy_ref[...], o_ref[...]).astype(BF)
-        for w in range(CHUNKS):
-            put_rows(own_ref, oth_ref, me, w, 288, got[w * 96 : (w + 1) * 96])
+    for k, left, right in ((2, dy_ref, o_ref), (3, dyt_ref, ot_ref)):
+
+        @pl.when(step == k)
+        def _():
+            got = tn(left[...], right[...]).astype(BF)
+            for w in range(CHUNKS):
+                put_rows(own_ref, oth_ref, me, w, 96 * (k + 1), got[w * 96 : (w + 1) * 96])
+
+    if hosted():
+
+        @pl.when(step == 3)
+        def _():
+            wait(line_copies())
+            for m in range(2):
+                fc_ref[m] = near_ref[m] + rz[m, 0].astype(F32) + rz[m, 1].astype(F32)
 
 
 def put_rows(own_ref, oth_ref, me, w, start, value):
@@ -625,66 +777,224 @@
 
 
 PIECE = (CHUNKS // 2, 384, WIDTH)
-
-
-def pair_grad(dz, h, dy, o, name):
-    rows = FRAMES * ROWS
-    return call(
-        pair_grad_kernel, name, (3,),
-        [pl.BlockSpec((rows, 3 * WIDTH // 2), lambda i: (0, jnp.minimum(i, 1))),
-         whole(rows, WIDTH), whole(rows, WIDTH), whole(rows, WIDTH)],
-        [(whole(*PIECE), jax.ShapeDtypeStruct(PIECE, BF))] * 2,
-    )(dz.reshape(rows, 3 * WIDTH), h.reshape(rows, WIDTH), dy.reshape(rows, WIDTH), o.reshape(rows, WIDTH))
+SPACE_ROWS = 480
+TIME_ROWS = 288
+
+
+def time_back_kernel(*refs):
+    refs = list(refs)
+
+    def take(n):
+        got = refs[:n]
+        del refs[:n]
+        return got
+
+    z_ref, a_ref, do_ref, h_any = take(4)
+    space_refs = take(2) if hosted() else None
+    dz_ref, own_ref, oth_ref = take(3)
+    parts_ref = take(1)[0] if hosted() else None
+    dz_buf, h_buf, h_sem = take(3)
+    step = pl.program_id(0)
+    chunks = ROWS // TILE
+    me = own_index()
+
+    def load():
+        return pltpu.make_async_copy(h_any, h_buf, h_sem)
+
+    if hosted():
+        plane = PlaneSum(*space_refs, *take(5))
+        pad = take(1)[0]
+
+        @pl.when(step == 0)
+        def _():
+            greet(PLANE)
+            plane.stage0()
+
+        pl.when(step == 5)(plane.stage1)
+        pl.when(step == chunks + 1)(plane.stage2)
+
+    pl.when(step == 0)(lambda: load().start())
+
+    @pl.when(step < chunks)
+    def _():
+        z = z_ref[...].reshape(FRAMES * TILE, 3 * WIDTH)
+        dot = do_ref[...].reshape(FRAMES * TILE, WIDTH)
+        for g in range(GROUPS):
+            a = a_ref[0, g]
+            q = head_masked(z[:, group_cols(g, 0)])
+            do = head_masked(dot[:, g * GW : (g + 1) * GW])
+            da = nt(do, z[:, group_cols(g, 2)])
+            af = a.astype(F32)
+            ds = (af * (da - jnp.sum(af * da, axis=-1, keepdims=True))).astype(BF)
+            dq = head_select(nn(ds, z[:, group_cols(g, 1)])) * HEAD_DIM**-0.5
+            for which, v in enumerate((dq, tn(ds, q), tn(a, do))):
+                dz_ref[:, :, group_cols(g, which)] = v.astype(BF).reshape(FRAMES, TILE, GW)
+        dz_buf[:, pl.ds(pl.multiple_of(step * TILE, TILE), TILE), :] = dz_ref[...]
+
+    pl.when(step == chunks)(lambda: load().wait())
+    half = CHUNKS // 2
+    for k in range(2):
+
+        @pl.when(step == chunks + k)
+        def _():
+            left = dz_buf[:, :, k * half * 288 : (k + 1) * half * 288]
+            got = tn(left.reshape(FRAMES * ROWS, half * 288), h_buf[...]).astype(BF)
+            for i in range(half):
+                put_rows(own_ref, oth_ref, me, k * half + i, 0, got[i * 288 : (i + 1) * 288])
+
+    if hosted():
+
+        @pl.when(step == chunks + 1)
+        def _():
+            plane.stage3()
+            transposed(plane.got, pad, parts_ref)
+
+
+def transposed(got, pad, parts_ref):
+    half = got.shape[2]
+    for h in range(2):
+        pad[h * half : (h + 1) * half, :] = got[0, h]
+    rest = pad.shape[0] - 2 * half
+    pad[2 * half :, :] = jnp.zeros((rest, WIDTH), BF)
+    cols = pad[...].T
+    size = WIDTH // parts_ref.shape[0]
+    for n in range(parts_ref.shape[0]):
+        parts_ref[n] = cols[n * size : (n + 1) * size]
+
+
+VEC_ROWS = 24
+
+
+def time_out_kernel(*refs):
+    refs = list(refs)
+
+    def take(n):
+        got = refs[:n]
+        del refs[:n]
+        return got
+
+    dz_ref, p_ref, df_ref, vec_ref, w_ref = take(5)
+    if hosted():
+        time_refs = take(2)
+        s_parts, gvm_ref, gvs_ref, gba_ref, gbb_ref = take(5)
+    dp_ref, gv_ref = take(2)
+    step = pl.program_id(0)
+    row_steps = FRAMES // FPS
+    line = lax.axis_index("narrow")
+    if hosted():
+        sq_ref, sp_ref, tp_ref, tq_ref, share_ref, hid_ref = take(6)
+        plane = PlaneSum(*time_refs, *take(5))
+        pad, parts = take(2)
+        s_line = LineSum(s_parts, *take(2))
+        t_line = LineSum(parts, *take(2))
+        vbuf, vrecv, vsem = take(3)
+
+        @pl.when(step == 0)
+        def _():
+            greet()
+            plane.stage0()
+            start(s_line.copies())
+
+        pl.when(step == 2)(plane.stage1)
+
+    @pl.when(step == 0)
+    def _():
+        gv_ref[...] = jnp.zeros_like(gv_ref)
+        dp_ref[0:1, 0, :] = jnp.zeros((1, WIDTH), F32)
+
+    @pl.when(step < row_steps)
+    def _():
+        dz = dz_ref[...].reshape(STEP, 3 * WIDTH)
+        gv_ref[0:1, :] += colsum(dz)
+        dh = nt(dz, w_ref[...])
+        xhat, scale = normed(p_ref[...].reshape(STEP, WIDTH).astype(F32))
+        gv_ref[1:2, :WIDTH] += colsum(dh * xhat)
+        gv_ref[2:3, :WIDTH] += colsum(dh)
+        df = df_ref[...].reshape(STEP, WIDTH)
+        dp = df + norm_back(dh, xhat, scale, vec_ref[0:1])
+        for j in range(FPS):
+            dp_ref[0:1, 0, :] += df[j * ROWS + CLASS : j * ROWS + CLASS + 1]
+        for k in range(row_steps):
+
+            @pl.when(step == k)
+            def _():
+                for j in range(FPS):
+                    begin = 1 + (k * FPS + j) * PATCHES
+                    dp_ref[begin : begin + PATCHES, 0, :] = dp[j * ROWS : j * ROWS + PATCHES]
+
+    if hosted():
+
+        @pl.when(step == row_steps)
+        def _():
+            vbuf[...] = jnp.zeros_like(vbuf)
+            vbuf[0:3, :] = gvm_ref[0:3, :]
+            for i, r, c in ((3, 0, 0), (4, 1, 0), (5, 1, 2), (6, 2, 0), (7, 3, 0), (8, 4, 0)):
+                vbuf[i : i + 1, :] = gvs_ref[r : r + 1, c * WIDTH : (c + 1) * WIDTH]
+            for i, r, c in ((9, 0, 0), (10, 0, 2), (11, 1, 0), (12, 2, 0)):
+                vbuf[i : i + 1, :] = gv_ref[r : r + 1, c * WIDTH : (c + 1) * WIDTH]
+            low = line < 2
+            places = (line, jnp.bitwise_xor(line, 1), jnp.where(low, 2, 1), jnp.where(low, 3, 0))
+            for place, (ref, r) in zip(places, ((gba_ref, 0), (gba_ref, 1), (gbb_ref, 0), (gbb_ref, 1))):
+                vbuf[pl.ds(13 + place, 1), :] = ref[r : r + 1, :]
+
+            def exchange(k, axis, bit):
+                return send(vbuf, vrecv.at[k], vsem, k, axis, bit)
+
+            def added(k, axis, bit):
+                exchange(k, axis, bit).wait()
+                vbuf[...] += vrecv[k]
+
+            exchange(0, "wide", 1).start()
+            plane.stage2()
+            added(0, "wide", 1)
+            exchange(1, "wide", 2).start()
+            added(1, "wide", 2)
+            exchange(2, "wide", 4).start()
+            added(2, "wide", 4)
+            for b in (1, 2, 3):
+                exchange(2 + b, "narrow", b).start()
+            plane.stage3()
+            transposed(plane.got, pad, parts)
+            start(t_line.copies())
+            total = s_line.result()
+            sq_ref[...] = total[:, :288]
+            sp_ref[...] = total[:, 288:384]
+            tp_ref[...] = total[:, 384:480]
+            for b in (1, 2, 3):
+                exchange(2 + b, "narrow", b).wait()
+            vectors = vbuf[...] + vrecv[3] + vrecv[4] + vrecv[5]
+            size = WIDTH // 4
+            share = vectors[:, :size]
+            hidden = vectors[13:14, :]
+            for n in range(1, 4):
+                share = jnp.where(line == n, vectors[:, n * size : (n + 1) * size], share)
+                hidden = jnp.where(line == n, vectors[13 + n : 14 + n, :], hidden)
+            share_ref[...] = share
+            hid_ref[...] = hidden
+            tq_ref[...] = t_line.result()[:, :288]
 
 
 def flip(value, axis, bit):
     return lax.ppermute(value, axis, [(i, i ^ bit) for i in range(lax.axis_size(axis))])
 
 
-def hop(value, pairs):
-    return lax.ppermute(value, "narrow", pairs)
-
-
-def add(a, b):
-    return (a.astype(F32) + b.astype(F32)).astype(BF)
-
-
-def plane_sum(own, oth):
-    got = add(own, flip(oth, "wide", 1))
-    half = 192
-    rx = flip(jnp.stack([got[1, :half], got[3, :half]]), "wide", 2)
-    ry = flip(jnp.stack([got[2, half:], got[3, half:]]), "wide", 4)
-    na, ya = add(got[0, :half], rx[0]), add(got[2, :half], rx[1])
-    nb, xb = add(got[0, half:], ry[0]), add(got[1, half:], ry[1])
-    ra = flip(ya, "wide", 4)
-    rb = flip(xb, "wide", 2)
-    return jnp.concatenate([add(na, ra), add(nb, rb)])
-
-
 def unit_sum(own, oth):
-    if lax.axis_size("wide") == CHUNKS:
-        return plane_sum(own.reshape(PIECE), oth.reshape(PIECE)).reshape(2, 2, 96, WIDTH)
     both = jnp.stack([own, oth], axis=1).reshape(CHUNKS, 4, 96, WIDTH)
     both = both.transpose(1, 0, 2, 3).reshape(4, WIDTH, WIDTH)
     both = lax.psum_scatter(both, "wide", scatter_dimension=1, tiled=True)
     return both.reshape(2, 2, -1, WIDTH)
 
 
-def pair_sum(own, oth, me):
-    if lax.axis_size("wide") == CHUNKS:
-        rows = plane_sum(own, oth)
-        cut = 288
-    else:
-        both = jnp.stack([own, oth], axis=1).reshape(CHUNKS, 384, WIDTH)
-        first = both[:, :288].reshape(3 * WIDTH, WIDTH)
-        second = both[:, 288:].reshape(WIDTH, WIDTH)
-        first = lax.psum_scatter(first, "wide", scatter_dimension=0, tiled=True)
-        second = lax.psum_scatter(second, "wide", scatter_dimension=0, tiled=True)
-        rows = jnp.concatenate([first, second])
-        cut = first.shape[0]
-    parts = rows.T.reshape(lax.axis_size("narrow"), -1, rows.shape[0])
-    total = line_sum(parts, me)
-    return total[:, :cut], total[:, cut:]
+def piece_sum(own, oth, sizes, me):
+    both = jnp.stack([own, oth], axis=1).reshape(CHUNKS, -1, WIDTH)
+    found, at = [], 0
+    for size in sizes:
+        rows = both[:, at * 96 : (at + size) * 96].reshape(size * WIDTH, WIDTH)
+        at += size
+        rows = lax.psum_scatter(rows, "wide", scatter_dimension=0, tiled=True)
+        parts = rows.T.reshape(lax.axis_size("narrow"), -1, rows.shape[0])
+        found.append(line_sum(parts, me))
+    return found
 
 
 def line_sum(parts, me):
@@ -713,61 +1023,55 @@
     me_n = lax.axis_index("narrow")
     me_w = lax.axis_index("wide")
     mine = jnp.where(me_w % 2 == 0, fc_in, fc_out)
-    bias_rows = jnp.broadcast_to(in_bias[None], (TILE, WIDTH))
-    mine = jnp.concatenate([mine, bias_rows], axis=0)
-    near = flip(mine, "narrow", 1)
-    mid1 = hop(mine, [(1, 2), (2, 1)])
-    near_s = flip(near, "wide", 1)
-    end1 = hop(mid1, [(1, 0), (2, 3)])
-    mid2 = hop(near, [(1, 2), (2, 1)])
-    end2 = hop(mid2, [(1, 0), (2, 3)])
-    inner = (me_n == 1) | (me_n == 2)
-    far1 = jnp.where(inner, mid1, end1)
-    far1_s = flip(far1, "wide", 1)
-    far2 = jnp.where(inner, mid2, end2)
-    far2_s = flip(far2, "wide", 1)
+    mine = jnp.concatenate([mine, jnp.broadcast_to(in_bias[None], (TILE, WIDTH))], axis=0)
+    any_ref = pl.BlockSpec(memory_space=pl.ANY)
+    message = (any_ref, jax.ShapeDtypeStruct((WIDTH + TILE, WIDTH), BF))
 
     chunks = ROWS // TILE
-    a_time = (pl.BlockSpec((1, GROUPS, GROUP * FRAMES * TILE, FRAMES * TILE), lambda i: (i, 0, 0, 0)),
-              jax.ShapeDtypeStruct((chunks, GROUPS, GROUP * FRAMES * TILE, FRAMES * TILE), BF))
+    a_time = jax.ShapeDtypeStruct((chunks, GROUPS, GROUP * FRAMES * TILE, FRAMES * TILE), BF)
+
+    def a_chunk(first):
+        return pl.BlockSpec((1, *a_time.shape[1:]), lambda i: (jnp.clip(i - first, 0, chunks - 1), 0, 0, 0))
+
     a_space = (pl.BlockSpec((FPS, GROUPS, GROUP * ROWS, ROWS), lambda i: (i, 0, 0, 0)),
                jax.ShapeDtypeStruct((FRAMES, GROUPS, GROUP * ROWS, ROWS), BF))
 
-    def chunk(width):
-        return pl.BlockSpec((FRAMES, TILE, width), lambda i: (0, i, 0))
-
-    def chunk_out(width):
-        return chunk(width), jax.ShapeDtypeStruct((FRAMES, ROWS, width), BF)
-
+    last = FRAMES // FPS - 1
+    steps = last + 1
     rows = FRAMES * ROWS
-    steps = (FRAMES // FPS,)
-    p, g, ht, zt = call(
-        time_in_kernel, "time_in", steps,
-        [whole(tokens, WIDTH), whole(tokens, WIDTH), whole(nvec, WIDTH), whole(2, WIDTH), whole(WIDTH, 3 * WIDTH)],
-        [frames_out(WIDTH, BF), frames_out(WIDTH, BF), frames_out(WIDTH, BF), frames_out(3 * WIDTH, BF)],
-        flops=6 * rows * WIDTH * WIDTH, nbytes=24 * 2**20,
-    )(clip, cot, vec, t_bias, time_qkv)
-    ot, at = call(
-        time_attention_kernel, "time_attention", (chunks,),
-        [chunk(3 * WIDTH)], [chunk_out(WIDTH), a_time],
-        flops=10**10, nbytes=16 * 2**20,
-    )(zt)
-    full, hs, zs, a_s, o_s, xs, ycls = call(
-        space_kernel, "space", steps,
+
+    def row_in(width):
+        return pl.BlockSpec((FPS, ROWS, width), lambda i: (jnp.minimum(i, last), 0, 0))
+
+    def row_out(width, dtype):
+        return row_in(width), jax.ShapeDtypeStruct((FRAMES, ROWS, width), dtype)
+
+    def chunk(width, first):
+        return pl.BlockSpec((FRAMES, TILE, width), lambda i: (0, jnp.clip(i - first, 0, chunks - 1), 0))
+
+    def chunk_out(width, first):
+        return chunk(width, first), jax.ShapeDtypeStruct((FRAMES, ROWS, width), BF)
+
+    p, g, ht, zt, ot, at, near, mid, near_s = call(
+        time_kernel, "time", (steps + chunks,),
+        [whole(tokens, WIDTH), whole(tokens, WIDTH), whole(nvec, WIDTH), whole(2, WIDTH), whole(WIDTH, 3 * WIDTH),
+         any_ref],
+        [row_out(WIDTH, BF), row_out(WIDTH, BF), row_out(WIDTH, BF), row_out(3 * WIDTH, BF),
+         chunk_out(WIDTH, steps), (a_chunk(steps), a_time)] + [message] * 3,
+        scratch=[pltpu.VMEM((FRAMES, ROWS, 3 * WIDTH), BF), pltpu.SemaphoreType.DMA((2, 3))],
+        remote=1,
+    )(clip, cot, vec, t_bias, time_qkv, mine)
+    full, hs, zs, a_s, o_s, xs, ycls, end, mid2 = call(
+        space_kernel, "space", (steps,),
         [frames(WIDTH), frames(WIDTH), whole(nvec, WIDTH), whole(2, WIDTH),
-         whole(WIDTH, WIDTH), whole(WIDTH, 3 * WIDTH), whole(WIDTH, WIDTH)],
+         whole(WIDTH, WIDTH), whole(WIDTH, 3 * WIDTH), whole(WIDTH, WIDTH), any_ref, any_ref],
         [frames_out(WIDTH, F32), frames_out(WIDTH, BF), frames_out(3 * WIDTH, BF), a_space,
          frames_out(WIDTH, BF), frames_out(WIDTH, F32),
-         (pl.BlockSpec((FPS, 8, WIDTH), lambda i: (i, 0, 0)), jax.ShapeDtypeStruct((FRAMES, 8, WIDTH), F32))],
-        flops=3 * 10**10, nbytes=40 * 2**20,
-    )(p, ot, vec, s_bias, time_proj, space_qkv, space_proj)
-    any_ref = pl.BlockSpec(memory_space=pl.ANY)
-    last = FRAMES // FPS - 1
-    row_in = pl.BlockSpec((FPS, ROWS, WIDTH), lambda i: (jnp.minimum(i, last), 0, 0))
-
-    def row_out(dtype):
-        return row_in, jax.ShapeDtypeStruct((FRAMES, ROWS, WIDTH), dtype)
-
+         (pl.BlockSpec((FPS, 8, WIDTH), lambda i: (i, 0, 0)), jax.ShapeDtypeStruct((FRAMES, 8, WIDTH), F32))]
+        + [message] * 2,
+        scratch=[pltpu.SemaphoreType.DMA((2, 2))],
+        remote=2,
+    )(p, ot, vec, s_bias, time_proj, space_qkv, space_proj, near, mid)
     unit_shape = (CHUNKS // 2, 4, 96, WIDTH)
     units = [(whole(*unit_shape), jax.ShapeDtypeStruct(unit_shape, BF))] * 2
     vec_out = [(whole(8, WIDTH), jax.ShapeDtypeStruct((8, WIDTH), F32))] * 2
@@ -775,84 +1079,135 @@
         pltpu.VMEM((2, 2, WIDTH, WIDTH), BF), pltpu.VMEM((2, TILE, WIDTH), BF),
         pltpu.VMEM((rows, WIDTH), BF), pltpu.VMEM((rows, WIDTH), BF),
         pltpu.VMEM((rows, 2 * WIDTH), BF), pltpu.VMEM((rows, 2 * WIDTH), BF), pltpu.VMEM((WIDTH, rows), BF),
+        pltpu.SemaphoreType.DMA((6,)),
     ]
-    hm, acc, dh, a_own, a_oth, _, gb_a = call(
+    mlp_in = [row_in(WIDTH), whole(FRAMES, 8, WIDTH),
+              pl.BlockSpec((1, TILE, WIDTH), lambda i: (0, CLASS // TILE, 0)), row_in(WIDTH), whole(nvec, WIDTH)]
+    hm, acc, dh, a_own, a_oth, _, gb_a, end2, far_s, far2_s = call(
         partial(mlp_kernel, True), "mlp_near", (last + 3,),
-        [row_in, whole(FRAMES, 8, WIDTH),
-         pl.BlockSpec((1, TILE, WIDTH), lambda i: (0, CLASS // TILE, 0)), row_in,
-         whole(nvec, WIDTH), whole(WIDTH, WIDTH), whole(WIDTH, WIDTH), whole(1, WIDTH), any_ref, any_ref],
-        [row_out(BF), row_out(F32), row_out(F32)] + units + vec_out,
-        scratch=bufs + [pltpu.SemaphoreType.DMA((8,))],
-    )(xs, ycls, p, g, vec, fc_in, fc_out, in_bias.astype(F32)[None], near, near_s)
+        mlp_in + [whole(WIDTH, WIDTH), whole(WIDTH, WIDTH), whole(1, WIDTH)] + [any_ref] * 5,
+        [row_out(WIDTH, BF), row_out(WIDTH, F32), row_out(WIDTH, F32)] + units + vec_out + [message] * 3,
+        scratch=bufs + [pltpu.SemaphoreType.DMA((2, 3))],
+        remote=3,
+    )(xs, ycls, p, g, vec, fc_in, fc_out, in_bias.astype(F32)[None], near, near_s, mid, end, mid2)
     units_in = []
     near_out = []
     near_args = []
     near_scratch = []
     if hosted():
-        units_in = [any_ref, any_ref]
+        units_in = [any_ref] * 2
         near_args = [halves(a_own), halves(a_oth)]
         near_out = [(whole(2, 96, WIDTH), jax.ShapeDtypeStruct((2, 96, WIDTH), F32))]
         near_scratch = PlaneSum.scratch(384) + [pltpu.VMEM((2, 96, WIDTH), BF), pltpu.SemaphoreType.DMA((2, 2))]
     layer_out, dxs, b_own, b_oth, gv_m, gb_b, *near_sum = call(
         partial(mlp_kernel, False), "mlp_far", (last + 3,),
-        [row_in, whole(FRAMES, 8, WIDTH),
-         pl.BlockSpec((1, TILE, WIDTH), lambda i: (0, CLASS // TILE, 0)), row_in,
-         whole(nvec, WIDTH), row_in, row_in, row_in, any_ref, any_ref, any_ref, any_ref] + units_in,
-        [(whole(1, tokens, WIDTH), jax.ShapeDtypeStruct((1, tokens, WIDTH), BF)), row_out(F32)] + units + vec_out + near_out,
-        scratch=bufs + [pltpu.VMEM((tokens, WIDTH), F32), pltpu.SemaphoreType.DMA((8,))] + near_scratch,
-        remote=1 if hosted() else None,
-    )(xs, ycls, p, g, vec, hm, acc, dh, far1, far1_s, far2, far2_s, *near_args)
-    dys, dzs, df, dyt, dot, gv_s = call(
-        space_back_kernel, "space_back", steps,
+        mlp_in + [row_in(WIDTH), row_in(WIDTH), row_in(WIDTH)] + [any_ref] * 6 + units_in,
+        [(whole(1, tokens, WIDTH), jax.ShapeDtypeStruct((1, tokens, WIDTH), BF)), row_out(WIDTH, F32)]
+        + units + vec_out + near_out,
+        scratch=bufs + [pltpu.VMEM((tokens, WIDTH), F32)] + near_scratch,
+        remote=4 if hosted() else None,
+    )(xs, ycls, p, g, vec, hm, acc, dh, mid, end, far_s, mid2, end2, far2_s, *near_args)
+
+    far_in, far_args, far_out, far_scratch = [], [], [], []
+    if hosted():
+        far_in = [any_ref] * 2
+        far_args = [halves(b_own), halves(b_oth)]
+        far_out = [(whole(2, 192, WIDTH), jax.ShapeDtypeStruct((2, 192, WIDTH), BF))]
+        far_scratch = PlaneSum.scratch(384)
+    dys, dzs, df, dyt, dot, gv_s, *far_sum = call(
+        space_back_kernel, "space_back", (steps,),
         [frames(WIDTH), pl.BlockSpec((1, 8, WIDTH), lambda i: (0, CLASS // 8, 0)), frames(WIDTH),
          frames(3 * WIDTH), a_space[0], whole(nvec, WIDTH),
-         whole(WIDTH, WIDTH), whole(WIDTH, 3 * WIDTH), whole(WIDTH, WIDTH)],
+         whole(WIDTH, WIDTH), whole(WIDTH, 3 * WIDTH), whole(WIDTH, WIDTH)] + far_in,
         [frames_out(WIDTH, BF), frames_out(3 * WIDTH, BF), frames_out(WIDTH, F32),
          frames_out(WIDTH, BF), frames_out(WIDTH, BF),
-         (whole(8, 3 * WIDTH), jax.ShapeDtypeStruct((8, 3 * WIDTH), F32))],
-        scratch=[pltpu.VMEM((STEP, WIDTH), BF)],
-        flops=3 * 10**10, nbytes=50 * 2**20,
-    )(dxs, dxs, full, zs, a_s, vec, space_proj, space_qkv, time_proj)
-    s_own, s_oth = pair_grad(dzs, hs, dys, o_s, "grad_space")
-    dzt, = call(
-        time_back_kernel, "time_back", (chunks,),
-        [chunk(3 * WIDTH), a_time[0], chunk(WIDTH)], [chunk_out(3 * WIDTH)],
-        flops=10**10, nbytes=24 * 2**20,
-    )(zt, at, dot)
-    t_own, t_oth = pair_grad(dzt, ht, dyt, ot, "grad_time")
-    grad_clips, gv_t = call(
-        time_out_kernel, "time_out", steps,
-        [frames(3 * WIDTH), frames(WIDTH), frames(WIDTH), whole(nvec, WIDTH), whole(WIDTH, 3 * WIDTH)],
-        [(whole(1, tokens, WIDTH), jax.ShapeDtypeStruct((1, tokens, WIDTH), F32)),
-         (whole(8, 3 * WIDTH), jax.ShapeDtypeStruct((8, 3 * WIDTH), F32))],
-        flops=6 * rows * WIDTH * WIDTH, nbytes=28 * 2**20,
-    )(dzt, p, df, vec, time_qkv)
-
+         (whole(8, 3 * WIDTH), jax.ShapeDtypeStruct((8, 3 * WIDTH), F32))] + far_out,
+        scratch=[pltpu.VMEM((STEP, WIDTH), BF)] + far_scratch,
+        remote=5 if hosted() else None,
+    )(dxs, dxs, full, zs, a_s, vec, space_proj, space_qkv, time_proj, *far_args)
+
+    def flat(value):
+        return value.reshape(rows, value.shape[-1])
+
+    piece = (CHUNKS // 2, SPACE_ROWS, WIDTH)
+    line_in, line_args, line_out, line_scratch = [], [], [], []
     if hosted():
-        fc = near_sum[0]
+        line_in = [whole(2, 96, WIDTH), any_ref]
+        line_args = [near_sum[0], far_sum[0]]
+        line_out = [(whole(2, 96, WIDTH), jax.ShapeDtypeStruct((2, 96, WIDTH), F32))]
+        line_scratch = [pltpu.VMEM((2, 2, 96, WIDTH), BF), pltpu.SemaphoreType.DMA((2, 4))]
+    s_own, s_oth, *fc_sum = call(
+        space_grad_kernel, "space_grad", (4,),
+        [pl.BlockSpec((rows, 3 * WIDTH // 2), lambda i: (0, jnp.minimum(i, 1)))] + [whole(rows, WIDTH)] * 5 + line_in,
+        [(whole(*piece), jax.ShapeDtypeStruct(piece, BF))] * 2 + line_out,
+        scratch=line_scratch,
+        remote=6 if hosted() else None,
+    )(flat(dzs), flat(hs), flat(dys), flat(o_s), flat(dyt), flat(ot), *line_args)
+
+    t_piece = (CHUNKS // 2, TIME_ROWS, WIDTH)
+    share = WIDTH // slices
+    back_in, back_args, back_out, back_scratch = [], [], [], []
+    if hosted():
+        back_in = [any_ref] * 2
+        back_args = [halves(s_own), halves(s_oth)]
+        back_out = [(whole(slices, share, 512), jax.ShapeDtypeStruct((slices, share, 512), BF))]
+        back_scratch = PlaneSum.scratch(SPACE_ROWS) + [pltpu.VMEM((512, WIDTH), BF)]
+    dzt, t_own, t_oth, *s_parts = call(
+        time_back_kernel, "time_back", (chunks + 2,),
+        [chunk(3 * WIDTH, 0), a_chunk(0), chunk(WIDTH, 0), any_ref] + back_in,
+        [chunk_out(3 * WIDTH, 0)] + [(whole(*t_piece), jax.ShapeDtypeStruct(t_piece, BF))] * 2 + back_out,
+        scratch=[pltpu.VMEM((FRAMES, ROWS, 3 * WIDTH), BF), pltpu.VMEM((rows, WIDTH), BF), pltpu.SemaphoreType.DMA]
+        + back_scratch,
+        remote=7 if hosted() else None,
+    )(zt, at, dot, flat(ht), *back_args)
+
+    out_in, out_args, out_out, out_scratch = [], [], [], []
+    if hosted():
+        out_in = [any_ref] * 2 + [whole(slices, share, 512), whole(8, WIDTH), whole(8, 3 * WIDTH)] + [whole(8, WIDTH)] * 2
+        out_args = [halves(t_own), halves(t_oth), s_parts[0], gv_m, gv_s, gb_a, gb_b]
+        out_out = [
+            (whole(*shape), jax.ShapeDtypeStruct(shape, F32))
+            for shape in ((share, 288), (share, 96), (share, 96), (share, 288), (VEC_ROWS, share), (1, WIDTH))
+        ]
+        out_scratch = (
+            PlaneSum.scratch(TIME_ROWS)
+            + [pltpu.VMEM((384, WIDTH), BF), pltpu.VMEM((slices, share, 384), BF)]
+            + LineSum.scratch(share, 512) + LineSum.scratch(share, 384)
+            + [pltpu.VMEM((VEC_ROWS, WIDTH), F32), pltpu.VMEM((6, VEC_ROWS, WIDTH), F32), pltpu.SemaphoreType.DMA((2, 6))]
+        )
+    grad_clips, gv_t, *sums = call(
+        time_out_kernel, "time_out", (steps + (1 if hosted() else 0),),
+        [row_in(3 * WIDTH), row_in(WIDTH), row_in(WIDTH), whole(nvec, WIDTH), whole(WIDTH, 3 * WIDTH)] + out_in,
+        [(whole(tokens, 1, WIDTH), jax.ShapeDtypeStruct((tokens, 1, WIDTH), F32)),
+         (whole(8, 3 * WIDTH), jax.ShapeDtypeStruct((8, 3 * WIDTH), F32))] + out_out,
+        scratch=out_scratch,
+        remote=8 if hosted() else None,
+    )(dzt, p, df, vec, time_qkv, *out_args)
+    grad_clips = grad_clips.reshape(1, tokens, WIDTH)
+
+    if hosted():
+        fc = fc_sum[0]
+        s_qkv, s_proj, t_proj, t_qkv, mine, grad_in_bias = sums
+        grad_in_bias = grad_in_bias[0]
     else:
-        near_sum = unit_sum(a_own, a_oth)
-        fc = near_sum[:, 0].astype(F32) + flip(near_sum[:, 1], "narrow", 1).astype(F32)
-    far_sum = unit_sum(b_own, b_oth)
-    fc = fc + flip(far_sum[:, 0], "narrow", 2).astype(F32) + flip(far_sum[:, 1], "narrow", 3).astype(F32)
-    s_qkv, s_proj = pair_sum(s_own, s_oth, me_n)
-    t_qkv, t_proj = pair_sum(t_own, t_oth, me_n)
-
-    vectors = jnp.stack(
-        [gv_m[0], gv_m[1], gv_m[2],
-         gv_s[0, :WIDTH], gv_s[1, :WIDTH], gv_s[1, 2 * WIDTH :], gv_s[2, :WIDTH], gv_s[3, :WIDTH], gv_s[4, :WIDTH],
-         gv_t[0, :WIDTH], gv_t[0, 2 * WIDTH :], gv_t[1, :WIDTH], gv_t[2, :WIDTH]]
-    )
-    lower = me_n < 2
-    places = (me_n, jnp.bitwise_xor(me_n, 1), jnp.where(lower, 2, 1), jnp.where(lower, 3, 0))
-    hidden_rows = jnp.zeros((slices, WIDTH), F32)
-    for place, row in zip(places, (gb_a[0], gb_a[1], gb_b[0], gb_b[1])):
-        hidden_rows = lax.dynamic_update_slice(hidden_rows, row[None], (place, 0))
-    vectors = jnp.concatenate([vectors, hidden_rows], axis=0)
-    vectors = lax.psum(vectors, ("wide", "narrow"))
-    share = WIDTH // slices
-    mine = lax.dynamic_slice(vectors, (0, me_n * share), (13, share))
-    grad_in_bias = lax.dynamic_slice(vectors, (13 + me_n, 0), (1, WIDTH))[0]
+        near_part = unit_sum(a_own, a_oth)
+        far_part = unit_sum(b_own, b_oth)
+        fc = near_part[:, 0].astype(F32) + flip(near_part[:, 1], "narrow", 1).astype(F32)
+        fc = fc + flip(far_part[:, 0], "narrow", 2).astype(F32) + flip(far_part[:, 1], "narrow", 3).astype(F32)
+        s_qkv, s_proj, t_proj = piece_sum(s_own, s_oth, (3, 1, 1), me_n)
+        (t_qkv,) = piece_sum(t_own, t_oth, (3,), me_n)
+        vectors = jnp.concatenate(
+            [gv_m[0:3], gv_s[0:1, :WIDTH], gv_s[1:2, :WIDTH], gv_s[1:2, 2 * WIDTH :], gv_s[2:5, :WIDTH],
+             gv_t[0:1, :WIDTH], gv_t[0:1, 2 * WIDTH :], gv_t[1:3, :WIDTH]]
+        )
+        lower = me_n < 2
+        places = (me_n, jnp.bitwise_xor(me_n, 1), jnp.where(lower, 2, 1), jnp.where(lower, 3, 0))
+        hidden_rows = jnp.zeros((slices, WIDTH), F32)
+        for place, row in zip(places, (gb_a[0], gb_a[1], gb_b[0], gb_b[1])):
+            hidden_rows = lax.dynamic_update_slice(hidden_rows, row[None], (place, 0))
+        vectors = lax.psum(jnp.concatenate([vectors, hidden_rows], axis=0), ("wide", "narrow"))
+        mine = lax.dynamic_slice(vectors, (0, me_n * share), (13, share))
+        grad_in_bias = lax.dynamic_slice(vectors, (13 + me_n, 0), (1, WIDTH))[0]
     return (
         layer_out,
         grad_clips,

time: 503 us -> 388 us (0.77)
  waiting for transfers between devices: 106 us -> 0 us
  Pallas kernels: 269 us -> 352 us
  blocking collectives: 39 us -> 0 us
  starting transfers between devices: 32.8 us -> 0 us
  other arithmetic: 18.6 us -> 6.95 us
  local copies, waits for them, and re-layouts: 28.1 us -> 20.3 us
    ppermute x31 -> x0, waiting for transfers between devices: 106 us -> none  [the longest x27 89.2 us: flip(): lax.ppermute(value, axis, [(i, i ^ bit) for i in range(lax.axis_size(axis...]
    pallas_call x10 -> x8, Pallas kernels: 269 us -> 352 us  [the longest x1 54.6 us: local(): call(time_out_kernel, 'time_out', (steps + (1 if hosted() else 0),), [row...]
    psum x1 -> x0, blocking collectives: 39 us -> none  [local(): vectors = lax.psum(vectors, ('wide', 'narrow'))]
    ppermute x31 -> x0, starting transfers between devices: 32.8 us -> none  [the longest x27 27.7 us: flip(): lax.ppermute(value, axis, [(i, i ^ bit) for i in range(lax.axis_size(axis...]
    convert_element_type x9 -> x0, other arithmetic: 9.79 us -> none  [add(): return (a.astype(F32) + b.astype(F32)).astype(BF)]
    slice x13 -> x0, local copies, waits for them, and re-layouts: 6.99 us -> none  [the longest x2 1.51 us: pair_sum(): return (total[:, :cut], total[:, cut:])]
    unnamed x50 -> x18, local copies, waits for them, and re-layouts: 14.7 us -> 8.47 us
    another operation x10, local copies, waits for them, and re-layouts: 0.11 us -> 6.23 us  [local(): jnp.stack([time_gain, time_shift, time_offset, space_gain, space_shift, s...]
  transfers between devices with their start and end apart: 31 -> 0, of which waited for: 10 -> 0; matrix products, arithmetic and copies ran while one was open for 8% -> 0% of each run, Pallas kernels for 43% -> 0%
where the time goes in v3:
time: 388 us; the launch traced here: 380 us
  Pallas kernels  352 us (91%)
  local copies, waits for them, and re-layouts  20.3 us (5%)
  other arithmetic  6.95 us (2%)
    pallas_call x1, Pallas kernels, local(): call(time_out_kernel, 'time_out', (steps + (1 if hosted() else 0),), [row...  54.6 us
    pallas_call x1, Pallas kernels, local(): call(partial(mlp_kernel, False), 'mlp_far', (last + 3,), mlp_in + [row_in...  52.1 us
    pallas_call x1, Pallas kernels, local(): call(partial(mlp_kernel, True), 'mlp_near', (last + 3,), mlp_in + [whole(...  48.1 us
    pallas_call x1, Pallas kernels, local(): call(space_back_kernel, 'space_back', (steps,), [frames(WIDTH), pl.BlockS...  47 us
    pallas_call x1, Pallas kernels, local(): call(time_kernel, 'time', (steps + chunks,), [whole(tokens, WIDTH), whole...  39.6 us
    pallas_call x1, Pallas kernels, local(): call(time_back_kernel, 'time_back', (chunks + 2,), [chunk(3 * WIDTH, 0),...  39.6 us
    pallas_call x1, Pallas kernels, local(): call(space_kernel, 'space', (steps,), [frames(WIDTH), frames(WIDTH), whol...  36.4 us
    pallas_call x1, Pallas kernels, local(): call(space_grad_kernel, 'space_grad', (4,), [pl.BlockSpec((rows, 3 * WIDT...  34.6 us

profile of v3, /device:TPU:0, one launch (start us, length us, event | category | flops | bytes accessed | tf_op | source)
XLA Modules:
  0.0 380.2 jit_solution(18155498731782782661)
XLA Ops:
  0.7 0.7 stack.30
  1.4 0.7 stack.31
  2.0 0.7 stack.32
  2.7 0.7 stack.33
  3.4 0.7 stack.34
  4.1 0.7 stack.35
  4.8 0.7 stack.36
  5.5 0.7 stack.37
  6.2 0.7 stack.38
  6.8 0.1 stack.39
  6.9 1.3 reshape.105.refs_7_
  8.2 1.3 convert_element_type.11.bias_ref
  9.4 1.3 convert_element_type.12.bias_ref
  10.7 0.6 convert_element_type.10.vec_ref.refs_4_.refs_5_.refs_3_
  11.3 0.7 broadcast_in_dim.11
  12.0 1.4 broadcast_select_fusion
  13.4 1.1 pad_maximum_fusion.mine_ref
  14.5 39.6 %time.1 = (bf16[8,208,768]{2,1,0:T(8,128)(2,1)}, bf16[8,208,768]{2,1,0:T(8,128)(2,1)}, bf16[8,208,768]{2,1,0:T(8,128)(2,1)}, bf16[8,208,2304]{2,1,0:T(8,128)(2,1...) custom-call(bf16[1569,768]{1,0:T(8,128)(2,1)} %bitcast.43, ...), custom_call_target="tpu_custom_call" | custom-call | tf_op jit(solution)/shard_map/time/pallas_call | solution.py:1055
  54.1 36.4 %space.1 = (f32[8,208,768]{2,1,0:T(8,128)}, bf16[8,208,768]{2,1,0:T(8,128)(2,1)}, bf16[8,208,2304]{2,1,0:T(8,128)(2,1)}, bf16[8,3,832,208]{3,2,1,0:T(8,128)(2,1)...) custom-call(bf16[8,208,768]{2,1,0:T(8,128)(2,1)} %get-tuple-element., ...), custom_call_target="tpu_custom_call" | custom-call | tf_op jit(solution)/shard_map/space/pallas_call | solution.py:1064
  90.6 48.1 %mlp_near.1 = (bf16[8,208,768]{2,1,0:T(8,128)(2,1)}, f32[8,208,768]{2,1,0:T(8,128)}, f32[8,208,768]{2,1,0:T(8,128)}, bf16[4,4,96,768]{3,2,1,0:T(8,128)(2,1)}, bf...) custom-call(f32[8,208,768]{2,1,0:T(8,128)} %get-tuple-element.79.ref, ...), custom_call_target="tpu_custom_call" | custom-call | tf_op jit(solution)/shard_map/mlp_near/pallas_call | solution.py:1086
  138.7 52.1 %mlp_far.1 = (bf16[1,1569,768]{2,1,0:T(8,128)(2,1)}, f32[8,208,768]{2,1,0:T(8,128)}, bf16[4,4,96,768]{3,2,1,0:T(8,128)(2,1)}, bf16[4,4,96,768]{3,2,1,0:T(8,128)(...) custom-call(f32[8,208,768]{2,1,0:T(8,128)} %get-tuple-element.79.refs_0_, ...), custom_call_target="tpu_custom_call" | custom-call | tf_op jit(solution)/shard_map/mlp_far/pallas_call | solution.py:1102
  190.8 47.0 %space_back.1 = (bf16[8,208,768]{2,1,0:T(8,128)(2,1)}, bf16[8,208,2304]{2,1,0:T(8,128)(2,1)}, f32[8,208,768]{2,1,0:T(8,128)}, bf16[8,208,768]{2,1,0:T(8,128)(2,1...) custom-call(f32[8,208,768]{2,1,0:T(8,128)} %get-tuple-element.96.refs_0_.refs_1_, ...), custom_call_target="tpu_custom_call" | custom-call | tf_op jit(solution)/shard_map/space_back/pallas_call | solution.py:1117
  237.8 34.6 %space_grad.1 = (bf16[4,480,768]{2,1,0:T(8,128)(2,1)}, bf16[4,480,768]{2,1,0:T(8,128)(2,1)}, f32[2,96,768]{2,1,0:T(8,128)}) custom-call(bf16[1664,2304]{1,0:T(8,128)(2,1)} %bitcast.34, bf16[1664,768]{1,0:T(8,128)(2,1)} %bitcast.39, bf16[1664,768]{1,0:T(8,128)(2,1)} %bitcast.41, bf16[1664,768]{1,0:T(8,128)(2,1)} %bitcast.40, bf16[1664,768]{1,0:T(8,128)(2,1)} %bitcast.42, ...), custom_call_target="tpu_custom_call" | custom-call | tf_op jit(solution)/shard_map/space_grad/pallas_call | solution.py:1139
  272.4 39.6 %time_back.1 = (bf16[8,208,2304]{2,1,0:T(8,128)(2,1)}, bf16[4,288,768]{2,1,0:T(8,128)(2,1)}, bf16[4,288,768]{2,1,0:T(8,128)(2,1)}, bf16[4,192,512]{2,1,0:T(8,128)(2,1)}) custom-call(bf16[8,208,2304]{2,1,0:T(8,128)(2,1)} %get-tuple-element.94.refs_0_, bf16[13,3,512,128]{3,2,1,0:T(8,128)(2,1)} %get-tuple-element.95.refs_1_, ...), custom_call_target="tpu_custom_call" | custom-call | tf_op jit(solution)/shard_map/time_back/pallas_call | solution.py:1155
  312.0 0.0 copy-start.1
  312.0 54.6 %time_out.1 = (f32[1569,1,768]{2,1,0:T(1,128)}, f32[8,2304]{1,0:T(8,128)}, f32[192,288]{1,0:T(8,128)}, f32[192,96]{1,0:T(8,128)}, f32[192,96]{1,0:T(8,128)}, /*i...) custom-call(bf16[8,208,2304]{2,1,0:T(8,128)(2,1)} %get-tuple-element.113.refs_0_, ...), custom_call_target="tpu_custom_call" | custom-call | tf_op jit(solution)/shard_map/time_out/pallas_call | solution.py:1178
  366.6 1.3 reduce
  367.9 1.3 fusion.1
  369.2 1.5 fusion
  370.7 0.0 copy-done.1
  370.7 0.8 slice_bitcast_fusion
  371.6 0.0 copy-start
  371.6 3.4 copy.46
  375.0 0.1 copy-done
  375.1 0.0 copy-start.3
  375.1 0.0 copy-start.5
  375.1 0.0 copy-start.2
  375.1 0.0 copy-start.4
  375.1 2.2 copy.47
  377.3 0.0 copy-done.3
  377.3 0.7 copy.48
  378.0 0.0 copy-done.5
  378.0 0.6 copy.49
  378.7 0.0 copy-done.2
  378.7 0.7 copy.50
  379.4 0.0 copy-done.4
  379.4 0.6 copy.51
Async XLA Ops:
  312.0 58.7 %copy-start.1 = (f32[2,96,768]{2,1,0:T(8,128)S(1)}, f32[2,96,768]{2,1,0:T(8,128)}, u32[]{:S(2)}) copy-start(f32[2,96,768]{2,1,0:T(8,128)} %get-tuple-element.128) | copy-start | bytes 1769476
  371.6 3.5 copy-start
  375.1 2.2 copy-start.3
  375.1 3.0 copy-start.5
  375.1 3.6 copy-start.2
  375.1 4.3 %copy-start.4 = (f32[192,96]{1,0:T(8,128)S(1)}, f32[192,96]{1,0:T(8,128)}, u32[]{:S(2)}) copy-start(f32[192,96]{1,0:T(8,128)} %get-tuple-element.175) | copy-start | bytes 221188
